TPU v7x, 256 devices: a whole 4x4x8 slice. The times are simulated.
256 devices in a mesh: ctx: 32 (over y, x, core), tp: 8 (over z).
Axes of the slice: x: 4, y: 4, z: 8, core: 2. Of those that a mesh axis runs over, the one named last changes fastest.
Arguments:
- slow_x: bfloat16 [16384, 1024], P(('ctx', 'tp')), may hold values from -24 to 24
- q_weight: bfloat16 [1024, 1024], P(None, 'tp'), may hold values from -0.1875 to 0.1875
- o_weight: bfloat16 [1024, 1024], P('tp'), may hold values from -0.1875 to 0.1875
- fast_kv: bfloat16 [2, 131072, 1024], P(None, 'ctx', 'tp'), may hold values from -26 to 26
- mask_lists: int32 [128, 32], replicated, may hold values from 0 to 1023, as said below
- cotangent: bfloat16 [16384, 1024], P(('ctx', 'tp')), may hold values from -6 to 6
Outputs:
- attended: bfloat16 [16384, 1024], P(('ctx', 'tp'))
- grad_slow: bfloat16 [16384, 1024], P(('ctx', 'tp'))
- grad_q_weight: float32 [1024, 1024], P(None, 'tp')
- grad_o_weight: float32 [1024, 1024], P('tp')
- grad_kv: bfloat16 [2, 131072, 1024], P(None, 'ctx', 'tp')
Inputs may be any that keep to these rules, and one draw needn't show every extreme that they name: `mask_lists`: row b lists the key blocks c - w to c + w - 1 that lie within the clip, where c = (2 b + 1) * 4 and w, drawn for each row, lies between 8 and 16; the remaining entries repeat c.
All inputs are finite; a program needn't handle non-finite values.
Results may differ from a plain program's by a relative error of at most 0.03.
Values may be sent and summed in bfloat16 or wider, within the bound.
No kernel may reach another device: no remote copies, remote signals or barrier semaphores. Data moves between devices by JAX's collectives and lax.ppermute only.
A program may use at most 128 MiB of HBM per device.

v0:
```python
import jax
import jax.numpy as jnp
from jax import lax
from jax.sharding import PartitionSpec as P

BLK = 128
DH = 64


def extended_2(cells, sides, width):
    for axis, dim in sides:
        count = lax.axis_size(axis)
        ends = count - 1
        head = lax.slice_in_dim(cells, 0, width, axis=dim)
        tail = lax.slice_in_dim(cells, cells.shape[dim] - width, cells.shape[dim], axis=dim)
        cells = jnp.concatenate(
            [
                lax.ppermute(tail, axis, [(i, (i + 1) % count) for i in range(ends)]),
                cells,
                lax.ppermute(head, axis, [((i + 1) % count, i) for i in range(ends)]),
            ],
            axis=dim,
        )
    return cells


def band_live(band_lists, base_block, window_first, reach_blocks, block_rows):
    span_index = jnp.arange(2 * reach_blocks, dtype=jnp.int32)
    window_blocks = window_first[:, None] + span_index[None, :]
    wanted = base_block + window_blocks
    allowed = jnp.any(band_lists[:, :, None] == wanted[:, None, :], axis=1)
    block_count = band_lists.shape[0]
    spread = jnp.broadcast_to(allowed[:, :, None], (block_count, 2 * reach_blocks, block_rows))
    return spread.reshape(block_count, 1, 2 * reach_blocks * block_rows)


def on_device(slow_x, q_weight, o_weight, fast_kv, mask_lists, cotangent):
    rows_x, rows_g = (
        lax.all_gather(slow_x, "tp", axis=0, tiled=True),
        lax.all_gather(cotangent, "tp", axis=0, tiled=True),
    )
    block_rows = BLK
    total_rows = rows_x.shape[0]
    query_blocks = total_rows // block_rows
    fast_rows = fast_kv.shape[1]
    fast_blocks = fast_rows // block_rows
    half_step = fast_blocks // (2 * query_blocks)
    reach_blocks = mask_lists.shape[1] // 2
    rim_blocks = reach_blocks - half_step
    rim_rows = rim_blocks * block_rows
    window_rows = 2 * reach_blocks * block_rows
    head_cols = q_weight.shape[1]
    head_count = head_cols // DH
    score_scale = DH ** (-0.5)
    ctx_index = lax.axis_index("ctx")
    base_block = ctx_index * fast_blocks
    band_lists = lax.dynamic_slice_in_dim(mask_lists, ctx_index * query_blocks, query_blocks, 0)
    queries = (jnp.dot(rows_x, q_weight, preferred_element_type=jnp.float32) * score_scale).astype(
        jnp.bfloat16
    )
    grad_attn = jnp.einsum(
        "rd,cd->rc", rows_g, o_weight, preferred_element_type=jnp.float32
    ).astype(jnp.bfloat16)
    extended = extended_2(fast_kv, (("ctx", 1),), rim_rows)
    window_starts = [
        2 * local_block * half_step * block_rows for local_block in range(query_blocks)
    ]
    key_windows = jnp.stack(
        [extended[0, first_row : first_row + window_rows] for first_row in window_starts]
    )
    value_windows = jnp.stack(
        [extended[1, first_row : first_row + window_rows] for first_row in window_starts]
    )
    window_first = jnp.array(
        [(2 * local_block + 1) * half_step - reach_blocks for local_block in range(query_blocks)],
        dtype=jnp.int32,
    )
    live_keys = band_live(band_lists, base_block, window_first, reach_blocks, block_rows)
    grads_ext = jnp.zeros(extended.shape, jnp.float32)
    attn_parts = []
    query_grads = []
    total_parts = []
    delta_parts = []
    for head_index in range(head_count):
        columns = slice(head_index * DH, (head_index + 1) * DH)
        query_head = queries[:, columns].reshape(query_blocks, block_rows, DH)
        grad_head = grad_attn[:, columns].reshape(query_blocks, block_rows, DH)
        key_head = key_windows[:, :, columns]
        value_head = value_windows[:, :, columns]
        scores = jnp.einsum(
            "lqd,lkd->lqk", query_head, key_head, preferred_element_type=jnp.float32
        )
        scores = jnp.where(live_keys, scores, -jnp.inf)
        row_max = jnp.max(scores, axis=-1, keepdims=True)
        log_total = row_max + jnp.log(jnp.sum(jnp.exp(scores - row_max), axis=-1, keepdims=True))
        prob_full = jnp.exp(scores - log_total)
        prob_half = prob_full.astype(jnp.bfloat16)
        attn_head = jnp.einsum(
            "lqk,lkd->lqd", prob_half, value_head, preferred_element_type=jnp.float32
        ).astype(jnp.bfloat16)
        row_delta = jnp.sum(
            grad_head.astype(jnp.float32) * attn_head.astype(jnp.float32), axis=-1, keepdims=True
        )
        grad_prob = jnp.einsum(
            "lqd,lkd->lqk", grad_head, value_head, preferred_element_type=jnp.float32
        )
        grad_score = (prob_full * (grad_prob - row_delta)).astype(jnp.bfloat16)
        grad_query = jnp.einsum(
            "lqk,lkd->lqd", grad_score, key_head, preferred_element_type=jnp.float32
        )
        attn_parts.append(attn_head.reshape(total_rows, DH))
        query_grads.append(grad_query.reshape(total_rows, DH))
        total_parts.append(log_total.reshape(total_rows, 1))
        delta_parts.append(row_delta.reshape(total_rows, 1))
        grad_key = jnp.einsum(
            "lqk,lqd->lkd", grad_score, query_head, preferred_element_type=jnp.float32
        )
        grad_value = jnp.einsum(
            "lqk,lqd->lkd", prob_half, grad_head, preferred_element_type=jnp.float32
        )
        for local_block, first_row in enumerate(window_starts):
            grads_ext = grads_ext.at[0, first_row : first_row + window_rows, columns].add(
                grad_key[local_block]
            )
            grads_ext = grads_ext.at[1, first_row : first_row + window_rows, columns].add(
                grad_value[local_block]
            )
    attn_rows = jnp.concatenate(attn_parts, axis=1)
    grad_pre = (jnp.concatenate(query_grads, axis=1) * score_scale).astype(jnp.bfloat16)
    own_grads = grads_ext[:, rim_rows : rim_rows + fast_rows]
    edges = jnp.concatenate([grads_ext[:, :rim_rows], grads_ext[:, rim_rows + fast_rows :]], axis=1)
    arrived = extended_2(edges, (("ctx", 1),), rim_rows)
    own_grads = own_grads.at[:, :rim_rows].add(arrived[:, :rim_rows])
    own_grads = own_grads.at[:, fast_rows - rim_rows :].add(arrived[:, 3 * rim_rows :])
    grad_kv = own_grads.astype(jnp.bfloat16)
    forward_term = jnp.dot(attn_rows, o_weight, preferred_element_type=jnp.float32)
    input_term = jnp.einsum("rc,dc->rd", grad_pre, q_weight, preferred_element_type=jnp.float32)
    summed = lax.psum_scatter(
        jnp.concatenate([forward_term, input_term], axis=1), "tp", scatter_dimension=0, tiled=True
    )
    model_width = slow_x.shape[1]
    attended = summed[:, :model_width].astype(jnp.bfloat16)
    grad_slow = summed[:, model_width:].astype(jnp.bfloat16)
    query_term = jnp.einsum("rd,rc->dc", rows_x, grad_pre, preferred_element_type=jnp.float32)
    output_term = jnp.einsum("rc,rd->cd", attn_rows, rows_g, preferred_element_type=jnp.float32)
    grad_q_weight, grad_o_weight = lax.psum((query_term, output_term), "ctx")
    return (attended, grad_slow, grad_q_weight, grad_o_weight, grad_kv)


def solution(mesh):
    in_specs = (
        P(("ctx", "tp"), None),
        P(None, "tp"),
        P("tp", None),
        P(None, "ctx", "tp"),
        P(),
        P(("ctx", "tp"), None),
    )
    out_specs = (
        P(("ctx", "tp"), None),
        P(("ctx", "tp"), None),
        P(None, "tp"),
        P("tp", None),
        P(None, "ctx", "tp"),
    )
    return jax.shard_map(
        on_device, mesh=mesh, in_specs=in_specs, out_specs=out_specs, check_vma=False
    )
```

profile of v0, /device:TPU:1, one launch (start us, length us, event | category | flops | bytes accessed | tf_op | source)
XLA Modules:
  0.0 330.9 jit_solution(9208406113447125153)
XLA Ops:
  8.0 2.9 copy.47
  12.2 4.5 %collective-permute-start = (bf16[2,1536,128]{1,2,0:T(8,128)(2,1)}, bf16[2,1536,128]{1,2,0:T(8,128)(2,1)S(1)}, u32[]{:S(2)}, u32[]{:S(2)}) collective-permute-start(bf16[2,1536,128]{1,2,0:T(8,128)(2,1)} %get-tuple-element.251), channel_id=1, source_target_pairs={{0,8},{8,16},{16,24},{24,32},{32,40},{40,48},{48,56},{56,64},{64,7... | collective-permute-start | bytes 2359304 | tf_op jit(solution)/shard_map/ppermute | solution.py:18
  19.2 6.7 %collective-permute-done = bf16[2,1536,128]{1,2,0:T(8,128)(2,1)S(1)} collective-permute-done((bf16[2,1536,128]{1,2,0:T(8,128)(2,1)}, bf16[2,1536,128]{1,2,0:T(8,128)(2,1)S(1)}, u32[]{:S(2)}, u32[]{:S(2)}) %collective-permute-start) | collective-permute-done | bytes 786464 | tf_op jit(solution)/shard_map/ppermute | solution.py:18
  25.9 4.5 %collective-permute-done.1 = bf16[2,1536,128]{1,2,0:T(8,128)(2,1)} collective-permute-done((bf16[2,1536,128]{1,2,0:T(8,128)(2,1)}, bf16[2,1536,128]{1,2,0:T(8,128)(2,1)}, u32[]{:S(2)}, u32[]{:S(2)}) %collective-permute-start.1) | collective-permute-done | bytes 786464 | tf_op jit(solution)/shard_map/ppermute | solution.py:20
  34.2 3.4 %fusion.10 = bf16[4,4096,128]{1,2,0:T(8,128)(2,1)} fusion(bf16[2,1536,128]{1,2,0:T(8,128)(2,1)} %collective-permute-done.1, bf16[2,4096,128]{1,2,0:T(8,128)(2,1)S(1)} %copy.47, bf16[2,1536,128]{1,2,0:T(8,128)(2,1)S(1)} %collective-permute-done, bf16[1,4096,128]{1,2,0:T(8,128)(2,1)S(1)} %get-tuple-element.250, bf16[1,4096,128]{1,2,0:T(8,128)(2,1)S(1)} %get-tuple-element.242), kind=kLoop, calls=%fused_computation.27 | loop fusion | flops 41943040 | bytes 9961472 | tf_op jit(solution)/shard_map/stack | solution.py:71
  37.7 9.6 %all-gather.5.cloned.1.call-done = bf16[512,1024]{1,0:T(8,128)(2,1)} async-done(((bf16[64,1024]{1,0:T(8,128)(2,1)}), bf16[512,1024]{1,0:T(8,128)(2,1)}) %all-gather.5.cloned.1.call-update) | async-done | bytes 1048592 | tf_op jit(solution)/shard_map/all_gather | solution.py:40
  49.0 37.3 %all-gather.3.cloned.1.call-done = bf16[512,1024]{1,0:T(8,128)(2,1)} async-done(((bf16[64,1024]{1,0:T(8,128)(2,1)}), bf16[512,1024]{1,0:T(8,128)(2,1)}) %all-gather.3.cloned.1.call-update) | async-done | bytes 1048592 | tf_op jit(solution)/shard_map/all_gather | solution.py:39
  88.1 3.1 select_reduce_fusion.1
  91.2 3.8 %exponential_reduce_fusion.1 = (f32[4,128]{1,0:T(4,128)S(1)}, f32[4,128]{1,0:T(4,128)S(1)}, f32[4,128,4096]{2,1,0:T(8,128)S(1)}) fusion(f32[4,128,4096]{2,1,0:T(8,128)S(1)} %get-tuple-element.260, f32[4,128]{1,0:T(4,128)S(1)} %get-tuple-element.259, pred[4,4096]{1,0:T(4,128)(4,1)S(1)} %bitcast.76, bf16[4,4096,128]{1,2,0:T(8,128)(2,1)S(1)} %copy-done.3, ...), kind=kOutput, calls=%fused_computation.10 | convolution fusion | flops 278920192 | bytes 18962432 | tf_op jit(solution)/shard_map/lqd,lkd->lqk/dot_general | solution.py:90
  96.8 3.8 %fusion.64 = f32[4,4096,64]{1,2,0:T(8,128)} fusion(f32[4,128,4096]{2,1,0:T(8,128)S(1)} %get-tuple-element.260, f32[4,128]{1,0:T(4,128)S(1)} %get-tuple-element.267, pred[4,4096]{1,0:T(4,128)(4,1)S(1)} %bitcast.78, bf16[8,4,8,128]{3,2,1,0:T(8,128)(2,1)S(1)} %get-tuple-element.255), kind=kOutput, calls=%fused_computation.99 | convolution fusion | flops 274726912 | bytes 12666880 | tf_op jit(solution)/shard_map/lqk,lqd->lkd/dot_general | solution.py:118
  100.7 3.4 %multiply_reduce_fusion.1 = (f32[4,128]{1,0:T(4,128)S(1)}, bf16[4,128,64]{1,2,0:T(8,128)(2,1)S(1)}) fusion(bf16[8,4,8,128]{3,2,1,0:T(8,128)(2,1)S(1)} %get-tuple-element.255, bf16[4,4096,128]{1,2,0:T(8,128)(2,1)} %fusion.10, f32[4,128,4096]{2,1,0:T(8,128)S(1)} %get-tuple-element.260, f32[4,128]{1,0:T(4,128)S(1)} %get-tuple-element.267, ...), kind=kOutput, calls=%fused_computation.105 | convolution fusion | flops 274890240 | bytes 10637312 | tf_op jit(solution)/shard_map/lqk,lkd->lqd/dot_general | solution.py:98
  104.0 4.3 %multiply_convert_fusion.1 = bf16[4,128,4096]{2,1,0:T(8,128)(2,1)S(1)} fusion(f32[4,128,4096]{2,1,0:T(8,128)S(1)} %get-tuple-element.260, f32[4,128]{1,0:T(4,128)S(1)} %get-tuple-element.264, f32[4,128]{1,0:T(4,128)S(1)} %get-tuple-element.267, pred[4,4096]{1,0:T(4,128)(4,1)S(1)} %bitcast.80, bf16[4,4096,128]{1,2,0:T(8,128)(2,1)} %fusion.10, ...), kind=kOutput, calls=%fused_computation.6 | convolution fusion | flops 278921216 | bytes 14766080 | tf_op jit(solution)/shard_map/lqd,lkd->lqk/dot_general | solution.py:104
  113.9 3.0 multiply_convert_fusion
  123.1 3.8 %scatter-add.60 = f32[2,7168,128]{1,2,0:T(8,128)} pad(f32[1,4096,64]{1,2,0:T(8,128)S(1)} %slice.743, f32[]{:T(128)} %constant.538.clone.1), padding=0_1x0_3072x0_64 | pad | bytes 8388612 | tf_op jit(solution)/shard_map/scatter-add | solution.py:122
  145.1 3.9 %pad_maximum_fusion.1 = f32[512,2048]{1,0:T(8,128)} fusion(f32[512,1024]{1,0:T(8,128)S(1)} %fusion.87, f32[512,1024]{1,0:T(8,128)} %fusion.100), kind=kLoop, calls=%fused_computation.30 | loop fusion | flops 1048576 | bytes 8388608 | tf_op jit(solution)/shard_map/concatenate | solution.py:139
  149.0 7.3 %fusion.61 = f32[4,4096,64]{1,2,0:T(8,128)} fusion(f32[4,128,4096]{2,1,0:T(8,128)} %copy-done.1, f32[4,128]{1,0:T(4,128)S(1)} %get-tuple-element.266, pred[4,4096]{1,0:T(4,128)(4,1)S(1)} %bitcast.83, bf16[8,4,8,128]{3,2,1,0:T(8,128)(2,1)S(1)} %get-tuple-element.256), kind=kOutput, calls=%fused_computation.98 | convolution fusion | flops 274726912 | bytes 12666880 | tf_op jit(solution)/shard_map/lqk,lqd->lkd/dot_general | solution.py:118
  159.2 3.4 %fusion.53 = f32[2,7168,128]{1,2,0:T(8,128)} fusion(f32[2,7168,128]{1,2,0:T(8,128)} %fusion.54, f32[4,4096,64]{1,2,0:T(8,128)} %fusion.61), kind=kLoop, calls=%fused_computation.82 | loop fusion | flops 262144 | bytes 3145728 | tf_op jit(solution)/shard_map/scatter-add | solution.py:125
  176.5 3.3 %fusion.97 = (f32[2,1536,128]{1,2,0:T(8,128)S(1)}, f32[2,1536,128]{1,2,0:T(8,128)}) fusion(f32[2,7168,128]{1,2,0:T(8,128)} %fusion.47), kind=kLoop, calls=%fused_computation.146 | loop fusion | bytes 6291456 | tf_op jit(solution)/shard_map/slice | solution.py:131
  179.8 8.7 %collective-permute-start.2 = (f32[2,1536,128]{1,2,0:T(8,128)}, f32[2,1536,128]{1,2,0:T(8,128)}, u32[]{:S(2)}, u32[]{:S(2)}) collective-permute-start(f32[2,1536,128]{1,2,0:T(8,128)} %get-tuple-element.241), channel_id=1, source_target_pairs={{0,8},{8,16},{16,24},{24,32},{32,40},{40,48},{48,56},{56,64},{64,7... | collective-permute-start | bytes 4718600 | tf_op jit(solution)/shard_map/ppermute | solution.py:18
  190.5 4.6 %slice.773 = f32[2,4096,128]{1,2,0:T(8,128)} slice(f32[2,7168,128]{1,2,0:T(8,128)} %fusion.47), slice={[0:2], [1536:5632], [0:128]} | slice | bytes 8388608 | tf_op jit(solution)/shard_map/slice | solution.py:130
  195.1 69.2 %all-reduce.4.cloned.1.call-done = (f32[1024,128]{0,1:T(8,128)}, f32[128,1024]{1,0:T(8,128)}) async-done(((f32[1024,128]{0,1:T(8,128)}, f32[128,1024]{1,0:T(8,128)}), (f32[1024,128]{0,1:T(8,128)}, f32[128,1024]{1,0:T(8,128)})) %all-reduce.4.cloned.1.call-update) | async-done | bytes 1048592 | tf_op jit(solution)/shard_map/psum | solution.py:146
  266.3 3.3 fusion.27
  269.5 2.8 fusion.26
  277.3 44.5 %reduce-scatter.2.cloned.1.call-done = f32[64,2048]{1,0:T(8,128)} async-done(((f32[512,2048]{1,0:T(8,128)}), f32[64,2048]{1,0:T(8,128)}) %reduce-scatter.2.cloned.1.call-update) | async-done | bytes 524304 | tf_op jit(solution)/shard_map/reduce_scatter | solution.py:138
  (89 shorter events, 71.7 us)
Async XLA Ops:
  7.2 40.1 %copy-start = (bf16[128,1024]{1,0:T(8,128)(2,1)S(1)}, bf16[128,1024]{1,0:T(8,128)(2,1)}, u32[]{:S(2)}) copy-start(bf16[128,1024]{1,0:T(8,128)(2,1)} %param.45) | copy-start | bytes 786436
  7.2 11.8 %copy-start.13 = (s32[4]{0:T(128)S(1)}, s32[4]{0:T(128)}, u32[]{:S(2)}) copy-start(s32[4]{0:T(128)} %constant.545.clone) | copy-start | bytes 52
  7.2 11.6 %copy-start.12 = (s32[128,32]{0,1:T(8,128)S(1)}, s32[128,32]{0,1:T(8,128)}, u32[]{:S(2)}) copy-start(s32[128,32]{0,1:T(8,128)} %param.47) | copy-start | bytes 49156
  7.2 40.1 %all-gather.5.cloned.1.call-start = ((), (), s32[]{:S(2)}) async-start(), calls=%async_computation.2 | async-start | bytes 1179648 | tf_op jit(solution)/shard_map/all_gather | solution.py:40
  7.9 78.4 %all-gather.3.cloned.1.call-start = ((), (), s32[]{:S(2)}) async-start(), calls=%async_computation.1 | async-start | bytes 1179648 | tf_op jit(solution)/shard_map/all_gather | solution.py:39
  12.2 13.7 %collective-permute-start = (bf16[2,1536,128]{1,2,0:T(8,128)(2,1)}, bf16[2,1536,128]{1,2,0:T(8,128)(2,1)S(1)}, u32[]{:S(2)}, u32[]{:S(2)}) collective-permute-start(bf16[2,1536,128]{1,2,0:T(8,128)(2,1)} %get-tuple-element.251), channel_id=1, source_target_pairs={{0,8},{8,16},{16,24},{24,32},{32,40},{40,48},{48,56},{56,64},{64,7... | collective-permute-start | bytes 2359304 | tf_op jit(solution)/shard_map/ppermute | solution.py:18
  16.7 13.7 %collective-permute-start.1 = (bf16[2,1536,128]{1,2,0:T(8,128)(2,1)}, bf16[2,1536,128]{1,2,0:T(8,128)(2,1)}, u32[]{:S(2)}, u32[]{:S(2)}) collective-permute-start(bf16[2,1536,128]{1,2,0:T(8,128)(2,1)} %get-tuple-element.252), channel_id=1, source_target_pairs={{8,0},{16,8},{24,16},{32,24},{40,32},{48,40},{56,48},{64,56},{72,6... | collective-permute-start | bytes 2359304 | tf_op jit(solution)/shard_map/ppermute | solution.py:20
  18.7 245.5 %all-reduce.4.cloned.1.call-start = ((), (), s32[]{:S(2)}) async-start(), calls=%async_computation.4 | async-start | bytes 2097152 | tf_op jit(solution)/shard_map/psum | solution.py:146
  34.2 52.1 %copy-start.10 = (bf16[1024,128]{1,0:T(8,128)(2,1)S(1)}, bf16[1024,128]{1,0:T(8,128)(2,1)}, u32[]{:S(2)}) copy-start(bf16[1024,128]{1,0:T(8,128)(2,1)} %param.44) | copy-start | bytes 786436
  88.0 3.1 copy-start.3
  95.0 18.9 %copy-start.1 = (f32[4,128,4096]{2,1,0:T(8,128)}, f32[4,128,4096]{2,1,0:T(8,128)S(1)}, u32[]{:S(2)}) copy-start(f32[4,128,4096]{2,1,0:T(8,128)S(1)} %get-tuple-element.261) | copy-start | bytes 25165828
  110.0 2.2 copy-start.8
  113.9 3.0 copy-start.4
  123.1 3.8 %copy-start.5 = (f32[4,4096,64]{1,2,0:T(8,128)S(1)}, f32[4,4096,64]{1,2,0:T(8,128)}, u32[]{:S(2)}) copy-start(f32[4,4096,64]{1,2,0:T(8,128)} %fusion.64) | copy-start | bytes 12582916
  137.5 5.3 %copy-start.9 = (bf16[512,1024]{1,0:T(8,128)(2,1)S(1)}, bf16[512,1024]{1,0:T(8,128)(2,1)}, u32[]{:S(2)}) copy-start(bf16[512,1024]{1,0:T(8,128)(2,1)} %all-gather.5.cloned.1.call-done) | copy-start | bytes 3145732
  139.9 4.0 %copy-start.7 = (bf16[512,1024]{1,0:T(8,128)(2,1)S(1)}, bf16[512,1024]{1,0:T(8,128)(2,1)}, u32[]{:S(2)}) copy-start(bf16[512,1024]{1,0:T(8,128)(2,1)} %all-gather.3.cloned.1.call-done) | copy-start | bytes 3145732
  145.1 176.8 %reduce-scatter.2.cloned.1.call-start = ((), (), s32[]{:S(2)}) async-start(), calls=%async_computation.3 | async-start | bytes 4718592 | tf_op jit(solution)/shard_map/reduce_scatter | solution.py:138
  156.4 6.2 %copy-start.2 = (f32[4,4096,64]{1,2,0:T(8,128)S(1)}, f32[4,4096,64]{1,2,0:T(8,128)}, u32[]{:S(2)}) copy-start(f32[4,4096,64]{1,2,0:T(8,128)} %fusion.72) | copy-start | bytes 12582916
  156.4 8.5 %copy-start.6 = (f32[4,4096,64]{1,2,0:T(8,128)S(1)}, f32[4,4096,64]{1,2,0:T(8,128)}, u32[]{:S(2)}) copy-start(f32[4,4096,64]{1,2,0:T(8,128)} %fusion.61) | copy-start | bytes 12582916
  179.8 86.4 %collective-permute-start.2 = (f32[2,1536,128]{1,2,0:T(8,128)}, f32[2,1536,128]{1,2,0:T(8,128)}, u32[]{:S(2)}, u32[]{:S(2)}) collective-permute-start(f32[2,1536,128]{1,2,0:T(8,128)} %get-tuple-element.241), channel_id=1, source_target_pairs={{0,8},{8,16},{16,24},{24,32},{32,40},{40,48},{48,56},{56,64},{64,7... | collective-permute-start | bytes 4718600 | tf_op jit(solution)/shard_map/ppermute | solution.py:18
  188.5 81.0 %collective-permute-start.3 = (f32[2,1536,128]{1,2,0:T(8,128)S(1)}, f32[2,1536,128]{1,2,0:T(8,128)S(1)}, u32[]{:S(2)}, u32[]{:S(2)}) collective-permute-start(f32[2,1536,128]{1,2,0:T(8,128)S(1)} %get-tuple-element.240), channel_id=1, source_target_pairs={{8,0},{16,8},{24,16},{32,24},{40,32},{48,40},{56,48},{64,56},{72,6... | collective-permute-start | bytes 4718600 | tf_op jit(solution)/shard_map/ppermute | solution.py:20
  274.8 48.8 %copy-start.11 = (f32[128,1024]{1,0:T(8,128)S(1)}, f32[128,1024]{1,0:T(8,128)}, u32[]{:S(2)}) copy-start(f32[128,1024]{1,0:T(8,128)} %get-tuple-element.271) | copy-start | bytes 1572868
Sparse Core Ops, SparseCore 0:
  9.8 37.4 all-gather.4
  49.1 37.1 all-gather.2
  145.2 119.0 all-reduce.3
  266.8 54.9 reduce-scatter.1
where the time goes:
time: 332 us; the launch traced here: 331 us
  waiting for transfers between devices  172 us (52%)
  other arithmetic  57.3 us (17%)
  matrix products  44.8 us (13%)
  local copies, waits for them, and re-layouts  25 us (8%)
  starting transfers between devices  17.2 us (5%)
  between operations  14.1 us (4%)
    psum x1, waiting for transfers between devices, on_device(): grad_q_weight, grad_o_weight = lax.psum((query_term, output_term), 'ctx')  69.2 us
    reduce_scatter x1, waiting for transfers between devices, on_device(): lax.psum_scatter(jnp.concatenate([forward_term, input_term], axis=1), 'tp...  44.5 us
    all_gather x1, waiting for transfers between devices, on_device(): lax.all_gather(slow_x, 'tp', axis=0, tiled=True)  37.3 us
    scatter-add x7, other arithmetic, on_device(): grads_ext.at[1, first_row:first_row + window_rows, columns]  17.4 us
    scatter-add x7, other arithmetic, on_device(): grads_ext.at[0, first_row:first_row + window_rows, columns]  17 us
    ppermute x2, starting transfers between devices, extended_2(): lax.ppermute(tail, axis, [(i, (i + 1) % count) for i in range(ends)])  13.2 us
    dot_general x2, matrix products, on_device(): jnp.einsum('lqk,lqd->lkd', prob_half, grad_head, preferred_element_type=j...  11.1 us
    unnamed x37, local copies, waits for them, and re-layouts  9.89 us
  transfers between devices with their start and end apart: 8, of which 6 were waited for; matrix products, arithmetic and copies ran while one was open for 20% of the time, Pallas kernels for 0%

commit v1 on v0

v1 whole, which is shorter than its diff:
```python
import functools

import jax
import jax.numpy as jnp
from jax import lax
from jax.experimental import pallas as pl
from jax.experimental.pallas import tpu as pltpu
from jax.sharding import PartitionSpec as P

BLK = 128
DH = 64
CHUNK = 512
MASKED = -1e30
VMEM_LIMIT = 56 * 1024 * 1024


def contract(a, b, dims):
    return lax.dot_general(a, b, (dims, ((), ())), preferred_element_type=jnp.float32)


def row_split(block):
    lane = lax.broadcasted_iota(jnp.int32, block.shape, 1)
    zero = jnp.zeros_like(block)
    return jnp.concatenate([jnp.where(lane < DH, block, zero), jnp.where(lane >= DH, block, zero)], axis=0)


def column_split(block):
    row = lax.broadcasted_iota(jnp.int32, block.shape, 0)
    zero = jnp.zeros_like(block)
    return jnp.concatenate([jnp.where(row < DH, block, zero), jnp.where(row >= DH, block, zero)], axis=1)


def column_join(wide):
    row = lax.broadcasted_iota(jnp.int32, (wide.shape[0], BLK), 0)
    return jnp.where(row < DH, wide[:, :BLK], wide[:, BLK:])


def load_extended(half, left, own, right, dest, sems):
    rim, rows = left.shape[1], own.shape[1]
    copies = [
        pltpu.make_async_copy(left.at[half], dest.at[pl.ds(0, rim)], sems.at[0]),
        pltpu.make_async_copy(own.at[half], dest.at[pl.ds(rim, rows)], sems.at[1]),
        pltpu.make_async_copy(right.at[half], dest.at[pl.ds(rim + rows, rim)], sems.at[2]),
    ]
    for copy in copies:
        copy.start()
    return copies


def transpose_into(source, dest):
    for first in range(0, source.shape[0], CHUNK):
        dest[:, first : first + CHUNK] = source[first : first + CHUNK, :].T


def forward_kernel(step_rows, window, bias, q, left, own, right, probs, attn, inverse,
                   keys, values, values_t, score, sems_k, sems_v):
    block = pl.program_id(0)

    @pl.when(block == 0)
    def _():
        first = load_extended(1, left, own, right, values, sems_v)
        second = load_extended(0, left, own, right, keys, sems_k)
        for copy in first:
            copy.wait()
        transpose_into(values, values_t)
        for copy in second:
            copy.wait()

    base = block * step_rows
    q_t = column_split(q[...].T)
    top = jnp.full((8, 2 * BLK), -jnp.inf, jnp.float32)
    for c in range(window // CHUNK):
        at = pl.multiple_of(base + c * CHUNK, CHUNK)
        s = contract(keys[pl.ds(at, CHUNK), :], q_t, ((1,), (0,)))
        for j in range(CHUNK // BLK):
            part = s[j * BLK : (j + 1) * BLK] + bias[block, c * (CHUNK // BLK) + j]
            score[c * CHUNK + j * BLK : c * CHUNK + (j + 1) * BLK, :] = part
            top = jnp.maximum(top, jnp.max(part.reshape(BLK // 8, 8, 2 * BLK), axis=0))
    row_max = jnp.max(top, axis=0, keepdims=True)
    total = jnp.zeros((8, 2 * BLK), jnp.float32)
    out = jnp.zeros((BLK, 2 * BLK), jnp.float32)
    for c in range(window // CHUNK):
        at = pl.multiple_of(base + c * CHUNK, CHUNK)
        e = jnp.exp(score[c * CHUNK : (c + 1) * CHUNK, :] - row_max)
        total = total + jnp.sum(e.reshape(CHUNK // 8, 8, 2 * BLK), axis=0)
        half = e.astype(jnp.bfloat16)
        probs[0, c * CHUNK : (c + 1) * CHUNK, :] = half
        out = out + contract(values_t[:, pl.ds(at, CHUNK)], half, ((1,), (0,)))
    inv = 1.0 / jnp.sum(total, axis=0, keepdims=True)
    attn[...] = column_join(out * inv).T.astype(jnp.bfloat16)
    inverse[0] = jnp.broadcast_to(inv, (8, 2 * BLK))


def backward_kernel(step_rows, window, scale, q, grad, attn, inverse, probs, left, own, right,
                    grad_pre, own_grads, left_grads, right_grads,
                    keys, values, keys_t, acc_k, acc_v, sems_k, sems_v):
    block = pl.program_id(0)
    rim, rows = left.shape[1], own.shape[1]
    kept = window - step_rows

    @pl.when(block == 0)
    def _():
        first = load_extended(0, left, own, right, keys, sems_k)
        second = load_extended(1, left, own, right, values, sems_v)
        acc_k[:kept, :] = jnp.zeros((kept, BLK), jnp.float32)
        acc_v[:kept, :] = jnp.zeros((kept, BLK), jnp.float32)
        for copy in first:
            copy.wait()
        transpose_into(keys, keys_t)
        for copy in second:
            copy.wait()

    base = block * step_rows
    inv = inverse[0, :1, :]
    grad_t = grad[...].astype(jnp.float32).T
    attn_t = attn[...].astype(jnp.float32).T
    product = grad_t * attn_t
    delta = jnp.concatenate(
        [jnp.sum(product[:DH], axis=0, keepdims=True), jnp.sum(product[DH:], axis=0, keepdims=True)], axis=1
    ) * inv
    scaled = column_split(grad_t) * inv
    grad_cols = scaled.astype(jnp.bfloat16)
    grad_rows = scaled.T.astype(jnp.bfloat16)
    query_rows = row_split(q[...])
    total = jnp.zeros((BLK, 2 * BLK), jnp.float32)
    for c in range(window // CHUNK):
        at = pl.multiple_of(base + c * CHUNK, CHUNK)
        e = probs[0, c * CHUNK : (c + 1) * CHUNK, :]
        dp = contract(values[pl.ds(at, CHUNK), :], grad_cols, ((1,), (0,)))
        ds = (e.astype(jnp.float32) * (dp - delta)).astype(jnp.bfloat16)
        total = total + contract(keys_t[:, pl.ds(at, CHUNK)], ds, ((1,), (0,)))
        gk = contract(ds, query_rows, ((1,), (0,)))
        gv = contract(e, grad_rows, ((1,), (0,)))
        if c * CHUNK < kept:
            gk = gk + acc_k[pl.ds(at, CHUNK), :]
            gv = gv + acc_v[pl.ds(at, CHUNK), :]
        acc_k[pl.ds(at, CHUNK), :] = gk
        acc_v[pl.ds(at, CHUNK), :] = gv
    grad_pre[...] = (column_join(total) * scale).T.astype(jnp.bfloat16)

    @pl.when(block == pl.num_programs(0) - 1)
    def _():
        for half, acc in ((0, acc_k), (1, acc_v)):
            left_grads[half] = acc[:rim, :].astype(jnp.bfloat16)
            right_grads[half] = acc[rim + rows :, :].astype(jnp.bfloat16)
            own_grads[half] = acc[rim : rim + rows, :]


def whole(shape):
    return pl.BlockSpec(shape, lambda i: (0,) * len(shape))


def attention_forward(bias, q, left, own, right, step_rows, window):
    blocks = q.shape[0] // BLK
    ext = left.shape[1] + own.shape[1] + right.shape[1]
    anywhere = pl.BlockSpec(memory_space=pl.ANY)
    return pl.pallas_call(
        functools.partial(forward_kernel, step_rows, window),
        grid=(blocks,),
        in_specs=[
            pl.BlockSpec(memory_space=pltpu.SMEM),
            pl.BlockSpec((BLK, BLK), lambda i: (i, 0)),
            anywhere, anywhere, anywhere,
        ],
        out_specs=[
            pl.BlockSpec((1, window, 2 * BLK), lambda i: (i, 0, 0)),
            pl.BlockSpec((BLK, BLK), lambda i: (i, 0)),
            pl.BlockSpec((1, 8, 2 * BLK), lambda i: (i, 0, 0)),
        ],
        out_shape=[
            jax.ShapeDtypeStruct((blocks, window, 2 * BLK), jnp.bfloat16),
            jax.ShapeDtypeStruct(q.shape, jnp.bfloat16),
            jax.ShapeDtypeStruct((blocks, 8, 2 * BLK), jnp.float32),
        ],
        scratch_shapes=[
            pltpu.VMEM((ext, BLK), jnp.bfloat16),
            pltpu.VMEM((ext, BLK), jnp.bfloat16),
            pltpu.VMEM((BLK, ext), jnp.bfloat16),
            pltpu.VMEM((window, 2 * BLK), jnp.float32),
            pltpu.SemaphoreType.DMA((3,)),
            pltpu.SemaphoreType.DMA((3,)),
        ],
        compiler_params=pltpu.CompilerParams(
            dimension_semantics=("arbitrary",), vmem_limit_bytes=VMEM_LIMIT
        ),
        cost_estimate=pl.CostEstimate(
            flops=blocks * 4 * window * BLK * BLK * 2, bytes_accessed=14_000_000,
            transcendentals=blocks * window * 2 * BLK,
        ),
        name="attention_forward",
    )(bias, q, left, own, right)


def attention_backward(q, grad, attn, inverse, probs, left, own, right, step_rows, window):
    blocks = q.shape[0] // BLK
    rim, rows = left.shape[1], own.shape[1]
    ext = rim + rows + rim
    anywhere = pl.BlockSpec(memory_space=pl.ANY)
    row_block = pl.BlockSpec((BLK, BLK), lambda i: (i, 0))
    return pl.pallas_call(
        functools.partial(backward_kernel, step_rows, window, DH ** -0.5),
        grid=(blocks,),
        in_specs=[
            row_block, row_block, row_block,
            pl.BlockSpec((1, 8, 2 * BLK), lambda i: (i, 0, 0)),
            pl.BlockSpec((1, window, 2 * BLK), lambda i: (i, 0, 0)),
            anywhere, anywhere, anywhere,
        ],
        out_specs=[row_block, whole((2, rows, BLK)), whole((2, rim, BLK)), whole((2, rim, BLK))],
        out_shape=[
            jax.ShapeDtypeStruct(q.shape, jnp.bfloat16),
            jax.ShapeDtypeStruct((2, rows, BLK), jnp.float32),
            jax.ShapeDtypeStruct((2, rim, BLK), jnp.bfloat16),
            jax.ShapeDtypeStruct((2, rim, BLK), jnp.bfloat16),
        ],
        scratch_shapes=[
            pltpu.VMEM((ext, BLK), jnp.bfloat16),
            pltpu.VMEM((ext, BLK), jnp.bfloat16),
            pltpu.VMEM((BLK, ext), jnp.bfloat16),
            pltpu.VMEM((ext, BLK), jnp.float32),
            pltpu.VMEM((ext, BLK), jnp.float32),
            pltpu.SemaphoreType.DMA((3,)),
            pltpu.SemaphoreType.DMA((3,)),
        ],
        compiler_params=pltpu.CompilerParams(
            dimension_semantics=("arbitrary",), vmem_limit_bytes=VMEM_LIMIT
        ),
        cost_estimate=pl.CostEstimate(
            flops=blocks * 8 * window * BLK * BLK * 2, bytes_accessed=20_000_000, transcendentals=0
        ),
        name="attention_backward",
    )(q, grad, attn, inverse, probs, left, own, right)


def shifted(count, by):
    return [(i, (i + by) % count) for i in range(count)]


def ring_gather(shard, axis):
    count = lax.axis_size(axis)
    here = lax.axis_index(axis)
    rows = shard.shape[0]
    pieces = [(shard, 0)]
    forward = backward = shard
    for step in range(1, count // 2 + 1):
        forward = lax.ppermute(forward, axis, shifted(count, 1))
        pieces.append((forward, -step))
        if step < count - step:
            backward = lax.ppermute(backward, axis, shifted(count, -1))
            pieces.append((backward, step))
    out = jnp.zeros((count * rows,) + shard.shape[1:], shard.dtype)
    for piece, by in pieces:
        out = lax.dynamic_update_slice_in_dim(out, piece, lax.rem(here + by + count, count) * rows, 0)
    return out


def band_bias(band_lists, base_block, query_blocks, half_step, reach_blocks):
    local = jnp.arange(query_blocks, dtype=jnp.int32)
    window_first = base_block + (2 * local + 1) * half_step - reach_blocks
    wanted = window_first[:, None] + jnp.arange(2 * reach_blocks, dtype=jnp.int32)[None, :]
    allowed = jnp.any(band_lists[:, :, None] == wanted[:, None, :], axis=1)
    return jnp.where(allowed, 0.0, MASKED).astype(jnp.float32)


def sum_everywhere(partial, axis):
    count = lax.axis_size(axis)
    shape = partial.shape
    parts = partial.astype(jnp.bfloat16).reshape(count, -1, BLK)
    arrived = lax.all_to_all(parts, axis, 0, 0, tiled=True)
    own = jnp.sum(arrived.astype(jnp.float32), axis=0, keepdims=True).astype(jnp.bfloat16)
    spread = lax.all_to_all(jnp.broadcast_to(own, parts.shape), axis, 0, 0, tiled=True)
    return spread.reshape(shape).astype(jnp.float32)


def on_device(slow_x, q_weight, o_weight, fast_kv, mask_lists, cotangent):
    own_rows, width = slow_x.shape
    tp = lax.axis_size("tp")
    ctx = lax.axis_size("ctx")
    total_rows = own_rows * tp
    query_blocks = total_rows // BLK
    fast_rows = fast_kv.shape[1]
    fast_blocks = fast_rows // BLK
    half_step = fast_blocks // (2 * query_blocks)
    reach_blocks = mask_lists.shape[1] // 2
    rim = (reach_blocks - half_step) * BLK
    window = 2 * reach_blocks * BLK
    step_rows = 2 * half_step * BLK
    scale = DH ** -0.5

    up = [(i, i + 1) for i in range(ctx - 1)]
    down = [(i + 1, i) for i in range(ctx - 1)]
    left = lax.ppermute(fast_kv[:, fast_rows - rim :], "ctx", up)
    right = lax.ppermute(fast_kv[:, :rim], "ctx", down)

    weights = lax.all_gather(jnp.concatenate([o_weight, q_weight.T], axis=1), "tp", axis=0, tiled=True)

    both = ring_gather(jnp.concatenate([slow_x, cotangent], axis=1), "tp")
    rows_x, rows_g = both[:, :width], both[:, width:]

    ctx_index = lax.axis_index("ctx")
    band_lists = lax.dynamic_slice_in_dim(mask_lists, ctx_index * query_blocks, query_blocks, 0)
    bias = band_bias(band_lists, ctx_index * fast_blocks, query_blocks, half_step, reach_blocks)

    queries = (contract(rows_x, q_weight, ((1,), (0,))) * scale).astype(jnp.bfloat16)
    grad_attn = contract(rows_g, o_weight, ((1,), (1,))).astype(jnp.bfloat16)

    probs, attn, inverse = attention_forward(bias, queries, left, fast_kv, right, step_rows, window)
    grad_pre, own_grads, left_grads, right_grads = attention_backward(
        queries, grad_attn, attn, inverse, probs, left, fast_kv, right, step_rows, window
    )

    from_right = lax.ppermute(left_grads, "ctx", down)
    from_left = lax.ppermute(right_grads, "ctx", up)
    own_grads = own_grads.at[:, :rim].add(from_left.astype(jnp.float32))
    own_grads = own_grads.at[:, fast_rows - rim :].add(from_right.astype(jnp.float32))
    grad_kv = own_grads.astype(jnp.bfloat16)

    query_term = contract(rows_x, grad_pre, ((0,), (0,)))
    output_term = contract(attn, rows_g, ((0,), (0,)))
    mixed = jnp.concatenate([attn, grad_pre], axis=1).reshape(tp, own_rows, 2 * BLK)
    mixed = lax.all_to_all(mixed, "tp", 0, 0, tiled=True)
    full = weights.reshape(tp, BLK, 2 * width)
    attended = jnp.einsum(
        "trk,tkn->rn", mixed[:, :, :BLK], full[:, :, :width], preferred_element_type=jnp.float32
    ).astype(jnp.bfloat16)
    grad_slow = jnp.einsum(
        "trk,tkn->rn", mixed[:, :, BLK:], full[:, :, width:], preferred_element_type=jnp.float32
    ).astype(jnp.bfloat16)

    terms = jnp.concatenate([query_term.reshape(-1, BLK), output_term.reshape(-1, BLK)], axis=0)
    terms = sum_everywhere(terms, "ctx")
    half = width * q_weight.shape[1] // BLK
    grad_q_weight = terms[:half].reshape(q_weight.shape)
    grad_o_weight = terms[half:].reshape(o_weight.shape)
    return (attended, grad_slow, grad_q_weight, grad_o_weight, grad_kv)


def solution(mesh):
    in_specs = (
        P(("ctx", "tp"), None),
        P(None, "tp"),
        P("tp", None),
        P(None, "ctx", "tp"),
        P(),
        P(("ctx", "tp"), None),
    )
    out_specs = (
        P(("ctx", "tp"), None),
        P(("ctx", "tp"), None),
        P(None, "tp"),
        P("tp", None),
        P(None, "ctx", "tp"),
    )
    return jax.shard_map(on_device, mesh=mesh, in_specs=in_specs, out_specs=out_specs, check_vma=False)
```

time: 332 us -> 180 us (0.54)
  waiting for transfers between devices: 172 us -> 58.6 us
  other arithmetic: 57.3 us -> 13.5 us
  matrix products: 44.8 us -> 9.45 us
  Pallas kernels: 0 us -> 33.4 us
  starting transfers between devices: 17.2 us -> 40.9 us
  local copies, waits for them, and re-layouts: 25 us -> 8.43 us
    psum x1 -> x0, waiting for transfers between devices: 69.2 us -> none  [on_device(): grad_q_weight, grad_o_weight = lax.psum((query_term, output_term), 'ctx')]
    all_gather x2 -> x1, waiting for transfers between devices: 46.9 us -> 0.01 us  [on_device(): lax.all_gather(jnp.concatenate([o_weight, q_weight.T], axis=1), 'tp', axi...]
    reduce_scatter x1 -> x0, waiting for transfers between devices: 44.5 us -> none  [on_device(): lax.psum_scatter(jnp.concatenate([forward_term, input_term], axis=1), 'tp...]
    dot_general x18 -> x6, matrix products: 44.8 us -> 9.45 us  [the longest x4 4 us: contract(): lax.dot_general(a, b, (dims, ((), ())), preferred_element_type=jnp.float32)]
    scatter-add x16 -> x2, other arithmetic: 40.5 us -> 5.5 us  [the longest x1 2.75 us: on_device(): own_grads = own_grads.at[:, :rim].add(from_left.astype(jnp.float32))]
    pallas_call x0 -> x2, Pallas kernels: none -> 33.4 us  [the longest x1 18.4 us: attention_backward(): pl.pallas_call(functools.partial(backward_kernel, step_rows, window, DH *...]
    ppermute x4 -> x11, waiting for transfers between devices: 11.2 us -> 38.6 us  [the longest x4 38.6 us: ring_gather(): forward = lax.ppermute(forward, axis, shifted(count, 1))]
    all_to_all x0 -> x3, waiting for transfers between devices: none -> 20 us  [the longest x1 8.9 us: sum_everywhere(): lax.all_to_all(jnp.broadcast_to(own, parts.shape), axis, 0, 0, tiled=True)]
  transfers between devices with their start and end apart: 8 -> 15, of which waited for: 6 -> 6; matrix products, arithmetic and copies ran while one was open for 20% -> 12% of each run, Pallas kernels for 0% -> 19%
where the time goes in v1:
time: 180 us; the launch traced here: 179 us
  waiting for transfers between devices  58.6 us (33%)
  starting transfers between devices  40.9 us (23%)
  Pallas kernels  33.4 us (19%)
  between operations  14.4 us (8%)
  other arithmetic  13.5 us (8%)
  matrix products  9.45 us (5%)
  local copies, waits for them, and re-layouts  8.43 us (5%)
    ppermute x4, waiting for transfers between devices, ring_gather(): forward = lax.ppermute(forward, axis, shifted(count, 1))  38.6 us
    pallas_call x1, Pallas kernels, attention_backward(): pl.pallas_call(functools.partial(backward_kernel, step_rows, window, DH *...  18.4 us
    pallas_call x1, Pallas kernels, attention_forward(): pl.pallas_call(functools.partial(forward_kernel, step_rows, window), grid...  15.1 us
    ppermute x3, starting transfers between devices, ring_gather(): backward = lax.ppermute(backward, axis, shifted(count, -1))  9.38 us
    all_to_all x1, waiting for transfers between devices, sum_everywhere(): lax.all_to_all(jnp.broadcast_to(own, parts.shape), axis, 0, 0, tiled=True)  8.9 us
    all_to_all x1, waiting for transfers between devices, sum_everywhere(): arrived = lax.all_to_all(parts, axis, 0, 0, tiled=True)  8.63 us
    all_to_all x1, starting transfers between devices, sum_everywhere(): arrived = lax.all_to_all(parts, axis, 0, 0, tiled=True)  6.78 us
    all_to_all x1, starting transfers between devices, on_device(): mixed = lax.all_to_all(mixed, 'tp', 0, 0, tiled=True)  5.5 us
  transfers between devices with their start and end apart: 15, of which 6 were waited for; matrix products, arithmetic and copies ran while one was open for 12% of the time, Pallas kernels for 19%

profile of v1, /device:TPU:1, one launch (start us, length us, event | category | flops | bytes accessed | tf_op | source)
XLA Modules:
  0.0 178.7 jit_solution(10053117471019805591)
XLA Ops:
  10.4 2.5 %collective-permute-start = (bf16[64,2048]{1,0:T(8,128)(2,1)S(1)}, bf16[64,2048]{1,0:T(8,128)(2,1)}, u32[]{:S(2)}, u32[]{:S(2)}) collective-permute-start(bf16[64,2048]{1,0:T(8,128)(2,1)S(1)} %constant_dynamic-update-slice_fusion), channel_id=1, source_target_pairs={{0,1},{1,2},{2,3},{3,4},{4,5},{5,6},{6,7},{7,0},{8,9},{9,10},{10,1... | collective-permute-start | bytes 786440 | tf_op jit(solution)/shard_map/ppermute | solution.py:246
  12.9 4.0 %collective-permute-start.1 = (bf16[64,2048]{1,0:T(8,128)(2,1)S(1)}, bf16[64,2048]{1,0:T(8,128)(2,1)S(1)}, u32[]{:S(2)}, u32[]{:S(2)}) collective-permute-start(bf16[64,2048]{1,0:T(8,128)(2,1)S(1)} %constant_dynamic-update-slice_fusion), channel_id=1, source_target_pairs={{0,7},{1,0},{2,1},{3,2},{4,3},{5,4},{6,5},{7,6},{8,15},{9,8},{10,9... | collective-permute-start | bytes 786440 | tf_op jit(solution)/shard_map/ppermute | solution.py:249
  17.9 3.9 %collective-permute-start.7 = (bf16[2,1536,128]{2,1,0:T(8,128)(2,1)}, bf16[2,1536,128]{2,1,0:T(8,128)(2,1)S(1)}, u32[]{:S(2)}, u32[]{:S(2)}) collective-permute-start(bf16[2,1536,128]{2,1,0:T(8,128)(2,1)} %get-tuple-element.44), channel_id=1, source_target_pairs={{0,8},{8,16},{16,24},{24,32},{32,40},{40,48},{48,56},{56,64},{64,7... | collective-permute-start | bytes 2359304 | tf_op jit(solution)/shard_map/ppermute | solution.py:292
  21.9 1.9 %collective-permute-start.8 = (bf16[2,1536,128]{2,1,0:T(8,128)(2,1)S(1)}, bf16[2,1536,128]{2,1,0:T(8,128)(2,1)S(1)}, u32[]{:S(2)}, u32[]{:S(2)}) collective-permute-start(bf16[2,1536,128]{2,1,0:T(8,128)(2,1)S(1)} %get-tuple-element.43), channel_id=1, source_target_pairs={{8,0},{16,8},{24,16},{32,24},{40,32},{48,40},{56,48},{64,56},{72,6... | collective-permute-start | bytes 2359304 | tf_op jit(solution)/shard_map/ppermute | solution.py:293
  25.2 2.7 %collective-permute-start.3 = (bf16[64,2048]{1,0:T(8,128)(2,1)S(1)}, bf16[64,2048]{1,0:T(8,128)(2,1)S(1)}, u32[]{:S(2)}, u32[]{:S(2)}) collective-permute-start(bf16[64,2048]{1,0:T(8,128)(2,1)S(1)} %collective-permute-done.1), channel_id=1, source_target_pairs={{0,7},{1,0},{2,1},{3,2},{4,3},{5,4},{6,5},{7,6},{8,15},{9,8},{10,9... | collective-permute-start | bytes 786440 | tf_op jit(solution)/shard_map/ppermute | solution.py:249
  28.8 11.2 %collective-permute-done.2 = bf16[64,2048]{1,0:T(8,128)(2,1)S(1)} collective-permute-done((bf16[64,2048]{1,0:T(8,128)(2,1)}, bf16[64,2048]{1,0:T(8,128)(2,1)S(1)}, u32[]{:S(2)}, u32[]{:S(2)}) %collective-permute-start.2) | collective-permute-done | bytes 262176 | tf_op jit(solution)/shard_map/ppermute | solution.py:246
  40.1 2.7 %collective-permute-start.5 = (bf16[64,2048]{1,0:T(8,128)(2,1)S(1)}, bf16[64,2048]{1,0:T(8,128)(2,1)S(1)}, u32[]{:S(2)}, u32[]{:S(2)}) collective-permute-start(bf16[64,2048]{1,0:T(8,128)(2,1)S(1)} %collective-permute-done.3), channel_id=1, source_target_pairs={{0,7},{1,0},{2,1},{3,2},{4,3},{5,4},{6,5},{7,6},{8,15},{9,8},{10,9... | collective-permute-start | bytes 786440 | tf_op jit(solution)/shard_map/ppermute | solution.py:249
  42.8 12.3 %collective-permute-done.4 = bf16[64,2048]{1,0:T(8,128)(2,1)S(1)} collective-permute-done((bf16[64,2048]{1,0:T(8,128)(2,1)S(1)}, bf16[64,2048]{1,0:T(8,128)(2,1)S(1)}, u32[]{:S(2)}, u32[]{:S(2)}) %collective-permute-start.4) | collective-permute-done | bytes 262176 | tf_op jit(solution)/shard_map/ppermute | solution.py:246
  55.2 15.0 %collective-permute-done.6 = bf16[64,2048]{1,0:T(8,128)(2,1)S(1)} collective-permute-done((bf16[64,2048]{1,0:T(8,128)(2,1)S(1)}, bf16[64,2048]{1,0:T(8,128)(2,1)S(1)}, u32[]{:S(2)}, u32[]{:S(2)}) %collective-permute-start.6) | collective-permute-done | bytes 262176 | tf_op jit(solution)/shard_map/ppermute | solution.py:246
  73.2 15.1 %attention_forward.1 = (bf16[4,4096,256]{2,1,0:T(8,128)(2,1)}, bf16[512,128]{1,0:T(8,128)(2,1)}, f32[4,8,256]{2,1,0:T(8,128)}) custom-call(f32[4,32]{1,0:T(4,128)} %broadcast_select_fusion.bias, bf16[512,128]{1,0:T(8,128)(2,1)} %fusion.11.q, bf16[2,1536,128]{2,1,0:T(8,128)(2,1)} %copy-done.8, bf16[2,4096,128]{2,1,0:T(8,128)(2,1)} %own.3, ...), custom_call_target="tpu_custom_call" | custom-call | flops 2147483648 | bytes 14000000 | tf_op jit(solution)/shard_map/attention_forward/pallas_call | solution.py:157
  89.4 18.4 %attention_backward.1 = (bf16[512,128]{1,0:T(8,128)(2,1)}, f32[2,4096,128]{2,1,0:T(8,128)}, bf16[2,1536,128]{2,1,0:T(8,128)(2,1)}, bf16[2,1536,128]{2,1,0:T(8,128)(2,1)}) custom-call(bf16[512,128]{1,0:T(8,128)(2,1)} %fusion.11.q, bf16[512,128]{1,0:T(8,128)(2,1)} %convolution_convert_fusion.2.grad, bf16[512,128]{1,0:T(8,128)(2,1)} %get-tuple-element.36.attn, ...), custom_call_target="tpu_custom_call" | custom-call | flops 4294967296 | bytes 20000000 | tf_op jit(solution)/shard_map/attention_backward/pallas_call | solution.py:200
  107.8 4.6 %collective-permute-start.9 = (bf16[2,1536,128]{2,1,0:T(8,128)(2,1)}, bf16[2,1536,128]{2,1,0:T(8,128)(2,1)S(1)}, u32[]{:S(2)}, u32[]{:S(2)}) collective-permute-start(bf16[2,1536,128]{2,1,0:T(8,128)(2,1)} %get-tuple-element.41), channel_id=1, source_target_pairs={{0,8},{8,16},{16,24},{24,32},{32,40},{40,48},{48,56},{56,64},{64,7... | collective-permute-start | bytes 2359304 | tf_op jit(solution)/shard_map/ppermute | solution.py:313
  115.1 6.8 %all-to-all-start.1 = ((bf16[32,64,128]{2,1,0:T(8,128)(2,1)}), bf16[32,64,128]{2,1,0:T(8,128)(2,1)S(1)}, u32[]{:S(2)}, u32[]{:S(2)}) async-start(bf16[32,64,128]{2,1,0:T(8,128)(2,1)} %bitcast.5), calls=%async_computation.1 | async-start | bytes 1048576 | tf_op jit(solution)/shard_map/all_to_all | solution.py:269
  121.9 2.1 %collective-permute-start.10 = (bf16[2,1536,128]{2,1,0:T(8,128)(2,1)S(1)}, bf16[2,1536,128]{2,1,0:T(8,128)(2,1)S(1)}, u32[]{:S(2)}, u32[]{:S(2)}) collective-permute-start(bf16[2,1536,128]{2,1,0:T(8,128)(2,1)S(1)} %copy-done.10), channel_id=1, source_target_pairs={{8,0},{16,8},{24,16},{32,24},{40,32},{48,40},{56,48},{64,56},{72,6... | collective-permute-start | bytes 2359304 | tf_op jit(solution)/shard_map/ppermute | solution.py:312
  124.9 8.6 %all-to-all-done.1 = bf16[32,64,128]{2,1,0:T(8,128)(2,1)S(1)} async-done(((bf16[32,64,128]{2,1,0:T(8,128)(2,1)}), bf16[32,64,128]{2,1,0:T(8,128)(2,1)S(1)}, u32[]{:S(2)}, u32[]{:S(2)}) %all-to-all-start.1) | async-done | bytes 524320 | tf_op jit(solution)/shard_map/all_to_all | solution.py:269
  134.5 4.0 %all-to-all-start.2 = ((bf16[32,64,128]{2,1,0:T(8,128)(2,1)}), bf16[32,64,128]{2,1,0:T(8,128)(2,1)S(1)}, u32[]{:S(2)}, u32[]{:S(2)}) async-start(bf16[32,64,128]{2,1,0:T(8,128)(2,1)} %broadcast_in_dim.24), calls=%async_computation.2 | async-start | bytes 1048576 | tf_op jit(solution)/shard_map/all_to_all | solution.py:271
  138.5 2.8 %add_dynamic-update-slice_fusion = f32[2,4096,128]{2,1,0:T(8,128)} fusion(f32[2,4096,128]{2,1,0:T(8,128)} %get-tuple-element.40, bf16[2,1536,128]{2,1,0:T(8,128)(2,1)S(1)} %collective-permute-done.9), kind=kLoop, calls=%fused_computation.6 | loop fusion | flops 786432 | bytes 3932160 | tf_op jit(solution)/shard_map/scatter-add | solution.py:314
  141.2 8.9 %all-to-all-done.2 = bf16[32,64,128]{2,1,0:T(8,128)(2,1)S(1)} async-done(((bf16[32,64,128]{2,1,0:T(8,128)(2,1)}), bf16[32,64,128]{2,1,0:T(8,128)(2,1)S(1)}, u32[]{:S(2)}, u32[]{:S(2)}) %all-to-all-start.2) | async-done | bytes 524320 | tf_op jit(solution)/shard_map/all_to_all | solution.py:271
  150.1 5.5 %all-to-all-start = ((bf16[8,64,256]{2,1,0:T(8,128)(2,1)}), bf16[8,64,256]{2,1,0:T(8,128)(2,1)S(1)}, u32[]{:S(2)}, u32[]{:S(2)}) async-start(bf16[8,64,256]{2,1,0:T(8,128)(2,1)} %bitcast), calls=%async_computation | async-start | bytes 524288 | tf_op jit(solution)/shard_map/all_to_all | solution.py:321
  155.7 2.7 %fusion.4 = f32[2,4096,128]{2,1,0:T(8,128)} fusion(f32[2,4096,128]{2,1,0:T(8,128)} %add_dynamic-update-slice_fusion, bf16[2,1536,128]{2,1,0:T(8,128)(2,1)S(1)} %collective-permute-done.10), kind=kLoop, calls=%fused_computation.5 | loop fusion | flops 786432 | bytes 3932160 | tf_op jit(solution)/shard_map/scatter-add | solution.py:315
  158.4 3.8 %convert_element_type.45 = bf16[2,4096,128]{2,1,0:T(8,128)(2,1)} convert(f32[2,4096,128]{2,1,0:T(8,128)} %fusion.4) | non-fusion elementwise | flops 1048576 | bytes 6291456 | tf_op jit(solution)/shard_map/convert_element_type | solution.py:316
  164.0 2.5 %all-to-all-done = bf16[8,64,256]{2,1,0:T(8,128)(2,1)S(1)} async-done(((bf16[8,64,256]{2,1,0:T(8,128)(2,1)}), bf16[8,64,256]{2,1,0:T(8,128)(2,1)S(1)}, u32[]{:S(2)}, u32[]{:S(2)}) %all-to-all-start) | async-done | bytes 262176 | tf_op jit(solution)/shard_map/all_to_all | solution.py:321
  166.4 2.7 %fusion.12 = bf16[64,1024]{1,0:T(8,128)(2,1)} fusion(bf16[8,128,2048]{2,1,0:T(8,128)(2,1)} %bitcast.19, bf16[8,64,256]{2,1,0:T(8,128)(2,1)S(1)} %all-to-all-done), kind=kOutput, calls=%fused_computation.14 | convolution fusion | flops 134283264 | bytes 2359296 | tf_op jit(solution)/shard_map/trk,tkn->rn/dot_general | solution.py:326
  169.2 2.7 %fusion.15 = bf16[64,1024]{1,0:T(8,128)(2,1)} fusion(bf16[8,128,2048]{2,1,0:T(8,128)(2,1)} %bitcast.20, bf16[8,64,256]{2,1,0:T(8,128)(2,1)S(1)} %all-to-all-done), kind=kOutput, calls=%fused_computation.15 | convolution fusion | flops 134283264 | bytes 2359296 | tf_op jit(solution)/shard_map/trk,tkn->rn/dot_general | solution.py:323
  (67 shorter events, 16.8 us)
Async XLA Ops:
  7.2 16.7 %copy-start = (s32[128,32]{0,1:T(8,128)S(1)}, s32[128,32]{0,1:T(8,128)}, u32[]{:S(2)}) copy-start(s32[128,32]{0,1:T(8,128)} %param.14) | copy-start | bytes 49156
  7.2 3.1 %copy-start.5 = (bf16[64,1024]{1,0:T(8,128)(2,1)S(1)}, bf16[64,1024]{1,0:T(8,128)(2,1)}, u32[]{:S(2)}) copy-start(bf16[64,1024]{1,0:T(8,128)(2,1)} %param.10) | copy-start | bytes 393220
  7.2 3.2 %copy-start.6 = (bf16[64,1024]{1,0:T(8,128)(2,1)S(1)}, bf16[64,1024]{1,0:T(8,128)(2,1)}, u32[]{:S(2)}) copy-start(bf16[64,1024]{1,0:T(8,128)(2,1)} %param.15) | copy-start | bytes 393220
  7.2 9.8 %copy-start.1 = (bf16[2,4096,128]{2,1,0:T(8,128)(2,1)S(1)}, bf16[2,4096,128]{2,1,0:T(8,128)(2,1)}, u32[]{:S(2)}) copy-start(bf16[2,4096,128]{2,1,0:T(8,128)(2,1)} %own.3) | copy-start | bytes 6291460
  7.2 159.2 %all-gather.2.cloned.1.call-start = ((), (), s32[]{:S(2)}) async-start(), calls=%async_computation.3 | async-start | bytes 4718592 | tf_op jit(solution)/shard_map/all_gather | solution.py:295
  10.4 14.7 %collective-permute-start = (bf16[64,2048]{1,0:T(8,128)(2,1)S(1)}, bf16[64,2048]{1,0:T(8,128)(2,1)}, u32[]{:S(2)}, u32[]{:S(2)}) collective-permute-start(bf16[64,2048]{1,0:T(8,128)(2,1)S(1)} %constant_dynamic-update-slice_fusion), channel_id=1, source_target_pairs={{0,1},{1,2},{2,3},{3,4},{4,5},{5,6},{6,7},{7,0},{8,9},{9,10},{10,1... | collective-permute-start | bytes 786440 | tf_op jit(solution)/shard_map/ppermute | solution.py:246
  12.9 12.2 %collective-permute-start.1 = (bf16[64,2048]{1,0:T(8,128)(2,1)S(1)}, bf16[64,2048]{1,0:T(8,128)(2,1)S(1)}, u32[]{:S(2)}, u32[]{:S(2)}) collective-permute-start(bf16[64,2048]{1,0:T(8,128)(2,1)S(1)} %constant_dynamic-update-slice_fusion), channel_id=1, source_target_pairs={{0,7},{1,0},{2,1},{3,2},{4,3},{5,4},{6,5},{7,6},{8,15},{9,8},{10,9... | collective-permute-start | bytes 786440 | tf_op jit(solution)/shard_map/ppermute | solution.py:249
  17.9 53.5 %collective-permute-start.7 = (bf16[2,1536,128]{2,1,0:T(8,128)(2,1)}, bf16[2,1536,128]{2,1,0:T(8,128)(2,1)S(1)}, u32[]{:S(2)}, u32[]{:S(2)}) collective-permute-start(bf16[2,1536,128]{2,1,0:T(8,128)(2,1)} %get-tuple-element.44), channel_id=1, source_target_pairs={{0,8},{8,16},{16,24},{24,32},{32,40},{40,48},{48,56},{56,64},{64,7... | collective-permute-start | bytes 2359304 | tf_op jit(solution)/shard_map/ppermute | solution.py:292
  21.9 49.5 %collective-permute-start.8 = (bf16[2,1536,128]{2,1,0:T(8,128)(2,1)S(1)}, bf16[2,1536,128]{2,1,0:T(8,128)(2,1)S(1)}, u32[]{:S(2)}, u32[]{:S(2)}) collective-permute-start(bf16[2,1536,128]{2,1,0:T(8,128)(2,1)S(1)} %get-tuple-element.43), channel_id=1, source_target_pairs={{8,0},{16,8},{24,16},{32,24},{40,32},{48,40},{56,48},{64,56},{72,6... | collective-permute-start | bytes 2359304 | tf_op jit(solution)/shard_map/ppermute | solution.py:293
  25.0 45.3 %copy-start.3 = (bf16[1024,128]{1,0:T(8,128)(2,1)S(1)}, bf16[1024,128]{1,0:T(8,128)(2,1)}, u32[]{:S(2)}) copy-start(bf16[1024,128]{1,0:T(8,128)(2,1)} %param.11) | copy-start | bytes 786436
  25.1 15.0 %collective-permute-start.2 = (bf16[64,2048]{1,0:T(8,128)(2,1)}, bf16[64,2048]{1,0:T(8,128)(2,1)S(1)}, u32[]{:S(2)}, u32[]{:S(2)}) collective-permute-start(bf16[64,2048]{1,0:T(8,128)(2,1)} %collective-permute-done), channel_id=1, source_target_pairs={{0,1},{1,2},{2,3},{3,4},{4,5},{5,6},{6,7},{7,0},{8,9},{9,10},{10,1... | collective-permute-start | bytes 786440 | tf_op jit(solution)/shard_map/ppermute | solution.py:246
  25.2 14.9 %collective-permute-start.3 = (bf16[64,2048]{1,0:T(8,128)(2,1)S(1)}, bf16[64,2048]{1,0:T(8,128)(2,1)S(1)}, u32[]{:S(2)}, u32[]{:S(2)}) collective-permute-start(bf16[64,2048]{1,0:T(8,128)(2,1)S(1)} %collective-permute-done.1), channel_id=1, source_target_pairs={{0,7},{1,0},{2,1},{3,2},{4,3},{5,4},{6,5},{7,6},{8,15},{9,8},{10,9... | collective-permute-start | bytes 786440 | tf_op jit(solution)/shard_map/ppermute | solution.py:249
  40.1 15.1 %collective-permute-start.4 = (bf16[64,2048]{1,0:T(8,128)(2,1)S(1)}, bf16[64,2048]{1,0:T(8,128)(2,1)S(1)}, u32[]{:S(2)}, u32[]{:S(2)}) collective-permute-start(bf16[64,2048]{1,0:T(8,128)(2,1)S(1)} %collective-permute-done.2), channel_id=1, source_target_pairs={{0,1},{1,2},{2,3},{3,4},{4,5},{5,6},{6,7},{7,0},{8,9},{9,10},{10,1... | collective-permute-start | bytes 786440 | tf_op jit(solution)/shard_map/ppermute | solution.py:246
  40.1 15.1 %collective-permute-start.5 = (bf16[64,2048]{1,0:T(8,128)(2,1)S(1)}, bf16[64,2048]{1,0:T(8,128)(2,1)S(1)}, u32[]{:S(2)}, u32[]{:S(2)}) collective-permute-start(bf16[64,2048]{1,0:T(8,128)(2,1)S(1)} %collective-permute-done.3), channel_id=1, source_target_pairs={{0,7},{1,0},{2,1},{3,2},{4,3},{5,4},{6,5},{7,6},{8,15},{9,8},{10,9... | collective-permute-start | bytes 786440 | tf_op jit(solution)/shard_map/ppermute | solution.py:249
  55.1 15.1 %collective-permute-start.6 = (bf16[64,2048]{1,0:T(8,128)(2,1)S(1)}, bf16[64,2048]{1,0:T(8,128)(2,1)S(1)}, u32[]{:S(2)}, u32[]{:S(2)}) collective-permute-start(bf16[64,2048]{1,0:T(8,128)(2,1)S(1)} %collective-permute-done.4), channel_id=1, source_target_pairs={{0,1},{1,2},{2,3},{3,4},{4,5},{5,6},{6,7},{7,0},{8,9},{9,10},{10,1... | collective-permute-start | bytes 786440 | tf_op jit(solution)/shard_map/ppermute | solution.py:246
  71.4 16.9 %copy-start.4 = (bf16[128,1024]{1,0:T(8,128)(2,1)S(1)}, bf16[128,1024]{1,0:T(8,128)(2,1)}, u32[]{:S(2)}) copy-start(bf16[128,1024]{1,0:T(8,128)(2,1)} %param.12) | copy-start | bytes 786436
  89.4 22.9 %copy-start.2 = (bf16[512,128]{1,0:T(8,128)(2,1)S(1)}, bf16[512,128]{1,0:T(8,128)(2,1)}, u32[]{:S(2)}) copy-start(bf16[512,128]{1,0:T(8,128)(2,1)} %get-tuple-element.36.attn) | copy-start | bytes 393220
  107.8 30.7 %collective-permute-start.9 = (bf16[2,1536,128]{2,1,0:T(8,128)(2,1)}, bf16[2,1536,128]{2,1,0:T(8,128)(2,1)S(1)}, u32[]{:S(2)}, u32[]{:S(2)}) collective-permute-start(bf16[2,1536,128]{2,1,0:T(8,128)(2,1)} %get-tuple-element.41), channel_id=1, source_target_pairs={{0,8},{8,16},{16,24},{24,32},{32,40},{40,48},{48,56},{56,64},{64,7... | collective-permute-start | bytes 2359304 | tf_op jit(solution)/shard_map/ppermute | solution.py:313
  112.7 9.2 %copy-start.10 = (bf16[2,1536,128]{2,1,0:T(8,128)(2,1)S(1)}, bf16[2,1536,128]{2,1,0:T(8,128)(2,1)}, u32[]{:S(2)}) copy-start(bf16[2,1536,128]{2,1,0:T(8,128)(2,1)} %get-tuple-element.42) | copy-start | bytes 2359300
  112.7 11.4 %copy-start.7 = (bf16[512,128]{1,0:T(8,128)(2,1)S(1)}, bf16[512,128]{1,0:T(8,128)(2,1)}, u32[]{:S(2)}) copy-start(bf16[512,128]{1,0:T(8,128)(2,1)} %get-tuple-element.39) | copy-start | bytes 393220
  115.1 18.3 %all-to-all-start.1 = ((bf16[32,64,128]{2,1,0:T(8,128)(2,1)}), bf16[32,64,128]{2,1,0:T(8,128)(2,1)S(1)}, u32[]{:S(2)}, u32[]{:S(2)}) async-start(bf16[32,64,128]{2,1,0:T(8,128)(2,1)} %bitcast.5), calls=%async_computation.1 | async-start | bytes 1048576 | tf_op jit(solution)/shard_map/all_to_all | solution.py:269
  121.9 33.7 %collective-permute-start.10 = (bf16[2,1536,128]{2,1,0:T(8,128)(2,1)S(1)}, bf16[2,1536,128]{2,1,0:T(8,128)(2,1)S(1)}, u32[]{:S(2)}, u32[]{:S(2)}) collective-permute-start(bf16[2,1536,128]{2,1,0:T(8,128)(2,1)S(1)} %copy-done.10), channel_id=1, source_target_pairs={{8,0},{16,8},{24,16},{32,24},{40,32},{48,40},{56,48},{64,56},{72,6... | collective-permute-start | bytes 2359304 | tf_op jit(solution)/shard_map/ppermute | solution.py:312
  134.5 15.7 %all-to-all-start.2 = ((bf16[32,64,128]{2,1,0:T(8,128)(2,1)}), bf16[32,64,128]{2,1,0:T(8,128)(2,1)S(1)}, u32[]{:S(2)}, u32[]{:S(2)}) async-start(bf16[32,64,128]{2,1,0:T(8,128)(2,1)} %broadcast_in_dim.24), calls=%async_computation.2 | async-start | bytes 1048576 | tf_op jit(solution)/shard_map/all_to_all | solution.py:271
  150.1 16.3 %all-to-all-start = ((bf16[8,64,256]{2,1,0:T(8,128)(2,1)}), bf16[8,64,256]{2,1,0:T(8,128)(2,1)S(1)}, u32[]{:S(2)}, u32[]{:S(2)}) async-start(bf16[8,64,256]{2,1,0:T(8,128)(2,1)} %bitcast), calls=%async_computation | async-start | bytes 524288 | tf_op jit(solution)/shard_map/all_to_all | solution.py:321
  (2 other events, 1.8 us)
Sparse Core Ops, SparseCore 0:
  10.4 75.0 all-gather.1

commit v2 on v1

v2 whole, which is shorter than its diff:
```python
import functools

import jax
import jax.numpy as jnp
from jax import lax
from jax.experimental import pallas as pl
from jax.experimental.pallas import tpu as pltpu
from jax.sharding import PartitionSpec as P

BLK = 128
DH = 64
CHUNK = 512
MASKED = -1e30
VMEM_LIMIT = 56 * 1024 * 1024


def contract(a, b, dims):
    return lax.dot_general(a, b, (dims, ((), ())), preferred_element_type=jnp.float32)


def row_split(block):
    lane = lax.broadcasted_iota(jnp.int32, block.shape, 1)
    zero = jnp.zeros_like(block)
    return jnp.concatenate([jnp.where(lane < DH, block, zero), jnp.where(lane >= DH, block, zero)], axis=0)


def column_split(block):
    row = lax.broadcasted_iota(jnp.int32, block.shape, 0)
    zero = jnp.zeros_like(block)
    return jnp.concatenate([jnp.where(row < DH, block, zero), jnp.where(row >= DH, block, zero)], axis=1)


def column_join(wide):
    row = lax.broadcasted_iota(jnp.int32, (wide.shape[0], BLK), 0)
    return jnp.where(row < DH, wide[:, :BLK], wide[:, BLK:])


def load_extended(half, left, own, right, dest, sems):
    rim, rows = left.shape[1], own.shape[1]
    copies = [
        pltpu.make_async_copy(left.at[half], dest.at[pl.ds(0, rim)], sems.at[0]),
        pltpu.make_async_copy(own.at[half], dest.at[pl.ds(rim, rows)], sems.at[1]),
        pltpu.make_async_copy(right.at[half], dest.at[pl.ds(rim + rows, rim)], sems.at[2]),
    ]
    for copy in copies:
        copy.start()
    return copies


def transpose_kernel(left, own, right, out):
    first = 0
    for piece in (left, own, right):
        rows = piece.shape[1]
        for row in range(0, rows, CHUNK):
            out[0, :, first + row : first + row + CHUNK] = piece[0, row : row + CHUNK, :].T
        first += rows


def forward_kernel(step_rows, window, scale, bias, x, weight, left, own, right, flipped,
                   probs, attn, factor, queries, keys, values_t, parts, sems_k, sem_v):
    block = pl.program_id(0)

    @pl.when(block == 0)
    def _():
        first = load_extended(0, left, own, right, keys, sems_k)
        second = pltpu.make_async_copy(flipped.at[1], values_t, sem_v)
        second.start()
        for copy in first:
            copy.wait()
        second.wait()

    base = block * step_rows
    chunks = window // CHUNK
    per = CHUNK // BLK
    q = (contract(x[...], weight[...], ((1,), (0,))) * scale).astype(jnp.bfloat16)
    queries[...] = q
    q_t = column_split(q.T)
    at = lambda c: pl.ds(pl.multiple_of(base + c * CHUNK, CHUNK), CHUNK)
    scores = lambda c: contract(keys[at(c), :], q_t, ((1,), (0,)))
    tops, sums = [], []
    ahead, held = scores(0), None

    def weigh(c, half):
        parts[c] = contract(values_t[:, at(c)], half, ((1,), (0,)))

    for c in range(chunks):
        s = ahead
        if c + 1 < chunks:
            ahead = scores(c + 1)
        s = jnp.concatenate([s[j * BLK : (j + 1) * BLK] + bias[block, c * per + j] for j in range(per)], axis=0)
        top = jnp.max(jnp.max(s.reshape(CHUNK // 8, 8, 2 * BLK), axis=0), axis=0, keepdims=True)
        e = jnp.exp(s - top)
        tops.append(top)
        sums.append(jnp.sum(jnp.sum(e.reshape(CHUNK // 8, 8, 2 * BLK), axis=0), axis=0, keepdims=True))
        half = e.astype(jnp.bfloat16)
        probs[0, c * CHUNK : (c + 1) * CHUNK, :] = half
        if held is not None:
            weigh(c - 1, held)
        held = half
    weigh(chunks - 1, held)
    tops = jnp.concatenate(tops, axis=0)
    sums = jnp.concatenate(sums, axis=0)
    f = jnp.exp(tops - jnp.max(tops, axis=0, keepdims=True))
    f = f * (1.0 / jnp.sum(f * sums, axis=0, keepdims=True))
    out = parts[0] * f[:1]
    for c in range(1, chunks):
        out = out + parts[c] * f[c : c + 1]
    attn[...] = column_join(out).T.astype(jnp.bfloat16)
    factor[0] = f


def backward_kernel(step_rows, window, scale, x, g, weight, queries, attn, factor, probs,
                    left, own, right, flipped,
                    grad_pre, own_grads, left_grads, right_grads, terms,
                    values, keys_t, acc_k, acc_v, acc_q, acc_o, sems_v, sem_k):
    block = pl.program_id(0)
    rim, rows = left.shape[1], own.shape[1]
    kept = window - step_rows
    chunks = window // CHUNK

    @pl.when(block == 0)
    def _():
        first = load_extended(1, left, own, right, values, sems_v)
        second = pltpu.make_async_copy(flipped.at[0], keys_t, sem_k)
        second.start()
        acc_k[:kept, :] = jnp.zeros((kept, BLK), jnp.float32)
        acc_v[:kept, :] = jnp.zeros((kept, BLK), jnp.float32)
        acc_q[...] = jnp.zeros(acc_q.shape, jnp.float32)
        acc_o[...] = jnp.zeros(acc_o.shape, jnp.float32)
        for copy in first:
            copy.wait()
        second.wait()

    base = block * step_rows
    at = lambda c: pl.ds(pl.multiple_of(base + c * CHUNK, CHUNK), CHUNK)
    grad = contract(g[...], weight[...], ((1,), (1,))).astype(jnp.bfloat16).astype(jnp.float32)
    grad_t = grad.T
    product = grad_t * attn[...].astype(jnp.float32).T
    delta = jnp.concatenate(
        [jnp.sum(product[:DH], axis=0, keepdims=True), jnp.sum(product[DH:], axis=0, keepdims=True)], axis=1
    )
    wide, tall = column_split(grad_t), row_split(grad)
    query_rows = row_split(queries[...])
    f = factor[0]
    f_t = f.T
    lift = lambda c: contract(values[at(c), :], (wide * f[c : c + 1]).astype(jnp.bfloat16), ((1,), (0,)))
    total = jnp.zeros((BLK, 2 * BLK), jnp.float32)
    ahead = lift(0)
    for c in range(chunks):
        dp = ahead
        if c + 1 < chunks:
            ahead = lift(c + 1)
        e = probs[0, c * CHUNK : (c + 1) * CHUNK, :]
        ds = (e.astype(jnp.float32) * (dp - delta * f[c : c + 1])).astype(jnp.bfloat16)
        total = total + contract(keys_t[:, at(c)], ds, ((1,), (0,)))
        gk = contract(ds, query_rows, ((1,), (0,)))
        gv = contract(e, (tall * f_t[:, c : c + 1]).astype(jnp.bfloat16), ((1,), (0,)))
        if c * CHUNK < kept:
            gk = gk + acc_k[at(c), :]
            gv = gv + acc_v[at(c), :]
        acc_k[at(c), :] = gk
        acc_v[at(c), :] = gv
    pre = (column_join(total) * scale).T.astype(jnp.bfloat16)
    grad_pre[...] = pre
    acc_q[...] += contract(x[...], pre, ((0,), (0,)))
    acc_o[...] += contract(g[...], attn[...], ((0,), (0,)))

    @pl.when(block == pl.num_programs(0) - 1)
    def _():
        for half, acc in ((0, acc_k), (1, acc_v)):
            left_grads[half] = acc[:rim, :].astype(jnp.bfloat16)
            right_grads[half] = acc[rim + rows :, :].astype(jnp.bfloat16)
            own_grads[half] = acc[rim : rim + rows, :]
        count, both, _ = terms.shape
        cut = both // 2
        terms[:, :cut, :] = acc_q[...].astype(jnp.bfloat16).reshape(count, cut, BLK)
        terms[:, cut:, :] = acc_o[...].astype(jnp.bfloat16).reshape(count, cut, BLK)


def combine_kernel(own, from_left, from_right, out):
    rows, rim = own.shape[1], from_left.shape[1]
    for half in range(2):
        for first in range(0, rows, CHUNK):
            part = own[half, first : first + CHUNK, :]
            if first < rim:
                part = part + from_left[half, first : first + CHUNK, :].astype(jnp.float32)
            if first >= rows - rim:
                start = first - (rows - rim)
                part = part + from_right[half, start : start + CHUNK, :].astype(jnp.float32)
            out[half, first : first + CHUNK, :] = part.astype(jnp.bfloat16)


def params(limit=VMEM_LIMIT):
    return pltpu.CompilerParams(dimension_semantics=("arbitrary",), vmem_limit_bytes=limit)


ANYWHERE = pl.BlockSpec(memory_space=pl.ANY)
ROW_BLOCK = pl.BlockSpec((BLK, BLK), lambda i: (i, 0))
INVERSE = pl.BlockSpec((1, 8, 2 * BLK), lambda i: (i, 0, 0))


def flip_keys_values(left, own, right):
    rim, rows = left.shape[1], own.shape[1]
    ext = 2 * rim + rows
    half = lambda size: pl.BlockSpec((1, size, BLK), lambda i: (i, 0, 0))
    return pl.pallas_call(
        transpose_kernel,
        grid=(2,),
        in_specs=[half(rim), half(rows), half(rim)],
        out_specs=pl.BlockSpec((1, BLK, ext), lambda i: (i, 0, 0)),
        out_shape=jax.ShapeDtypeStruct((2, BLK, ext), jnp.bfloat16),
        compiler_params=params(),
        cost_estimate=pl.CostEstimate(flops=0, bytes_accessed=8_000_000, transcendentals=0),
        name="flip_keys_values",
    )(left, own, right)


def attention_forward(bias, x, weight, left, own, right, flipped, step_rows, window):
    blocks = x.shape[0] // BLK
    width = x.shape[1]
    ext = flipped.shape[2]
    chunks = window // CHUNK
    return pl.pallas_call(
        functools.partial(forward_kernel, step_rows, window, DH ** -0.5),
        grid=(blocks,),
        in_specs=[
            pl.BlockSpec(memory_space=pltpu.SMEM),
            pl.BlockSpec((BLK, width), lambda i: (i, 0)),
            pl.BlockSpec(weight.shape, lambda i: (0, 0)),
        ] + [ANYWHERE] * 4,
        out_specs=[
            pl.BlockSpec((1, window, 2 * BLK), lambda i: (i, 0, 0)),
            ROW_BLOCK,
            pl.BlockSpec((1, chunks, 2 * BLK), lambda i: (i, 0, 0)),
            ROW_BLOCK,
        ],
        out_shape=[
            jax.ShapeDtypeStruct((blocks, window, 2 * BLK), jnp.bfloat16),
            jax.ShapeDtypeStruct((blocks * BLK, BLK), jnp.bfloat16),
            jax.ShapeDtypeStruct((blocks, chunks, 2 * BLK), jnp.float32),
            jax.ShapeDtypeStruct((blocks * BLK, BLK), jnp.bfloat16),
        ],
        scratch_shapes=[
            pltpu.VMEM((ext, BLK), jnp.bfloat16),
            pltpu.VMEM((BLK, ext), jnp.bfloat16),
            pltpu.VMEM((chunks, BLK, 2 * BLK), jnp.float32),
            pltpu.SemaphoreType.DMA((3,)),
            pltpu.SemaphoreType.DMA,
        ],
        compiler_params=params(),
        cost_estimate=pl.CostEstimate(
            flops=blocks * 16 * window * BLK * BLK * 2, bytes_accessed=14_000_000,
            transcendentals=blocks * window * 2 * BLK,
        ),
        name="attention_forward",
    )(bias, x, weight, left, own, right, flipped)


def attention_backward(x, g, weight, queries, attn, factor, probs, left, own, right, flipped, step_rows, parts):
    blocks, window, _ = probs.shape
    width = x.shape[1]
    rim, rows = left.shape[1], own.shape[1]
    ext = flipped.shape[2]
    whole = lambda *shape: pl.BlockSpec(shape, lambda i: (0,) * len(shape))
    row_wide = pl.BlockSpec((BLK, width), lambda i: (i, 0))
    both = 2 * width // parts
    return pl.pallas_call(
        functools.partial(backward_kernel, step_rows, window, DH ** -0.5),
        grid=(blocks,),
        in_specs=[
            row_wide, row_wide, whole(*weight.shape), ROW_BLOCK, ROW_BLOCK,
            pl.BlockSpec((1,) + factor.shape[1:], lambda i: (i, 0, 0)),
            pl.BlockSpec((1, window, 2 * BLK), lambda i: (i, 0, 0)),
        ] + [ANYWHERE] * 4,
        out_specs=[
            ROW_BLOCK, whole(2, rows, BLK), whole(2, rim, BLK), whole(2, rim, BLK), whole(parts, both, BLK),
        ],
        out_shape=[
            jax.ShapeDtypeStruct(attn.shape, jnp.bfloat16),
            jax.ShapeDtypeStruct((2, rows, BLK), jnp.float32),
            jax.ShapeDtypeStruct((2, rim, BLK), jnp.bfloat16),
            jax.ShapeDtypeStruct((2, rim, BLK), jnp.bfloat16),
            jax.ShapeDtypeStruct((parts, both, BLK), jnp.bfloat16),
        ],
        scratch_shapes=[
            pltpu.VMEM((ext, BLK), jnp.bfloat16),
            pltpu.VMEM((BLK, ext), jnp.bfloat16),
            pltpu.VMEM((ext, BLK), jnp.float32),
            pltpu.VMEM((ext, BLK), jnp.float32),
            pltpu.VMEM((width, BLK), jnp.float32),
            pltpu.VMEM((width, BLK), jnp.float32),
            pltpu.SemaphoreType.DMA((3,)),
            pltpu.SemaphoreType.DMA,
        ],
        compiler_params=params(),
        cost_estimate=pl.CostEstimate(
            flops=blocks * 20 * window * BLK * BLK * 2, bytes_accessed=20_000_000, transcendentals=0
        ),
        name="attention_backward",
    )(x, g, weight, queries, attn, factor, probs, left, own, right, flipped)


def combine_grads(own, from_left, from_right):
    return pl.pallas_call(
        combine_kernel,
        out_shape=jax.ShapeDtypeStruct(own.shape, jnp.bfloat16),
        compiler_params=pltpu.CompilerParams(vmem_limit_bytes=VMEM_LIMIT),
        cost_estimate=pl.CostEstimate(flops=1_000_000, bytes_accessed=8_000_000, transcendentals=0),
        name="combine_grads",
    )(own, from_left, from_right)


def shifted(count, by):
    return [(i, (i + by) % count) for i in range(count)]


def ring_gather(shard, axis, ready, at_step):
    count = lax.axis_size(axis)
    here = lax.axis_index(axis)
    rows = shard.shape[0]
    pieces = [(shard, 0)]
    forward = backward = shard
    for step in range(1, count // 2 + 1):
        if step == at_step:
            forward, backward, ready = lax.optimization_barrier((forward, backward, ready))
        forward = lax.ppermute(forward, axis, shifted(count, 1))
        pieces.append((forward, -step))
        if step < count - step:
            backward = lax.ppermute(backward, axis, shifted(count, -1))
            pieces.append((backward, step))
    out = jnp.zeros((count * rows,) + shard.shape[1:], shard.dtype)
    for piece, by in pieces:
        out = lax.dynamic_update_slice_in_dim(out, piece, lax.rem(here + by + count, count) * rows, 0)
    return out, ready


def band_bias(band_lists, base_block, query_blocks, half_step, reach_blocks):
    local = jnp.arange(query_blocks, dtype=jnp.int32)
    window_first = base_block + (2 * local + 1) * half_step - reach_blocks
    wanted = window_first[:, None] + jnp.arange(2 * reach_blocks, dtype=jnp.int32)[None, :]
    allowed = jnp.any(band_lists[:, :, None] == wanted[:, None, :], axis=1)
    return jnp.where(allowed, 0.0, MASKED).astype(jnp.float32)


def added(arrived):
    return jnp.sum(arrived.astype(jnp.float32), axis=0, keepdims=True).astype(jnp.bfloat16)


def exchange(parts, axis):
    return lax.all_to_all(parts, axis, 0, 0, tiled=True)


def on_device(slow_x, q_weight, o_weight, fast_kv, mask_lists, cotangent):
    own_rows, width = slow_x.shape
    tp = lax.axis_size("tp")
    ctx = lax.axis_size("ctx")
    total_rows = own_rows * tp
    query_blocks = total_rows // BLK
    fast_rows = fast_kv.shape[1]
    fast_blocks = fast_rows // BLK
    half_step = fast_blocks // (2 * query_blocks)
    reach_blocks = mask_lists.shape[1] // 2
    rim = (reach_blocks - half_step) * BLK
    window = 2 * reach_blocks * BLK
    step_rows = 2 * half_step * BLK
    scale = DH ** -0.5

    up = [(i, i + 1) for i in range(ctx - 1)]
    down = [(i + 1, i) for i in range(ctx - 1)]
    left = lax.ppermute(fast_kv[:, fast_rows - rim :], "ctx", up)
    right = lax.ppermute(fast_kv[:, :rim], "ctx", down)

    rows_g = lax.all_gather(cotangent, "tp", axis=0, tiled=True)
    ctx_index = lax.axis_index("ctx")
    even = ctx_index % 2 == 0
    band_lists = lax.dynamic_slice_in_dim(mask_lists, ctx_index * query_blocks, query_blocks, 0)
    bias = band_bias(band_lists, ctx_index * fast_blocks, query_blocks, half_step, reach_blocks)
    shard = jnp.where(even, o_weight, q_weight.T)
    flipped = flip_keys_values(left, fast_kv, right)
    rows_x, (flipped, bias, shard) = ring_gather(slow_x, "tp", (flipped, bias, shard), 3)

    probs, attn, factor, queries = attention_forward(
        bias, rows_x, q_weight, left, fast_kv, right, flipped, step_rows, window
    )
    shard, rows_g, attn = lax.optimization_barrier((shard, rows_g, attn))
    mine = lax.all_gather(shard, "tp", axis=0, tiled=True)
    grad_pre, own_grads, left_grads, right_grads, terms = attention_backward(
        rows_x, rows_g, o_weight, queries, attn, factor, probs, left, fast_kv, right, flipped, step_rows, ctx
    )
    own_terms = added(exchange(terms, "ctx"))
    mine, own_terms = lax.optimization_barrier((mine, own_terms))
    other = lax.ppermute(mine, "ctx", [(i, i ^ 1) for i in range(ctx)])
    from_right = lax.ppermute(left_grads, "ctx", down)
    from_left = lax.ppermute(right_grads, "ctx", up)
    mixed = jnp.concatenate([attn, grad_pre], axis=1).reshape(tp, own_rows, 2 * BLK)
    mixed = exchange(mixed, "tp")
    summed = exchange(jnp.broadcast_to(own_terms, terms.shape), "ctx")
    grad_kv = combine_grads(own_grads, from_left, from_right)

    first = jnp.where(even, mixed[:, :, :BLK], mixed[:, :, BLK:])
    second = jnp.where(even, mixed[:, :, BLK:], mixed[:, :, :BLK])
    project = lambda rows, full: jnp.einsum(
        "trk,tkn->rn", rows, full.reshape(tp, BLK, width), preferred_element_type=jnp.float32
    ).astype(jnp.bfloat16)
    first = project(first, mine)
    second = project(second, other)
    attended = jnp.where(even, first, second)
    grad_slow = jnp.where(even, second, first)

    cut = terms.shape[1] // 2
    grad_q_weight = summed[:, :cut].astype(jnp.float32).reshape(q_weight.shape)
    grad_o_weight = summed[:, cut:].astype(jnp.float32).reshape(q_weight.shape).T
    return (attended, grad_slow, grad_q_weight, grad_o_weight, grad_kv)


def solution(mesh):
    in_specs = (
        P(("ctx", "tp"), None),
        P(None, "tp"),
        P("tp", None),
        P(None, "ctx", "tp"),
        P(),
        P(("ctx", "tp"), None),
    )
    out_specs = (
        P(("ctx", "tp"), None),
        P(("ctx", "tp"), None),
        P(None, "tp"),
        P("tp", None),
        P(None, "ctx", "tp"),
    )
    return jax.shard_map(on_device, mesh=mesh, in_specs=in_specs, out_specs=out_specs, check_vma=False)
```

time: 180 us -> 163 us (0.906)
  waiting for transfers between devices: 58.6 us -> 19 us
  blocking collectives: 0 us -> 37.7 us
  other arithmetic: 13.5 us -> 3.41 us
  starting transfers between devices: 40.9 us -> 34.2 us
  Pallas kernels: 33.4 us -> 39.8 us
  matrix products: 9.45 us -> 3.25 us
  local copies, waits for them, and re-layouts: 8.43 us -> 10.6 us
    all_to_all x0 -> x2, blocking collectives: none -> 37.7 us  [exchange(): return lax.all_to_all(parts, axis, 0, 0, tiled=True)]
    ppermute x4, waiting for transfers between devices: 38.6 us -> 11.8 us  [ring_gather(): forward = lax.ppermute(forward, axis, shifted(count, 1))]
    all_to_all x3 -> x1, waiting for transfers between devices: 20 us -> 4.84 us  [exchange(): return lax.all_to_all(parts, axis, 0, 0, tiled=True)]
    all_to_all x3 -> x1, starting transfers between devices: 16.3 us -> 7.43 us  [exchange(): return lax.all_to_all(parts, axis, 0, 0, tiled=True)]
    dot_general x6 -> x2, matrix products: 9.45 us -> 3.25 us  [on_device(): jnp.einsum('trk,tkn->rn', rows, full.reshape(tp, BLK, width), preferred_e...]
    pallas_call x1 -> x3, Pallas kernels: 15.1 us -> 21.2 us  [the longest x1 13 us: attention_forward(): pl.pallas_call(functools.partial(forward_kernel, step_rows, window, DH **...]
    scatter-add x2 -> x0, other arithmetic: 5.5 us -> none  [the longest x1 2.75 us: on_device(): own_grads = own_grads.at[:, :rim].add(from_left.astype(jnp.float32))]
    convert_element_type x1 -> x0, other arithmetic: 3.78 us -> none  [on_device(): grad_kv = own_grads.astype(jnp.bfloat16)]
  transfers between devices with their start and end apart: 15 -> 15, of which waited for: 6 -> 5; matrix products, arithmetic and copies ran while one was open for 12% -> 6% of each run, Pallas kernels for 19% -> 25%
where the time goes in v2:
time: 163 us; the launch traced here: 162 us
  Pallas kernels  39.8 us (24%)
  blocking collectives  37.7 us (23%)
  starting transfers between devices  34.2 us (21%)
  waiting for transfers between devices  19 us (12%)
  between operations  14.3 us (9%)
  local copies, waits for them, and re-layouts  10.6 us (7%)
  other arithmetic  3.41 us (2%)
  matrix products  3.25 us (2%)
    all_to_all x2, blocking collectives, exchange(): return lax.all_to_all(parts, axis, 0, 0, tiled=True)  37.7 us
    pallas_call x1, Pallas kernels, attention_backward(): pl.pallas_call(functools.partial(backward_kernel, step_rows, window, DH *...  18.6 us
    pallas_call x1, Pallas kernels, attention_forward(): pl.pallas_call(functools.partial(forward_kernel, step_rows, window, DH **...  13 us
    ppermute x4, waiting for transfers between devices, ring_gather(): forward = lax.ppermute(forward, axis, shifted(count, 1))  11.8 us
    ppermute x3, starting transfers between devices, ring_gather(): backward = lax.ppermute(backward, axis, shifted(count, -1))  9.42 us
    all_to_all x1, starting transfers between devices, exchange(): return lax.all_to_all(parts, axis, 0, 0, tiled=True)  7.43 us
    unnamed x24, local copies, waits for them, and re-layouts  5.13 us
    all_to_all x1, waiting for transfers between devices, exchange(): return lax.all_to_all(parts, axis, 0, 0, tiled=True)  4.84 us
  transfers between devices with their start and end apart: 15, of which 5 were waited for; matrix products, arithmetic and copies ran while one was open for 6% of the time, Pallas kernels for 25%

profile of v2, /device:TPU:1, one launch (start us, length us, event | category | flops | bytes accessed | tf_op | source)
XLA Modules:
  0.0 162.4 jit_solution(810788038654012434)
XLA Ops:
  7.2 2.5 %collective-permute-start = (bf16[64,1024]{1,0:T(8,128)(2,1)}, bf16[64,1024]{1,0:T(8,128)(2,1)}, u32[]{:S(2)}, u32[]{:S(2)}) collective-permute-start(bf16[64,1024]{1,0:T(8,128)(2,1)} %param.6), channel_id=1, source_target_pairs={{0,1},{1,2},{2,3},{3,4},{4,5},{5,6},{6,7},{7,0},{8,9},{9,10},{10,1... | collective-permute-start | bytes 393224 | tf_op jit(solution)/shard_map/ppermute | solution.py:326
  9.8 4.0 %collective-permute-start.2 = (bf16[64,1024]{1,0:T(8,128)(2,1)}, bf16[64,1024]{1,0:T(8,128)(2,1)}, u32[]{:S(2)}, u32[]{:S(2)}) collective-permute-start(bf16[64,1024]{1,0:T(8,128)(2,1)} %param.6), channel_id=1, source_target_pairs={{0,7},{1,0},{2,1},{3,2},{4,3},{5,4},{6,5},{7,6},{8,15},{9,8},{10,9... | collective-permute-start | bytes 393224 | tf_op jit(solution)/shard_map/ppermute | solution.py:329
  13.9 2.4 %fusion.10 = (bf16[2,1536,128]{2,1,0:T(8,128)(2,1)}, bf16[2,1536,128]{2,1,0:T(8,128)(2,1)S(1)}) fusion(bf16[2,4096,128]{2,1,0:T(8,128)(2,1)} %own.5), kind=kLoop, calls=%fused_computation.31 | loop fusion | bytes 3145728 | tf_op jit(solution)/shard_map/slice | solution.py:371
  16.3 3.0 %collective-permute-start.5 = (bf16[2,1536,128]{2,1,0:T(8,128)(2,1)}, bf16[2,1536,128]{2,1,0:T(8,128)(2,1)S(1)}, u32[]{:S(2)}, u32[]{:S(2)}) collective-permute-start(bf16[2,1536,128]{2,1,0:T(8,128)(2,1)} %get-tuple-element.53), channel_id=1, source_target_pairs={{8,0},{16,8},{24,16},{32,24},{40,32},{48,40},{56,48},{64,56},{72,6... | collective-permute-start | bytes 2359304 | tf_op jit(solution)/shard_map/ppermute | solution.py:371
  19.2 3.0 %collective-permute-start.4 = (bf16[2,1536,128]{2,1,0:T(8,128)(2,1)S(1)}, bf16[2,1536,128]{2,1,0:T(8,128)(2,1)S(1)}, u32[]{:S(2)}, u32[]{:S(2)}) collective-permute-start(bf16[2,1536,128]{2,1,0:T(8,128)(2,1)S(1)} %get-tuple-element.54), channel_id=1, source_target_pairs={{0,8},{8,16},{16,24},{24,32},{32,40},{40,48},{48,56},{56,64},{64,7... | collective-permute-start | bytes 2359304 | tf_op jit(solution)/shard_map/ppermute | solution.py:370
  24.4 2.7 %collective-permute-start.3 = (bf16[64,1024]{1,0:T(8,128)(2,1)}, bf16[64,1024]{1,0:T(8,128)(2,1)S(1)}, u32[]{:S(2)}, u32[]{:S(2)}) collective-permute-start(bf16[64,1024]{1,0:T(8,128)(2,1)} %collective-permute-done.2), channel_id=1, source_target_pairs={{0,7},{1,0},{2,1},{3,2},{4,3},{5,4},{6,5},{7,6},{8,15},{9,8},{10,9... | collective-permute-start | bytes 393224 | tf_op jit(solution)/shard_map/ppermute | solution.py:329
  28.9 1.7 %collective-permute-done.5.right = bf16[2,1536,128]{2,1,0:T(8,128)(2,1)S(1)} collective-permute-done((bf16[2,1536,128]{2,1,0:T(8,128)(2,1)}, bf16[2,1536,128]{2,1,0:T(8,128)(2,1)S(1)}, u32[]{:S(2)}, u32[]{:S(2)}) %collective-permute-start.5) | collective-permute-done | bytes 786464 | tf_op jit(solution)/shard_map/ppermute | solution.py:371
  32.4 3.8 %flip_keys_values.1.flipped = bf16[2,128,7168]{2,1,0:T(8,128)(2,1)} custom-call(bf16[2,1536,128]{2,1,0:T(8,128)(2,1)} %copy-done.4, bf16[2,4096,128]{2,1,0:T(8,128)(2,1)} %own.5, bf16[2,1536,128]{2,1,0:T(8,128)(2,1)} %copy-done.3), custom_call_target="tpu_custom_call" | custom-call | bytes 8000000 | tf_op jit(solution)/shard_map/flip_keys_values/pallas_call | solution.py:206
  36.3 2.7 %collective-permute-start.7 = (bf16[64,1024]{1,0:T(8,128)(2,1)S(1)}, bf16[64,1024]{1,0:T(8,128)(2,1)S(1)}, u32[]{:S(2)}, u32[]{:S(2)}) collective-permute-start(bf16[64,1024]{1,0:T(8,128)(2,1)S(1)} %collective-permute-done.3), channel_id=1, source_target_pairs={{0,7},{1,0},{2,1},{3,2},{4,3},{5,4},{6,5},{7,6},{8,15},{9,8},{10,9... | collective-permute-start | bytes 393224 | tf_op jit(solution)/shard_map/ppermute | solution.py:329
  39.1 4.9 %collective-permute-done.6 = bf16[64,1024]{1,0:T(8,128)(2,1)S(1)} collective-permute-done((bf16[64,1024]{1,0:T(8,128)(2,1)S(1)}, bf16[64,1024]{1,0:T(8,128)(2,1)S(1)}, u32[]{:S(2)}, u32[]{:S(2)}) %collective-permute-start.6) | collective-permute-done | bytes 131104 | tf_op jit(solution)/shard_map/ppermute | solution.py:326
  44.0 6.9 %collective-permute-done.8 = bf16[64,1024]{1,0:T(8,128)(2,1)S(1)} collective-permute-done((bf16[64,1024]{1,0:T(8,128)(2,1)S(1)}, bf16[64,1024]{1,0:T(8,128)(2,1)S(1)}, u32[]{:S(2)}, u32[]{:S(2)}) %collective-permute-start.8) | collective-permute-done | bytes 131104 | tf_op jit(solution)/shard_map/ppermute | solution.py:326
  50.9 1.0 copy-done.2
  51.9 13.0 %attention_forward.1 = (bf16[4,4096,256]{2,1,0:T(8,128)(2,1)}, bf16[512,128]{1,0:T(8,128)(2,1)}, f32[4,8,256]{2,1,0:T(8,128)}, bf16[512,128]{1,0:T(8,128)(2,1)}) custom-call(f32[4,32]{1,0:T(4,128)} %broadcast_select_fusion.2.bias, bf16[512,1024]{1,0:T(8,128)(2,1)} %copy-done.2, bf16[1024,128]{1,0:T(8,128)(2,1)} %weight.2, bf16[2,1536,128]{2,1,0:T(8,128)(2,1)} %copy-done.4, ...), custom_call_target="tpu_custom_call" | custom-call | flops 8589934592 | bytes 14000000 | tf_op jit(solution)/shard_map/attention_forward/pallas_call | solution.py:223
  65.0 18.6 %attention_backward.1 = (bf16[512,128]{1,0:T(8,128)(2,1)}, f32[2,4096,128]{2,1,0:T(8,128)}, bf16[2,1536,128]{2,1,0:T(8,128)(2,1)}, bf16[2,1536,128]{2,1,0:T(8,128)(2,1)}, bf16[32,64,128]{2,1,0:T(8,128)(2,1)}) custom-call(bf16[512,1024]{1,0:T(8,128)(2,1)} %copy-done.2, bf16[512,1024]{1,0:T(8,128)(2,1)} %all-gather.3.cloned.1.call-done.g, ...), custom_call_target="tpu_custom_call" | custom-call | flops 10737418240 | bytes 20000000 | tf_op jit(solution)/shard_map/attention_backward/pallas_call | solution.py:267
  83.6 21.8 %all_to_all.15 = bf16[32,64,128]{2,1,0:T(8,128)(2,1)S(1)} all-to-all(bf16[32,64,128]{2,1,0:T(8,128)(2,1)} %get-tuple-element.37), channel_id=1, replica_groups=mesh['ctx'=32,'tp'=8] {'ctx'}, dimensions={0} | all-to-all | bytes 1048576 | tf_op jit(solution)/shard_map/all_to_all | solution.py:350
  105.5 3.7 %collective-permute-start.9 = (bf16[1024,1024]{1,0:T(8,128)(2,1)}, bf16[1024,1024]{1,0:T(8,128)(2,1)}, u32[]{:S(2)}, u32[]{:S(2)}) collective-permute-start(bf16[1024,1024]{1,0:T(8,128)(2,1)} %all-gather.5.cloned.1.call-done), channel_id=1, source_target_pairs={{0,8},{8,0},{16,24},{24,16},{32,40},{40,32},{48,56},{56,48},{64,72... | collective-permute-start | bytes 6291464 | tf_op jit(solution)/shard_map/ppermute | solution.py:392
  109.2 3.0 %collective-permute-start.10 = (bf16[2,1536,128]{2,1,0:T(8,128)(2,1)}, bf16[2,1536,128]{2,1,0:T(8,128)(2,1)S(1)}, u32[]{:S(2)}, u32[]{:S(2)}) collective-permute-start(bf16[2,1536,128]{2,1,0:T(8,128)(2,1)} %get-tuple-element.41), channel_id=1, source_target_pairs={{0,8},{8,16},{16,24},{24,32},{32,40},{40,48},{48,56},{56,64},{64,7... | collective-permute-start | bytes 2359304 | tf_op jit(solution)/shard_map/ppermute | solution.py:394
  112.1 1.9 %collective-permute-start.11 = (bf16[2,1536,128]{2,1,0:T(8,128)(2,1)}, bf16[2,1536,128]{2,1,0:T(8,128)(2,1)S(1)}, u32[]{:S(2)}, u32[]{:S(2)}) collective-permute-start(bf16[2,1536,128]{2,1,0:T(8,128)(2,1)} %get-tuple-element.42), channel_id=1, source_target_pairs={{8,0},{16,8},{24,16},{32,24},{40,32},{48,40},{56,48},{64,56},{72,6... | collective-permute-start | bytes 2359304 | tf_op jit(solution)/shard_map/ppermute | solution.py:393
  115.0 15.9 %all_to_all.16 = bf16[8,64,256]{2,1,0:T(8,128)(2,1)S(1)} all-to-all(bf16[8,64,256]{2,1,0:T(8,128)(2,1)S(1)} %bitcast.26), channel_id=1, replica_groups=mesh['ctx'=32,'tp'=8] {'tp'}, dimensions={0} | all-to-all | bytes 524288 | tf_op jit(solution)/shard_map/all_to_all | solution.py:350
  131.8 7.4 %all-to-all-start.2 = ((bf16[32,64,128]{2,1,0:T(8,128)(2,1)}), bf16[32,64,128]{2,1,0:T(8,128)(2,1)S(1)}, u32[]{:S(2)}, u32[]{:S(2)}) async-start(bf16[32,64,128]{2,1,0:T(8,128)(2,1)} %broadcast_in_dim.27), calls=%async_computation.2 | async-start | bytes 1048576 | tf_op jit(solution)/shard_map/all_to_all | solution.py:350
  141.1 4.4 %combine_grads.1 = bf16[2,4096,128]{2,1,0:T(8,128)(2,1)} custom-call(f32[2,4096,128]{2,1,0:T(8,128)} %get-tuple-element.40.own, bf16[2,1536,128]{2,1,0:T(8,128)(2,1)} %copy-done.5, bf16[2,1536,128]{2,1,0:T(8,128)(2,1)} %copy-done.6), custom_call_target="tpu_custom_call" | custom-call | flops 1000000 | bytes 8000000 | tf_op jit(solution)/shard_map/combine_grads/pallas_call | solution.py:304
  146.0 4.8 %all-to-all-done.2 = bf16[32,64,128]{2,1,0:T(8,128)(2,1)S(1)} async-done(((bf16[32,64,128]{2,1,0:T(8,128)(2,1)}), bf16[32,64,128]{2,1,0:T(8,128)(2,1)S(1)}, u32[]{:S(2)}, u32[]{:S(2)}) %all-to-all-start.2) | async-done | bytes 524320 | tf_op jit(solution)/shard_map/all_to_all | solution.py:350
  151.8 1.0 copy.19
  152.8 2.8 %broadcast_select_fusion = (bf16[64,1024]{1,0:T(8,128)(2,1)}, bf16[64,1024]{1,0:T(8,128)(2,1)}) fusion(bf16[64,1024]{1,0:T(8,128)(2,1)S(1)} %fusion, pred[]{:T(512)S(6)} %eq.18, bf16[8,128,1024]{2,1,0:T(8,128)(2,1)} %bitcast.5, bf16[8,64,256]{2,1,0:T(8,128)(2,1)S(1)} %all_to_all.16), kind=kOutput, calls=%fused_computation.12 | convolution fusion | flops 134479872 | bytes 2753536 | tf_op jit(solution)/shard_map/trk,tkn->rn/dot_general | solution.py:402
  (62 shorter events, 11.1 us)
Async XLA Ops:
  7.2 15.2 %copy-start = (s32[128,32]{0,1:T(8,128)S(1)}, s32[128,32]{0,1:T(8,128)}, u32[]{:S(2)}) copy-start(s32[128,32]{0,1:T(8,128)} %param.10) | copy-start | bytes 49156
  7.2 15.4 %copy-start.7 = (bf16[1024,128]{1,0:T(8,128)(2,1)S(1)}, bf16[1024,128]{1,0:T(8,128)(2,1)}, u32[]{:S(2)}) copy-start(bf16[1024,128]{1,0:T(8,128)(2,1)} %weight.2) | copy-start | bytes 786436
  7.2 15.6 %copy-start.8 = (bf16[128,1024]{1,0:T(8,128)(2,1)S(1)}, bf16[128,1024]{1,0:T(8,128)(2,1)}, u32[]{:S(2)}) copy-start(bf16[128,1024]{1,0:T(8,128)(2,1)} %weight.3) | copy-start | bytes 786436
  7.2 57.8 %all-gather.3.cloned.1.call-start = ((), (), s32[]{:S(2)}) async-start(), calls=%async_computation.3 | async-start | bytes 1179648 | tf_op jit(solution)/shard_map/all_gather | solution.py:373
  7.2 17.0 %collective-permute-start = (bf16[64,1024]{1,0:T(8,128)(2,1)}, bf16[64,1024]{1,0:T(8,128)(2,1)}, u32[]{:S(2)}, u32[]{:S(2)}) collective-permute-start(bf16[64,1024]{1,0:T(8,128)(2,1)} %param.6), channel_id=1, source_target_pairs={{0,1},{1,2},{2,3},{3,4},{4,5},{5,6},{6,7},{7,0},{8,9},{9,10},{10,1... | collective-permute-start | bytes 393224 | tf_op jit(solution)/shard_map/ppermute | solution.py:326
  9.8 14.6 %collective-permute-start.2 = (bf16[64,1024]{1,0:T(8,128)(2,1)}, bf16[64,1024]{1,0:T(8,128)(2,1)}, u32[]{:S(2)}, u32[]{:S(2)}) collective-permute-start(bf16[64,1024]{1,0:T(8,128)(2,1)} %param.6), channel_id=1, source_target_pairs={{0,7},{1,0},{2,1},{3,2},{4,3},{5,4},{6,5},{7,6},{8,15},{9,8},{10,9... | collective-permute-start | bytes 393224 | tf_op jit(solution)/shard_map/ppermute | solution.py:329
  13.8 91.6 %all-gather.5.cloned.1.call-start = ((), (), s32[]{:S(2)}) async-start(), calls=%async_computation.4 | async-start | bytes 2359296 | tf_op jit(solution)/shard_map/all_gather | solution.py:386
  16.3 8.0 %copy-start.9 = (bf16[64,1024]{1,0:T(8,128)(2,1)S(1)}, bf16[64,1024]{1,0:T(8,128)(2,1)}, u32[]{:S(2)}) copy-start(bf16[64,1024]{1,0:T(8,128)(2,1)} %param.6) | copy-start | bytes 393220
  16.3 14.4 %collective-permute-start.5 = (bf16[2,1536,128]{2,1,0:T(8,128)(2,1)}, bf16[2,1536,128]{2,1,0:T(8,128)(2,1)S(1)}, u32[]{:S(2)}, u32[]{:S(2)}) collective-permute-start(bf16[2,1536,128]{2,1,0:T(8,128)(2,1)} %get-tuple-element.53), channel_id=1, source_target_pairs={{8,0},{16,8},{24,16},{32,24},{40,32},{48,40},{56,48},{64,56},{72,6... | collective-permute-start | bytes 2359304 | tf_op jit(solution)/shard_map/ppermute | solution.py:371
  19.2 11.9 %collective-permute-start.4 = (bf16[2,1536,128]{2,1,0:T(8,128)(2,1)S(1)}, bf16[2,1536,128]{2,1,0:T(8,128)(2,1)S(1)}, u32[]{:S(2)}, u32[]{:S(2)}) collective-permute-start(bf16[2,1536,128]{2,1,0:T(8,128)(2,1)S(1)} %get-tuple-element.54), channel_id=1, source_target_pairs={{0,8},{8,16},{16,24},{24,32},{32,40},{40,48},{48,56},{56,64},{64,7... | collective-permute-start | bytes 2359304 | tf_op jit(solution)/shard_map/ppermute | solution.py:370
  24.3 11.9 %collective-permute-start.1 = (bf16[64,1024]{1,0:T(8,128)(2,1)}, bf16[64,1024]{1,0:T(8,128)(2,1)S(1)}, u32[]{:S(2)}, u32[]{:S(2)}) collective-permute-start(bf16[64,1024]{1,0:T(8,128)(2,1)} %collective-permute-done), channel_id=1, source_target_pairs={{0,1},{1,2},{2,3},{3,4},{4,5},{5,6},{6,7},{7,0},{8,9},{9,10},{10,1... | collective-permute-start | bytes 393224 | tf_op jit(solution)/shard_map/ppermute | solution.py:326
  24.4 11.8 %collective-permute-start.3 = (bf16[64,1024]{1,0:T(8,128)(2,1)}, bf16[64,1024]{1,0:T(8,128)(2,1)S(1)}, u32[]{:S(2)}, u32[]{:S(2)}) collective-permute-start(bf16[64,1024]{1,0:T(8,128)(2,1)} %collective-permute-done.2), channel_id=1, source_target_pairs={{0,7},{1,0},{2,1},{3,2},{4,3},{5,4},{6,5},{7,6},{8,15},{9,8},{10,9... | collective-permute-start | bytes 393224 | tf_op jit(solution)/shard_map/ppermute | solution.py:329
  36.2 7.8 %collective-permute-start.6 = (bf16[64,1024]{1,0:T(8,128)(2,1)S(1)}, bf16[64,1024]{1,0:T(8,128)(2,1)S(1)}, u32[]{:S(2)}, u32[]{:S(2)}) collective-permute-start(bf16[64,1024]{1,0:T(8,128)(2,1)S(1)} %collective-permute-done.1), channel_id=1, source_target_pairs={{0,1},{1,2},{2,3},{3,4},{4,5},{5,6},{6,7},{7,0},{8,9},{9,10},{10,1... | collective-permute-start | bytes 393224 | tf_op jit(solution)/shard_map/ppermute | solution.py:326
  36.3 7.7 %collective-permute-start.7 = (bf16[64,1024]{1,0:T(8,128)(2,1)S(1)}, bf16[64,1024]{1,0:T(8,128)(2,1)S(1)}, u32[]{:S(2)}, u32[]{:S(2)}) collective-permute-start(bf16[64,1024]{1,0:T(8,128)(2,1)S(1)} %collective-permute-done.3), channel_id=1, source_target_pairs={{0,7},{1,0},{2,1},{3,2},{4,3},{5,4},{6,5},{7,6},{8,15},{9,8},{10,9... | collective-permute-start | bytes 393224 | tf_op jit(solution)/shard_map/ppermute | solution.py:329
  44.0 6.9 %collective-permute-start.8 = (bf16[64,1024]{1,0:T(8,128)(2,1)S(1)}, bf16[64,1024]{1,0:T(8,128)(2,1)S(1)}, u32[]{:S(2)}, u32[]{:S(2)}) collective-permute-start(bf16[64,1024]{1,0:T(8,128)(2,1)S(1)} %collective-permute-done.6), channel_id=1, source_target_pairs={{0,1},{1,2},{2,3},{3,4},{4,5},{5,6},{6,7},{7,0},{8,9},{9,10},{10,1... | collective-permute-start | bytes 393224 | tf_op jit(solution)/shard_map/ppermute | solution.py:326
  50.9 1.0 copy-start.2
  65.0 49.1 %copy-start.10 = (bf16[512,128]{1,0:T(8,128)(2,1)S(1)}, bf16[512,128]{1,0:T(8,128)(2,1)}, u32[]{:S(2)}) copy-start(bf16[512,128]{1,0:T(8,128)(2,1)} %get-tuple-element.30.attn) | copy-start | bytes 393220
  105.5 47.3 %collective-permute-start.9 = (bf16[1024,1024]{1,0:T(8,128)(2,1)}, bf16[1024,1024]{1,0:T(8,128)(2,1)}, u32[]{:S(2)}, u32[]{:S(2)}) collective-permute-start(bf16[1024,1024]{1,0:T(8,128)(2,1)} %all-gather.5.cloned.1.call-done), channel_id=1, source_target_pairs={{0,8},{8,0},{16,24},{24,16},{32,40},{40,32},{48,56},{56,48},{64,72... | collective-permute-start | bytes 6291464 | tf_op jit(solution)/shard_map/ppermute | solution.py:392
  109.2 30.1 %collective-permute-start.10 = (bf16[2,1536,128]{2,1,0:T(8,128)(2,1)}, bf16[2,1536,128]{2,1,0:T(8,128)(2,1)S(1)}, u32[]{:S(2)}, u32[]{:S(2)}) collective-permute-start(bf16[2,1536,128]{2,1,0:T(8,128)(2,1)} %get-tuple-element.41), channel_id=1, source_target_pairs={{0,8},{8,16},{16,24},{24,32},{32,40},{40,48},{48,56},{56,64},{64,7... | collective-permute-start | bytes 2359304 | tf_op jit(solution)/shard_map/ppermute | solution.py:394
  112.1 27.1 %collective-permute-start.11 = (bf16[2,1536,128]{2,1,0:T(8,128)(2,1)}, bf16[2,1536,128]{2,1,0:T(8,128)(2,1)S(1)}, u32[]{:S(2)}, u32[]{:S(2)}) collective-permute-start(bf16[2,1536,128]{2,1,0:T(8,128)(2,1)} %get-tuple-element.42), channel_id=1, source_target_pairs={{8,0},{16,8},{24,16},{32,24},{40,32},{48,40},{56,48},{64,56},{72,6... | collective-permute-start | bytes 2359304 | tf_op jit(solution)/shard_map/ppermute | solution.py:393
  131.8 19.0 %all-to-all-start.2 = ((bf16[32,64,128]{2,1,0:T(8,128)(2,1)}), bf16[32,64,128]{2,1,0:T(8,128)(2,1)S(1)}, u32[]{:S(2)}, u32[]{:S(2)}) async-start(bf16[32,64,128]{2,1,0:T(8,128)(2,1)} %broadcast_in_dim.27), calls=%async_computation.2 | async-start | bytes 1048576 | tf_op jit(solution)/shard_map/all_to_all | solution.py:350
  139.3 0.9 copy-start.5
  140.2 0.9 copy-start.6
  141.1 4.4 %copy-start.1 = (bf16[1024,1024]{1,0:T(8,128)(2,1)S(1)}, bf16[1024,1024]{1,0:T(8,128)(2,1)}, u32[]{:S(2)}) copy-start(bf16[1024,1024]{1,0:T(8,128)(2,1)} %all-gather.5.cloned.1.call-done) | copy-start | bytes 6291460
  (2 other events, 1.8 us)
Sparse Core Ops, SparseCore 0:
  14.0 36.5 all-gather.2
  65.1 39.6 all-gather.4

commit v3 on v0

v3 whole, which is shorter than its diff:
```python
import functools

import jax
import jax.numpy as jnp
from jax import lax
from jax.experimental import pallas as pl
from jax.experimental.pallas import tpu as pltpu
from jax.sharding import PartitionSpec as P

BLK = 128
DH = 64
CHUNK = 512
MASKED = -1e30
VMEM_LIMIT = 58 * 1024 * 1024


def contract(a, b, dims):
    return lax.dot_general(a, b, (dims, ((), ())), preferred_element_type=jnp.float32)


def row_split(block):
    lane = lax.broadcasted_iota(jnp.int32, block.shape, 1)
    zero = jnp.zeros_like(block)
    return jnp.concatenate([jnp.where(lane < DH, block, zero), jnp.where(lane >= DH, block, zero)], axis=0)


def column_split(block):
    row = lax.broadcasted_iota(jnp.int32, block.shape, 0)
    zero = jnp.zeros_like(block)
    return jnp.concatenate([jnp.where(row < DH, block, zero), jnp.where(row >= DH, block, zero)], axis=1)


def column_join(wide):
    row = lax.broadcasted_iota(jnp.int32, (wide.shape[0], BLK), 0)
    return jnp.where(row < DH, wide[:, :BLK], wide[:, BLK:])


def spread_kernel(fill, *refs):
    pieces = refs[: len(fill)]
    natural, flipped = refs[-(len(fill) + 3) : -(len(fill) + 1)]
    turned, sems = refs[-(len(fill) + 1) : -1], refs[-1]
    copies = []
    for number, (piece, first) in enumerate(zip(pieces, fill)):
        rows = piece.shape[1]
        copies.append(pltpu.make_async_copy(piece, natural.at[:, pl.ds(first, rows)], sems.at[number, 0]))
        copies[-1].start()
    for number, (piece, first) in enumerate(zip(pieces, fill)):
        rows = piece.shape[1]
        for half in range(2):
            for row in range(0, rows, CHUNK):
                turned[number][half, :, row : row + CHUNK] = piece[half, row : row + CHUNK, :].T
            copies.append(
                pltpu.make_async_copy(
                    turned[number].at[half], flipped.at[half, :, pl.ds(first, rows)], sems.at[number, 1 + half]
                )
            )
            copies[-1].start()
    for copy in copies:
        copy.wait()


def pair_kernel(step_rows, window, scale, turn, moved, place, bias, lo_even, lo_odd, hi_even, hi_odd,
                q_weight, o_weight, natural, flipped, *rest):
    pieces, rest = rest[: len(moved)], rest[len(moved) :]
    (grads, mixed, rows_out, weights, keys, values, keys_t, values_t, probs, parts, grad_out, mixed_out, x_rows, g_rows,
     through, sems_in, sems_out, sems_row, sems_piece) = rest if turn == 0 else rest[4:]
    chunks, per = window // CHUNK, CHUNK // BLK
    pair = place[turn, 0]
    even = place[turn, 1] == 0
    start = pl.multiple_of(pair * step_rows, step_rows)
    span = pl.ds(start, window)
    copies = [
        pltpu.make_async_copy(natural.at[0, span], keys, sems_in.at[0]),
        pltpu.make_async_copy(flipped.at[1, :, span], values_t, sems_in.at[1]),
        pltpu.make_async_copy(natural.at[1, span], values, sems_in.at[2]),
        pltpu.make_async_copy(flipped.at[0, :, span], keys_t, sems_in.at[3]),
    ]
    for copy in copies:
        copy.start()
    half_rows = BLK // 2

    def fetch(lo, hi):
        return [
            pltpu.make_async_copy(
                source.at[pl.ds(part * half_rows, half_rows)], dest.at[pl.ds(side * half_rows, half_rows)],
                sems_row.at[2 + 2 * part + side],
            )
            for part, dest in enumerate((x_rows, g_rows))
            for side, source in enumerate((lo, hi))
        ]

    @pl.when(even)
    def _():
        for copy in fetch(lo_even, hi_even):
            copy.start()

    @pl.when(jnp.logical_not(even))
    def _():
        for copy in fetch(lo_odd, hi_odd):
            copy.start()

    arriving = [
        pltpu.make_async_copy(piece.at[pl.ds(first, BLK)], through.at[number], sems_piece.at[0, number])
        for number, (piece, (_, first)) in enumerate(zip(pieces, moved))
    ]
    for copy in arriving:
        copy.start()
    kept = []
    for copy in fetch(lo_even, hi_even):
        copy.wait()
    out_rows = pl.ds(pl.multiple_of(pair * BLK, BLK), BLK)
    for part, source in enumerate((x_rows, g_rows)):
        copy = pltpu.make_async_copy(source, rows_out.at[part, out_rows], sems_row.at[part])
        copy.start()
        kept.append(copy)

    q = (contract(x_rows[...], q_weight[...], ((1,), (0,))) * scale).astype(jnp.bfloat16)
    grad = contract(g_rows[...], o_weight[...], ((1,), (1,))).astype(jnp.bfloat16).astype(jnp.float32)
    q_t = column_split(q.T)
    query_rows = row_split(q)
    grad_t = grad.T
    wide, tall = column_split(grad_t), row_split(grad)

    at = lambda c: slice(c * CHUNK, (c + 1) * CHUNK)
    scores = lambda c: contract(keys[at(c), :], q_t, ((1,), (0,)))
    fold = lambda t, op: op(op(t.reshape(CHUNK // 8, 8, 2 * BLK), axis=0), axis=0, keepdims=True)

    def weigh(c, half):
        parts[c] = contract(values_t[:, at(c)], half, ((1,), (0,)))

    copies[0].wait()
    tops, sums = [], []
    ahead, held = scores(0), None
    copies[1].wait()
    for c in range(chunks):
        s = ahead
        if c + 1 < chunks:
            ahead = scores(c + 1)
        s = jnp.concatenate([s[j * BLK : (j + 1) * BLK] + bias[pair, c * per + j] for j in range(per)], axis=0)
        top = fold(s, jnp.max)
        e = jnp.exp(s - top)
        tops.append(top)
        sums.append(fold(e, jnp.sum))
        half = e.astype(jnp.bfloat16)
        probs[at(c), :] = half
        if held is not None:
            weigh(c - 1, held)
        held = half
    weigh(chunks - 1, held)
    tops = jnp.concatenate(tops, axis=0)
    sums = jnp.concatenate(sums, axis=0)
    f = jnp.exp(tops - jnp.max(tops, axis=0, keepdims=True))
    f = f * (1.0 / jnp.sum(f * sums, axis=0, keepdims=True))
    out = parts[0] * f[:1]
    for c in range(1, chunks):
        out = out + parts[c] * f[c : c + 1]
    attn = column_join(out).T.astype(jnp.bfloat16)
    mixed_out[:, :BLK] = attn

    product = grad_t * attn.astype(jnp.float32).T
    delta = jnp.concatenate(
        [jnp.sum(product[:DH], axis=0, keepdims=True), jnp.sum(product[DH:], axis=0, keepdims=True)], axis=1
    )
    f_t = f.T
    homes = weights.shape[0]
    for number, (by, _) in enumerate(moved):
        arriving[number].wait()
        home = lax.rem(place[turn, 2] + (by + homes), homes)
        copy = pltpu.make_async_copy(through.at[number], weights.at[home], sems_piece.at[1, number])
        copy.start()
        kept.append(copy)
    copies[2].wait()
    copies[3].wait()
    lift = lambda c: contract(values[at(c), :], (wide * f[c : c + 1]).astype(jnp.bfloat16), ((1,), (0,)))
    total = jnp.zeros((BLK, 2 * BLK), jnp.float32)
    ahead = lift(0)
    sent = []
    for c in range(chunks):
        dp = ahead
        if c + 1 < chunks:
            ahead = lift(c + 1)
        e = probs[at(c), :]
        ds = (e.astype(jnp.float32) * (dp - delta * f[c : c + 1])).astype(jnp.bfloat16)
        total = total + contract(keys_t[:, at(c)], ds, ((1,), (0,)))
        grad_out[0, at(c), :] = contract(ds, query_rows, ((1,), (0,))).astype(jnp.bfloat16)
        grad_out[1, at(c), :] = contract(
            e, (tall * f_t[:, c : c + 1]).astype(jnp.bfloat16), ((1,), (0,))
        ).astype(jnp.bfloat16)
        piece = pl.ds(c * CHUNK, CHUNK)
        copy = pltpu.make_async_copy(grad_out.at[:, piece], grads.at[pair, :, piece], sems_out.at[c])
        copy.start()
        sent.append(copy)
    mixed_out[:, BLK:] = (column_join(total) * scale).T.astype(jnp.bfloat16)
    copy = pltpu.make_async_copy(mixed_out, mixed.at[out_rows], sems_row.at[6])
    copy.start()
    for copy in sent + kept + [copy]:
        copy.wait()


def terms_kernel(rows, mixed, out):
    attn = mixed[:, :BLK]
    pre = mixed[:, BLK:]
    by_query = contract(pre, rows[0], ((0,), (0,))).T.astype(jnp.bfloat16)
    by_output = contract(attn, rows[1], ((0,), (0,))).astype(jnp.bfloat16)
    count, both, _ = out.shape
    cut = both // 2
    groups = BLK // cut
    for i in range(count):
        out[i, :cut, :] = by_query[i * cut : (i + 1) * cut, :]
        row, column = (i % groups) * cut, (i // groups) * BLK
        out[i, cut:, :] = by_output[row : row + cut, column : column + BLK]


def rim_kernel(step_rows, grads, left_out, right_out, far_l, near_l, far_r, near_r, sems):
    blocks, _, window, _ = grads.shape
    rim = left_out.shape[1]
    overlap = rim - step_rows
    copies = [
        pltpu.make_async_copy(grads.at[0, :, pl.ds(0, rim)], far_l, sems.at[0]),
        pltpu.make_async_copy(grads.at[1, :, pl.ds(0, overlap)], near_l, sems.at[1]),
        pltpu.make_async_copy(grads.at[blocks - 1, :, pl.ds(window - rim, rim)], far_r, sems.at[2]),
        pltpu.make_async_copy(grads.at[blocks - 2, :, pl.ds(window - overlap, overlap)], near_r, sems.at[3]),
    ]
    for copy in copies:
        copy.start()
    for copy in copies:
        copy.wait()
    add = lambda a, b: (a.astype(jnp.float32) + b.astype(jnp.float32)).astype(jnp.bfloat16)
    left_out[:, :step_rows, :] = far_l[:, :step_rows, :]
    left_out[:, step_rows:, :] = add(far_l[:, step_rows:, :], near_l[...])
    right_out[:, :overlap, :] = add(far_r[:, :overlap, :], near_r[...])
    right_out[:, overlap:, :] = far_r[:, overlap:, :]


def combine_kernel(step_rows, grads, from_left, from_right, out, held, result, sems, sems_out):
    blocks, _, window, _ = grads.shape
    rows, rim = out.shape[1], from_left.shape[1]
    plan = []
    slot = 0
    for first in range(0, rows, CHUNK):
        sources = []
        for block in range(blocks):
            local = first + rim - block * step_rows
            if 0 <= local < window:
                sources.append((grads.at[block, :, pl.ds(local, CHUNK)], slot))
                slot += 1
        if first < rim:
            sources.append((from_left.at[:, pl.ds(first, CHUNK)], slot))
            slot += 1
        if first >= rows - rim:
            sources.append((from_right.at[:, pl.ds(first - (rows - rim), CHUNK)], slot))
            slot += 1
        copies = [pltpu.make_async_copy(source, held.at[n], sems.at[n]) for source, n in sources]
        for copy in copies:
            copy.start()
        plan.append((first, sources, copies))
    sent = []
    for number, (first, sources, copies) in enumerate(plan):
        for copy in copies:
            copy.wait()
        part = held[sources[0][1]].astype(jnp.float32)
        for _, n in sources[1:]:
            part = part + held[n].astype(jnp.float32)
        result[:, first : first + CHUNK, :] = part.astype(jnp.bfloat16)
        piece = pl.ds(first, CHUNK)
        copy = pltpu.make_async_copy(result.at[:, piece], out.at[:, piece], sems_out.at[number])
        copy.start()
        sent.append(copy)
    for copy in sent:
        copy.wait()


ANYWHERE = pl.BlockSpec(memory_space=pl.ANY)
IN_VMEM = pl.BlockSpec(memory_space=pltpu.VMEM)
IN_SMEM = pl.BlockSpec(memory_space=pltpu.SMEM)


def params():
    return pltpu.CompilerParams(vmem_limit_bytes=VMEM_LIMIT)


def cost(flops, moved, exps=0):
    return pl.CostEstimate(flops=flops, bytes_accessed=moved, transcendentals=exps)


def pack_kernel(flag, x, g, o_weight, q_weight, kv, out, tail, head, sems):
    rows = x.shape[0]
    span, rim = kv.shape[1], tail.shape[1]
    copies = [
        pltpu.make_async_copy(kv.at[:, pl.ds(span - rim, rim)], tail, sems.at[0]),
        pltpu.make_async_copy(kv.at[:, pl.ds(0, rim)], head, sems.at[1]),
    ]
    for copy in copies:
        copy.start()
    out[:rows, :] = x[...]
    out[rows : 2 * rows, :] = g[...]

    @pl.when(flag[0] == 0)
    def _():
        out[2 * rows :, :] = o_weight[...]

    @pl.when(flag[0] != 0)
    def _():
        out[2 * rows :, :] = q_weight[...].T

    for copy in copies:
        copy.wait()


def pack(flag, x, g, o_weight, q_weight, kv, rim):
    edge = jax.ShapeDtypeStruct((2, rim, BLK), kv.dtype)
    return pl.pallas_call(
        pack_kernel,
        in_specs=[IN_SMEM] + [IN_VMEM] * 4 + [ANYWHERE],
        out_specs=[IN_VMEM] * 3,
        out_shape=[jax.ShapeDtypeStruct((2 * x.shape[0] + o_weight.shape[0], x.shape[1]), x.dtype), edge, edge],
        scratch_shapes=[pltpu.SemaphoreType.DMA((2,))],
        cost_estimate=cost(0, 4_000_000),
        name="pack",
    )(flag, x, g, o_weight, q_weight, kv)


def spread_rows(pieces, fill, ext, carried, name):
    extra = () if carried is None else tuple(carried)
    return pl.pallas_call(
        functools.partial(spread_kernel, fill),
        in_specs=[IN_VMEM] * len(pieces) + [ANYWHERE] * len(extra),
        out_specs=[ANYWHERE] * 2,
        out_shape=[
            jax.ShapeDtypeStruct((2, ext, BLK), jnp.bfloat16),
            jax.ShapeDtypeStruct((2, BLK, ext), jnp.bfloat16),
        ],
        input_output_aliases={len(pieces) + i: i for i in range(len(extra))},
        scratch_shapes=[pltpu.VMEM((2, BLK, piece.shape[1]), jnp.bfloat16) for piece in pieces]
        + [pltpu.SemaphoreType.DMA((len(pieces), 3))],
        compiler_params=params(),
        cost_estimate=cost(0, 8_000_000),
        name=name,
    )(*pieces, *extra)


def attention_pair(turn, place, bias, shards, moved, q_weight, o_weight, natural, flipped, carried, blocks, homes,
                   step_rows, window):
    width = q_weight.shape[0]
    chunks = window // CHUNK
    shapes = [
        jax.ShapeDtypeStruct((blocks, 2, window, BLK), jnp.bfloat16),
        jax.ShapeDtypeStruct((blocks * BLK, 2 * BLK), jnp.bfloat16),
        jax.ShapeDtypeStruct((2, blocks * BLK, width), jnp.bfloat16),
        jax.ShapeDtypeStruct((homes, BLK, width), jnp.bfloat16),
    ]
    extra = () if carried is None else tuple(carried)
    pieces = [piece for piece, _, _ in moved]
    first_extra = 10 + len(pieces)
    bf = lambda *shape: pltpu.VMEM(shape, jnp.bfloat16)
    return pl.pallas_call(
        functools.partial(pair_kernel, step_rows, window, DH ** -0.5, turn, [m[1:] for m in moved]),
        in_specs=[IN_SMEM, IN_SMEM] + [ANYWHERE] * 4 + [IN_VMEM] * 2 + [ANYWHERE] * (2 + len(pieces) + len(extra)),
        out_specs=[ANYWHERE] * 4,
        out_shape=shapes,
        input_output_aliases={first_extra + i: i for i in range(len(extra))},
        scratch_shapes=[
            bf(window, BLK), bf(window, BLK), bf(BLK, window), bf(BLK, window),
            bf(window, 2 * BLK), pltpu.VMEM((chunks, BLK, 2 * BLK), jnp.float32),
            bf(2, window, BLK), bf(BLK, 2 * BLK), bf(BLK, width), bf(BLK, width), bf(len(pieces), BLK, width),
            pltpu.SemaphoreType.DMA((4,)), pltpu.SemaphoreType.DMA((chunks,)), pltpu.SemaphoreType.DMA((7,)),
            pltpu.SemaphoreType.DMA((2, len(pieces))),
        ],
        compiler_params=params(),
        cost_estimate=cost(4_000_000_000, 10_000_000, window * 2 * BLK),
        name="attention_pair",
    )(place, bias, *shards, q_weight, o_weight, natural, flipped, *pieces, *extra)


def weight_terms(rows, mixed, parts):
    width = rows.shape[2]
    return pl.pallas_call(
        terms_kernel,
        in_specs=[IN_VMEM] * 2,
        out_specs=IN_VMEM,
        out_shape=jax.ShapeDtypeStruct((parts, 2 * width // parts, BLK), jnp.bfloat16),
        compiler_params=params(),
        cost_estimate=cost(1_000_000_000, 4_000_000),
        name="weight_terms",
    )(rows, mixed)


def rim_grads(grads, rim, step_rows):
    bf = lambda rows: pltpu.VMEM((2, rows, BLK), jnp.bfloat16)
    edge = jax.ShapeDtypeStruct((2, rim, BLK), jnp.bfloat16)
    return pl.pallas_call(
        functools.partial(rim_kernel, step_rows),
        in_specs=[ANYWHERE],
        out_specs=[IN_VMEM] * 2,
        out_shape=[edge, edge],
        scratch_shapes=[bf(rim), bf(rim - step_rows), bf(rim), bf(rim - step_rows), pltpu.SemaphoreType.DMA((4,))],
        compiler_params=params(),
        cost_estimate=cost(1_000_000, 5_000_000),
        name="rim_grads",
    )(grads)


def combine_grads(grads, from_left, from_right, rows, step_rows):
    blocks, _, window, _ = grads.shape
    rim = from_left.shape[1]
    inside = sum(
        0 <= first + rim - block * step_rows < window for first in range(0, rows, CHUNK) for block in range(blocks)
    )
    slots = inside + 2 * (rim // CHUNK)
    return pl.pallas_call(
        functools.partial(combine_kernel, step_rows),
        in_specs=[ANYWHERE] * 3,
        out_specs=ANYWHERE,
        out_shape=jax.ShapeDtypeStruct((2, rows, BLK), jnp.bfloat16),
        scratch_shapes=[
            pltpu.VMEM((slots, 2, CHUNK, BLK), jnp.bfloat16),
            pltpu.VMEM((2, rows, BLK), jnp.bfloat16),
            pltpu.SemaphoreType.DMA((slots,)),
            pltpu.SemaphoreType.DMA((rows // CHUNK,)),
        ],
        compiler_params=params(),
        cost_estimate=cost(5_000_000, 10_000_000),
        name="combine_grads",
    )(grads, from_left, from_right)


def unpack_kernel(summed, q_out, o_out):
    count, both, _ = summed.shape
    cut = both // 2
    groups = BLK // cut
    for i in range(count):
        q_out[i * cut : (i + 1) * cut, :] = summed[i, :cut, :].astype(jnp.float32)
        row, column = (i % groups) * cut, (i // groups) * BLK
        o_out[row : row + cut, column : column + BLK] = summed[i, cut:, :].astype(jnp.float32)


def unpack_terms(summed, q_shape, o_shape):
    return pl.pallas_call(
        unpack_kernel,
        out_shape=[jax.ShapeDtypeStruct(q_shape, jnp.float32), jax.ShapeDtypeStruct(o_shape, jnp.float32)],
        cost_estimate=cost(0, 1_500_000),
        name="unpack_terms",
    )(summed)


def shifted(count, by):
    return [(i, (i + by) % count) for i in range(count)]


def band_bias(band_lists, base_block, query_blocks, half_step, reach_blocks):
    local = jnp.arange(query_blocks, dtype=jnp.int32)
    window_first = base_block + (2 * local + 1) * half_step - reach_blocks
    wanted = window_first[:, None] + jnp.arange(2 * reach_blocks, dtype=jnp.int32)[None, :]
    allowed = jnp.any(band_lists[:, :, None] == wanted[:, None, :], axis=1)
    return jnp.where(allowed, 0.0, MASKED).astype(jnp.float32)


def added(arrived):
    return jnp.sum(arrived.astype(jnp.float32), axis=0, keepdims=True).astype(jnp.bfloat16)


def exchange(parts, axis):
    return lax.all_to_all(parts, axis, 0, 0, tiled=True)


def on_device(slow_x, q_weight, o_weight, fast_kv, mask_lists, cotangent):
    own_rows, width = slow_x.shape
    tp = lax.axis_size("tp")
    ctx = lax.axis_size("ctx")
    total_rows = own_rows * tp
    query_blocks = total_rows // BLK
    fast_rows = fast_kv.shape[1]
    fast_blocks = fast_rows // BLK
    half_step = fast_blocks // (2 * query_blocks)
    reach_blocks = mask_lists.shape[1] // 2
    rim = (reach_blocks - half_step) * BLK
    window = 2 * reach_blocks * BLK
    step_rows = 2 * half_step * BLK

    ctx_index = lax.axis_index("ctx")
    flag = (ctx_index % 2).reshape(1).astype(jnp.int32)
    own, tail, head = pack(flag, slow_x, cotangent, o_weight, q_weight, fast_kv, rim)
    up = [(i, i + 1) for i in range(ctx - 1)]
    down = [(i + 1, i) for i in range(ctx - 1)]
    left = lax.ppermute(tail, "ctx", up)
    right = lax.ppermute(head, "ctx", down)

    even = ctx_index % 2 == 0
    band_lists = lax.dynamic_slice_in_dim(mask_lists, ctx_index * query_blocks, query_blocks, 0)
    bias = band_bias(band_lists, ctx_index * fast_blocks, query_blocks, half_step, reach_blocks)
    ext = 2 * rim + fast_rows
    spread_own = spread_rows([fast_kv], [rim], ext, None, "spread_own")
    natural, flipped = spread_rows([left, right], [0, rim + fast_rows], ext, spread_own, "spread_rims")

    tp_index = lax.axis_index("tp")
    parity = tp_index % 2
    turn = 1 - 2 * parity
    middle = tp_index // 2
    moves = jnp.array([0, 0, 0, 2], jnp.int32) + jnp.array([0, -1, 1, 0], jnp.int32) * turn
    pairs = (middle + moves + query_blocks) % query_blocks
    spread = lambda value: jnp.broadcast_to(value, pairs.shape)
    place = jnp.stack([pairs, spread(parity), spread(tp_index)], axis=1).astype(jnp.int32)
    ahead, behind = shifted(tp, 1), shifted(tp, -1)
    shared = 2 * own_rows
    f, b = [own], [own]

    def pass_on(gate):
        back, front = f[-1], b[-1]
        if gate is not None:
            back, front, gate = lax.optimization_barrier((back, front, gate))
        if 2 * len(f) < tp:
            f.append(lax.ppermute(back, "tp", ahead))
            b.append(lax.ppermute(front, "tp", behind))
        else:
            f.append(lax.ppermute(back[:shared], "tp", ahead))
            b.append(lax.ppermute(front[shared:], "tp", behind))
        return gate

    picks = [
        lambda: ((own, f[1], b[1], own), [(own, 0, shared), (f[1], -1, shared), (b[1], 1, shared)]),
        lambda: ((f[2], b[1], f[1], b[2]), [(f[2], -2, shared), (b[2], 2, shared)]),
        lambda: ((b[2], f[3], b[3], f[2]), [(f[3], -3, shared), (b[3], 3, shared)]),
        lambda: ((f[4], b[3], f[3], f[4]), [(b[4], 4, 0)]),
    ]
    pass_on(None)
    pass_on(None)
    carried = None
    for number, pick in enumerate(picks):
        shards, moved = pick()
        carried = attention_pair(
            number, place, bias, shards, moved, q_weight, o_weight, natural, flipped, carried, query_blocks, tp,
            step_rows, window,
        )
        if len(f) <= tp // 2:
            carried = (carried[0], pass_on(carried[1])) + tuple(carried[2:])
    grads, rows_mixed, rows_all, mine = carried

    mixed = exchange(rows_mixed.reshape(tp, own_rows, 2 * BLK), "tp")
    terms = weight_terms(rows_all, rows_mixed, ctx)
    left_grads, right_grads = rim_grads(grads, rim, step_rows)
    terms, left_grads, right_grads, mixed = lax.optimization_barrier((terms, left_grads, right_grads, mixed))
    own_terms = added(exchange(terms, "ctx"))
    from_right = lax.ppermute(left_grads, "ctx", down)
    from_left = lax.ppermute(right_grads, "ctx", up)
    other = lax.ppermute(mine, "ctx", [(i, i ^ 1) for i in range(ctx)])
    summed = exchange(jnp.broadcast_to(own_terms, terms.shape), "ctx")
    grad_kv = combine_grads(grads, from_left, from_right, fast_rows, step_rows)

    first = jnp.where(even, mixed[:, :, :BLK], mixed[:, :, BLK:])
    second = jnp.where(even, mixed[:, :, BLK:], mixed[:, :, :BLK])
    project = lambda rows, full: jnp.einsum(
        "trk,tkn->rn", rows, full.reshape(tp, BLK, width), preferred_element_type=jnp.float32
    ).astype(jnp.bfloat16)
    first = project(first, mine)
    second = project(second, other)
    attended = jnp.where(even, first, second)
    grad_slow = jnp.where(even, second, first)

    summed, attended, grad_slow, grad_kv = lax.optimization_barrier((summed, attended, grad_slow, grad_kv))
    grad_q_weight, grad_o_weight = unpack_terms(summed, q_weight.shape, o_weight.shape)
    return (attended, grad_slow, grad_q_weight, grad_o_weight, grad_kv)


def solution(mesh):
    in_specs = (
        P(("ctx", "tp"), None),
        P(None, "tp"),
        P("tp", None),
        P(None, "ctx", "tp"),
        P(),
        P(("ctx", "tp"), None),
    )
    out_specs = (
        P(("ctx", "tp"), None),
        P(("ctx", "tp"), None),
        P(None, "tp"),
        P("tp", None),
        P(None, "ctx", "tp"),
    )
    return jax.shard_map(on_device, mesh=mesh, in_specs=in_specs, out_specs=out_specs, check_vma=False)
```

time: 332 us -> 136 us (0.41)
  waiting for transfers between devices: 172 us -> 23.6 us
  other arithmetic: 57.3 us -> 1.49 us
  Pallas kernels: 0 us -> 54.3 us
  matrix products: 44.8 us -> 3.26 us
  starting transfers between devices: 17.2 us -> 47.5 us
  local copies, waits for them, and re-layouts: 25 us -> 3.76 us
  between operations: 14.1 us -> 0.98 us
    psum x1 -> x0, waiting for transfers between devices: 69.2 us -> none  [on_device(): grad_q_weight, grad_o_weight = lax.psum((query_term, output_term), 'ctx')]
    pallas_call x0 -> x11, Pallas kernels: none -> 54.3 us  [the longest x4 31.1 us: attention_pair(): pl.pallas_call(functools.partial(pair_kernel, step_rows, window, DH ** (-...]
    all_gather x2 -> x0, waiting for transfers between devices: 46.9 us -> none  [the longest x1 37.3 us: on_device(): lax.all_gather(slow_x, 'tp', axis=0, tiled=True)]
    reduce_scatter x1 -> x0, waiting for transfers between devices: 44.5 us -> none  [on_device(): lax.psum_scatter(jnp.concatenate([forward_term, input_term], axis=1), 'tp...]
    dot_general x18 -> x2, matrix products: 44.8 us -> 3.26 us  [on_device(): jnp.einsum('trk,tkn->rn', rows, full.reshape(tp, BLK, width), preferred_e...]
    scatter-add x16 -> x0, other arithmetic: 40.5 us -> none  [the longest x7 17.4 us: on_device(): grads_ext.at[1, first_row:first_row + window_rows, columns]]
    all_to_all x0 -> x3, starting transfers between devices: none -> 17 us  [exchange(): return lax.all_to_all(parts, axis, 0, 0, tiled=True)]
    all_to_all x0 -> x3, waiting for transfers between devices: none -> 16.2 us  [exchange(): return lax.all_to_all(parts, axis, 0, 0, tiled=True)]
  transfers between devices with their start and end apart: 8 -> 16, of which waited for: 6 -> 9; matrix products, arithmetic and copies ran while one was open for 20% -> 4% of each run, Pallas kernels for 0% -> 30%
where the time goes in v3:
time: 136 us; the launch traced here: 135 us
  Pallas kernels  54.3 us (40%)
  starting transfers between devices  47.5 us (35%)
  waiting for transfers between devices  23.6 us (17%)
  local copies, waits for them, and re-layouts  3.76 us (3%)
  matrix products  3.26 us (2%)
  other arithmetic  1.49 us (1%)
    pallas_call x4, Pallas kernels, attention_pair(): pl.pallas_call(functools.partial(pair_kernel, step_rows, window, DH ** (-...  31.1 us
    all_to_all x3, starting transfers between devices, exchange(): return lax.all_to_all(parts, axis, 0, 0, tiled=True)  17 us
    all_to_all x3, waiting for transfers between devices, exchange(): return lax.all_to_all(parts, axis, 0, 0, tiled=True)  16.2 us
    ppermute x3, starting transfers between devices, pass_on(): b.append(lax.ppermute(front, 'tp', behind))  14.3 us
    pallas_call x2, Pallas kernels, spread_rows(): pl.pallas_call(functools.partial(spread_kernel, fill), in_specs=[IN_VMEM]...  6.68 us
    pallas_call x1, Pallas kernels, combine_grads(): pl.pallas_call(functools.partial(combine_kernel, step_rows), in_specs=[AN...  4.81 us
    ppermute x1, starting transfers between devices, on_device(): left = lax.ppermute(tail, 'ctx', up)  3.95 us
    pallas_call x1, Pallas kernels, pack(): pl.pallas_call(pack_kernel, in_specs=[IN_SMEM] + [IN_VMEM] * 4 + [ANYWHER...  3.88 us
  transfers between devices with their start and end apart: 16, of which 9 were waited for; matrix products, arithmetic and copies ran while one was open for 4% of the time, Pallas kernels for 30%

profile of v3, /device:TPU:1, one launch (start us, length us, event | category | flops | bytes accessed | tf_op | source)
XLA Modules:
  0.0 134.9 jit_solution(10300779705954374497)
XLA Ops:
  0.7 3.9 %pack.1 = (bf16[256,1024]{1,0:T(8,128)(2,1)}, bf16[2,1536,128]{2,1,0:T(8,128)(2,1)}, bf16[2,1536,128]{2,1,0:T(8,128)(2,1)}) custom-call(s32[1]{0:T(128)} %bitcast.1.flag, bf16[64,1024]{1,0:T(8,128)(2,1)} %x.1, bf16[64,1024]{1,0:T(8,128)(2,1)} %g.1, bf16[128,1024]{1,0:T(8,128)(2,1)} %o_weight.9, bf16[1024,128]{1,0:T(8,128)(2,1)} %q_weight.9, ...), custom_call_target="tpu_custom_call" | custom-call | bytes 4000000 | tf_op jit(solution)/shard_map/pack/pallas_call | solution.py:312
  4.6 6.5 %collective-permute-start.2 = (bf16[256,1024]{1,0:T(8,128)(2,1)}, bf16[256,1024]{1,0:T(8,128)(2,1)S(1)}, u32[]{:S(2)}, u32[]{:S(2)}) collective-permute-start(bf16[256,1024]{1,0:T(8,128)(2,1)} %get-tuple-element.46.lo_even.hi_odd.rest_0_), channel_id=1, source_target_pairs={{0,7},{1,0},{2,1},{3,2},{4,3},{5,4},{6,5},{7,6},{8,15},{9,8},{10,9... | collective-permute-start | bytes 1572872 | tf_op jit(solution)/shard_map/ppermute | solution.py:513
  11.1 3.9 %collective-permute-start.4 = (bf16[2,1536,128]{2,1,0:T(8,128)(2,1)}, bf16[2,1536,128]{2,1,0:T(8,128)(2,1)S(1)}, u32[]{:S(2)}, u32[]{:S(2)}) collective-permute-start(bf16[2,1536,128]{2,1,0:T(8,128)(2,1)} %get-tuple-element.47), channel_id=1, source_target_pairs={{0,8},{8,16},{16,24},{24,32},{32,40},{40,48},{48,56},{56,64},{64,7... | collective-permute-start | bytes 2359304 | tf_op jit(solution)/shard_map/ppermute | solution.py:485
  16.9 3.6 %spread_own.1 = (bf16[2,7168,128]{2,1,0:T(8,128)(2,1)}, bf16[2,128,7168]{2,1,0:T(8,128)(2,1)}) custom-call(bf16[2,4096,128]{2,1,0:T(8,128)(2,1)} %refs_0_.1), custom_call_target="tpu_custom_call" | custom-call | bytes 8000000 | tf_op jit(solution)/shard_map/spread_own/pallas_call | solution.py:325
  22.0 3.3 %collective-permute-start.3 = (bf16[256,1024]{1,0:T(8,128)(2,1)S(1)}, bf16[256,1024]{1,0:T(8,128)(2,1)S(1)}, u32[]{:S(2)}, u32[]{:S(2)}) collective-permute-start(bf16[256,1024]{1,0:T(8,128)(2,1)S(1)} %collective-permute-done.2.hi_even.rest_2_.lo_odd), channel_id=1, source_target_pairs={{0,7},{1,0},{2,1},{3,2},{4,3},{5,4},{6,5},{7,6},{8,15},{9,8},{10,9... | collective-permute-start | bytes 1572872 | tf_op jit(solution)/shard_map/ppermute | solution.py:513
  25.9 2.9 %collective-permute-done.5.refs_1_ = bf16[2,1536,128]{2,1,0:T(8,128)(2,1)S(1)} collective-permute-done((bf16[2,1536,128]{2,1,0:T(8,128)(2,1)}, bf16[2,1536,128]{2,1,0:T(8,128)(2,1)S(1)}, u32[]{:S(2)}, u32[]{:S(2)}) %collective-permute-start.5) | collective-permute-done | bytes 786464 | tf_op jit(solution)/shard_map/ppermute | solution.py:486
  29.7 3.1 %spread_rims.1 = (bf16[2,7168,128]{2,1,0:T(8,128)(2,1)}, bf16[2,128,7168]{2,1,0:T(8,128)(2,1)}) custom-call(bf16[2,1536,128]{2,1,0:T(8,128)(2,1)} %copy-done.8, bf16[2,1536,128]{2,1,0:T(8,128)(2,1)} %copy-done.9, bf16[2,7168,128]{2,1,0:T(8,128)(2,1)} %get-tuple-element.49.refs_2_, ...), custom_call_target="tpu_custom_call", output_to_operand_aliasing={{0}: (2, {}), {1}: (3, {})} | custom-call | bytes 8000000 | tf_op jit(solution)/shard_map/spread_rims/pallas_call | solution.py:325
  32.8 7.8 %attention_pair.4 = (bf16[4,2,4096,128]{3,2,1,0:T(8,128)(2,1)}, bf16[512,256]{1,0:T(8,128)(2,1)}, bf16[2,512,1024]{2,1,0:T(8,128)(2,1)}, bf16[8,128,1024]{2,1,0:T(8,128)(2,1)}) custom-call(s32[4,3]{1,0:T(4,128)} %add_add_fusion.place, f32[4,32]{1,0:T(4,128)} %broadcast_select_fusion.2.bias, bf16[256,1024]{1,0:T(8,128)(2,1)} %get-tuple-element.46.lo_even.hi_odd.rest_0_, ...), custom_call_target="tpu_custom_call" | custom-call | flops 4000000000 | bytes 10000000 | tf_op jit(solution)/shard_map/attention_pair/pallas_call | solution.py:356
  40.8 4.5 %collective-permute-start.7 = (bf16[256,1024]{1,0:T(8,128)(2,1)S(1)}, bf16[256,1024]{1,0:T(8,128)(2,1)S(1)}, u32[]{:S(2)}, u32[]{:S(2)}) collective-permute-start(bf16[256,1024]{1,0:T(8,128)(2,1)S(1)} %collective-permute-done.3.hi_odd.rest_1_.lo_even), channel_id=1, source_target_pairs={{0,7},{1,0},{2,1},{3,2},{4,3},{5,4},{6,5},{7,6},{8,15},{9,8},{10,9... | collective-permute-start | bytes 1572872 | tf_op jit(solution)/shard_map/ppermute | solution.py:513
  45.3 7.8 %attention_pair.5 = (bf16[4,2,4096,128]{3,2,1,0:T(8,128)(2,1)}, bf16[512,256]{1,0:T(8,128)(2,1)}, bf16[2,512,1024]{2,1,0:T(8,128)(2,1)}, bf16[8,128,1024]{2,1,0:T(8,128)(2,1)}) custom-call(s32[4,3]{1,0:T(4,128)} %add_add_fusion.place, ...), custom_call_target="tpu_custom_call", output_to_operand_aliasing={{0}: (12, {}), {1}: (13, {}), {2}: (14, {}), {3}: (15, {})} | custom-call | flops 4000000000 | bytes 10000000 | tf_op jit(solution)/shard_map/attention_pair/pallas_call | solution.py:356
  53.1 3.4 %collective-permute-done.6.lo_odd.rest_0_.hi_even = bf16[256,1024]{1,0:T(8,128)(2,1)S(1)} collective-permute-done((bf16[256,1024]{1,0:T(8,128)(2,1)S(1)}, bf16[256,1024]{1,0:T(8,128)(2,1)S(1)}, u32[]{:S(2)}, u32[]{:S(2)}) %collective-permute-start.6) | collective-permute-done | bytes 524320 | tf_op jit(solution)/shard_map/ppermute | solution.py:512
  56.7 3.2 %collective-permute-start.9 = (bf16[128,1024]{1,0:T(8,128)(2,1)S(1)}, bf16[128,1024]{1,0:T(8,128)(2,1)S(1)}, u32[]{:S(2)}, u32[]{:S(2)}) collective-permute-start(bf16[128,1024]{1,0:T(8,128)(2,1)S(1)} %slice.15), channel_id=1, source_target_pairs={{0,7},{1,0},{2,1},{3,2},{4,3},{5,4},{6,5},{7,6},{8,15},{9,8},{10,9... | collective-permute-start | bytes 786440 | tf_op jit(solution)/shard_map/ppermute | solution.py:516
  59.9 7.8 %attention_pair.6 = (bf16[4,2,4096,128]{3,2,1,0:T(8,128)(2,1)}, bf16[512,256]{1,0:T(8,128)(2,1)}, bf16[2,512,1024]{2,1,0:T(8,128)(2,1)}, bf16[8,128,1024]{2,1,0:T(8,128)(2,1)}) custom-call(s32[4,3]{1,0:T(4,128)} %add_add_fusion.place, ...), custom_call_target="tpu_custom_call", output_to_operand_aliasing={{0}: (12, {}), {1}: (13, {}), {2}: (14, {}), {3}: (15, {})} | custom-call | flops 4000000000 | bytes 10000000 | tf_op jit(solution)/shard_map/attention_pair/pallas_call | solution.py:356
  69.0 7.8 %attention_pair.7 = (bf16[4,2,4096,128]{3,2,1,0:T(8,128)(2,1)}, bf16[512,256]{1,0:T(8,128)(2,1)}, bf16[2,512,1024]{2,1,0:T(8,128)(2,1)}, bf16[8,128,1024]{2,1,0:T(8,128)(2,1)}) custom-call(s32[4,3]{1,0:T(4,128)} %add_add_fusion.place, ...), custom_call_target="tpu_custom_call", output_to_operand_aliasing={{0}: (11, {}), {1}: (12, {}), {2}: (13, {}), {3}: (14, {})} | custom-call | flops 4000000000 | bytes 10000000 | tf_op jit(solution)/shard_map/attention_pair/pallas_call | solution.py:356
  78.4 5.3 %all-to-all-start = ((bf16[8,64,256]{2,1,0:T(8,128)(2,1)}), bf16[8,64,256]{2,1,0:T(8,128)(2,1)S(1)}, u32[]{:S(2)}, u32[]{:S(2)}) async-start(bf16[8,64,256]{2,1,0:T(8,128)(2,1)} %bitcast.16), calls=%async_computation | async-start | bytes 524288 | tf_op jit(solution)/shard_map/all_to_all | solution.py:463
  83.6 2.8 %rim_grads.1 = (bf16[2,1536,128]{2,1,0:T(8,128)(2,1)}, bf16[2,1536,128]{2,1,0:T(8,128)(2,1)}) custom-call(bf16[4,2,4096,128]{3,2,1,0:T(8,128)(2,1)} %get-tuple-element.73.grads), custom_call_target="tpu_custom_call" | custom-call | flops 1000000 | bytes 5000000 | tf_op jit(solution)/shard_map/rim_grads/pallas_call | solution.py:391
  86.4 2.9 %weight_terms.1 = bf16[32,64,128]{2,1,0:T(8,128)(2,1)} custom-call(bf16[2,512,1024]{2,1,0:T(8,128)(2,1)} %get-tuple-element.71.rows, bf16[512,256]{1,0:T(8,128)(2,1)} %get-tuple-element.72.mixed), custom_call_target="tpu_custom_call" | custom-call | flops 1000000000 | bytes 4000000 | tf_op jit(solution)/shard_map/weight_terms/pallas_call | solution.py:377
  89.3 6.7 %all-to-all-done = bf16[8,64,256]{2,1,0:T(8,128)(2,1)S(1)} async-done(((bf16[8,64,256]{2,1,0:T(8,128)(2,1)}), bf16[8,64,256]{2,1,0:T(8,128)(2,1)S(1)}, u32[]{:S(2)}, u32[]{:S(2)}) %all-to-all-start) | async-done | bytes 262176 | tf_op jit(solution)/shard_map/all_to_all | solution.py:463
  96.0 7.8 %all-to-all-start.1 = ((bf16[32,64,128]{2,1,0:T(8,128)(2,1)}), bf16[32,64,128]{2,1,0:T(8,128)(2,1)S(1)}, u32[]{:S(2)}, u32[]{:S(2)}) async-start(bf16[32,64,128]{2,1,0:T(8,128)(2,1)} %weight_terms.1), calls=%async_computation.1 | async-start | bytes 1048576 | tf_op jit(solution)/shard_map/all_to_all | solution.py:463
  103.8 3.5 %collective-permute-start.11 = (bf16[2,1536,128]{2,1,0:T(8,128)(2,1)}, bf16[2,1536,128]{2,1,0:T(8,128)(2,1)}, u32[]{:S(2)}, u32[]{:S(2)}) collective-permute-start(bf16[2,1536,128]{2,1,0:T(8,128)(2,1)} %get-tuple-element.79), channel_id=1, source_target_pairs={{0,8},{8,16},{16,24},{24,32},{32,40},{40,48},{48,56},{56,64},{64,7... | collective-permute-start | bytes 2359304 | tf_op jit(solution)/shard_map/ppermute | solution.py:544
  109.2 6.1 %all-to-all-done.1 = bf16[32,64,128]{2,1,0:T(8,128)(2,1)S(1)} async-done(((bf16[32,64,128]{2,1,0:T(8,128)(2,1)}), bf16[32,64,128]{2,1,0:T(8,128)(2,1)S(1)}, u32[]{:S(2)}, u32[]{:S(2)}) %all-to-all-start.1) | async-done | bytes 524320 | tf_op jit(solution)/shard_map/all_to_all | solution.py:463
  116.3 4.0 %all-to-all-start.2 = ((bf16[32,64,128]{2,1,0:T(8,128)(2,1)}), bf16[32,64,128]{2,1,0:T(8,128)(2,1)S(1)}, u32[]{:S(2)}, u32[]{:S(2)}) async-start(bf16[32,64,128]{2,1,0:T(8,128)(2,1)} %broadcast_in_dim.20), calls=%async_computation.2 | async-start | bytes 1048576 | tf_op jit(solution)/shard_map/all_to_all | solution.py:463
  120.9 4.8 %combine_grads.1 = bf16[2,4096,128]{2,1,0:T(8,128)(2,1)} custom-call(bf16[4,2,4096,128]{3,2,1,0:T(8,128)(2,1)} %get-tuple-element.73.grads, bf16[2,1536,128]{2,1,0:T(8,128)(2,1)} %collective-permute-done.11.from_left, bf16[2,1536,128]{2,1,0:T(8,128)(2,1)} %collective-permute-done.12.from_right), custom_call_target="tpu_custom_call" | custom-call | flops 5000000 | bytes 10000000 | tf_op jit(solution)/shard_map/combine_grads/pallas_call | solution.py:410
  128.5 3.4 %all-to-all-done.2.summed = bf16[32,64,128]{2,1,0:T(8,128)(2,1)S(1)} async-done(((bf16[32,64,128]{2,1,0:T(8,128)(2,1)}), bf16[32,64,128]{2,1,0:T(8,128)(2,1)S(1)}, u32[]{:S(2)}, u32[]{:S(2)}) %all-to-all-start.2) | async-done | bytes 524320 | tf_op jit(solution)/shard_map/all_to_all | solution.py:463
  (66 shorter events, 17.2 us)
Async XLA Ops:
  0.6 20.0 %copy-start = (s32[128,32]{0,1:T(8,128)S(1)}, s32[128,32]{0,1:T(8,128)}, u32[]{:S(2)}) copy-start(s32[128,32]{0,1:T(8,128)} %param.12) | copy-start | bytes 49156
  0.7 20.1 %copy-start.13 = (s32[4]{0:T(128)S(1)}, s32[4]{0:T(128)}, u32[]{:S(2)}) copy-start(s32[4]{0:T(128)} %constant.78.clone) | copy-start | bytes 52
  0.7 20.1 %copy-start.14 = (s32[4]{0:T(128)S(1)}, s32[4]{0:T(128)}, u32[]{:S(2)}) copy-start(s32[4]{0:T(128)} %constant.77.clone) | copy-start | bytes 52
  4.6 17.4 %collective-permute-start.2 = (bf16[256,1024]{1,0:T(8,128)(2,1)}, bf16[256,1024]{1,0:T(8,128)(2,1)S(1)}, u32[]{:S(2)}, u32[]{:S(2)}) collective-permute-start(bf16[256,1024]{1,0:T(8,128)(2,1)} %get-tuple-element.46.lo_even.hi_odd.rest_0_), channel_id=1, source_target_pairs={{0,7},{1,0},{2,1},{3,2},{4,3},{5,4},{6,5},{7,6},{8,15},{9,8},{10,9... | collective-permute-start | bytes 1572872 | tf_op jit(solution)/shard_map/ppermute | solution.py:513
  11.1 14.2 %collective-permute-start = (bf16[256,1024]{1,0:T(8,128)(2,1)}, bf16[256,1024]{1,0:T(8,128)(2,1)S(1)}, u32[]{:S(2)}, u32[]{:S(2)}) collective-permute-start(bf16[256,1024]{1,0:T(8,128)(2,1)} %get-tuple-element.46.lo_even.hi_odd.rest_0_), channel_id=1, source_target_pairs={{0,1},{1,2},{2,3},{3,4},{4,5},{5,6},{6,7},{7,0},{8,9},{9,10},{10,1... | collective-permute-start | bytes 1572872 | tf_op jit(solution)/shard_map/ppermute | solution.py:512
  11.1 14.8 %collective-permute-start.4 = (bf16[2,1536,128]{2,1,0:T(8,128)(2,1)}, bf16[2,1536,128]{2,1,0:T(8,128)(2,1)S(1)}, u32[]{:S(2)}, u32[]{:S(2)}) collective-permute-start(bf16[2,1536,128]{2,1,0:T(8,128)(2,1)} %get-tuple-element.47), channel_id=1, source_target_pairs={{0,8},{8,16},{16,24},{24,32},{32,40},{40,48},{48,56},{56,64},{64,7... | collective-permute-start | bytes 2359304 | tf_op jit(solution)/shard_map/ppermute | solution.py:485
  15.0 13.8 %collective-permute-start.5 = (bf16[2,1536,128]{2,1,0:T(8,128)(2,1)}, bf16[2,1536,128]{2,1,0:T(8,128)(2,1)S(1)}, u32[]{:S(2)}, u32[]{:S(2)}) collective-permute-start(bf16[2,1536,128]{2,1,0:T(8,128)(2,1)} %get-tuple-element.48), channel_id=1, source_target_pairs={{8,0},{16,8},{24,16},{32,24},{40,32},{48,40},{56,48},{64,56},{72,6... | collective-permute-start | bytes 2359304 | tf_op jit(solution)/shard_map/ppermute | solution.py:486
  22.0 10.8 %copy-start.10 = (bf16[256,1024]{1,0:T(8,128)(2,1)}, bf16[256,1024]{1,0:T(8,128)(2,1)S(1)}, u32[]{:S(2)}) copy-start(bf16[256,1024]{1,0:T(8,128)(2,1)S(1)} %collective-permute-done.2.hi_even.rest_2_.lo_odd) | copy-start | bytes 1572868
  22.0 18.7 %collective-permute-start.3 = (bf16[256,1024]{1,0:T(8,128)(2,1)S(1)}, bf16[256,1024]{1,0:T(8,128)(2,1)S(1)}, u32[]{:S(2)}, u32[]{:S(2)}) collective-permute-start(bf16[256,1024]{1,0:T(8,128)(2,1)S(1)} %collective-permute-done.2.hi_even.rest_2_.lo_odd), channel_id=1, source_target_pairs={{0,7},{1,0},{2,1},{3,2},{4,3},{5,4},{6,5},{7,6},{8,15},{9,8},{10,9... | collective-permute-start | bytes 1572872 | tf_op jit(solution)/shard_map/ppermute | solution.py:513
  25.3 7.5 %copy-start.11 = (bf16[256,1024]{1,0:T(8,128)(2,1)}, bf16[256,1024]{1,0:T(8,128)(2,1)S(1)}, u32[]{:S(2)}) copy-start(bf16[256,1024]{1,0:T(8,128)(2,1)S(1)} %collective-permute-done.lo_odd.rest_1_.hi_even) | copy-start | bytes 1572868
  25.3 15.4 %collective-permute-start.1 = (bf16[256,1024]{1,0:T(8,128)(2,1)S(1)}, bf16[256,1024]{1,0:T(8,128)(2,1)S(1)}, u32[]{:S(2)}, u32[]{:S(2)}) collective-permute-start(bf16[256,1024]{1,0:T(8,128)(2,1)S(1)} %collective-permute-done.lo_odd.rest_1_.hi_even), channel_id=1, source_target_pairs={{0,1},{1,2},{2,3},{3,4},{4,5},{5,6},{6,7},{7,0},{8,9},{9,10},{10,1... | collective-permute-start | bytes 1572872 | tf_op jit(solution)/shard_map/ppermute | solution.py:512
  40.6 4.7 %copy-start.4 = (bf16[256,1024]{1,0:T(8,128)(2,1)}, bf16[256,1024]{1,0:T(8,128)(2,1)S(1)}, u32[]{:S(2)}) copy-start(bf16[256,1024]{1,0:T(8,128)(2,1)S(1)} %collective-permute-done.3.hi_odd.rest_1_.lo_even) | copy-start | bytes 1572868
  40.7 4.6 %copy-start.5 = (bf16[256,1024]{1,0:T(8,128)(2,1)}, bf16[256,1024]{1,0:T(8,128)(2,1)S(1)}, u32[]{:S(2)}) copy-start(bf16[256,1024]{1,0:T(8,128)(2,1)S(1)} %collective-permute-done.1.lo_even.rest_0_.hi_odd) | copy-start | bytes 1572868
  40.7 15.8 %collective-permute-start.6 = (bf16[256,1024]{1,0:T(8,128)(2,1)S(1)}, bf16[256,1024]{1,0:T(8,128)(2,1)S(1)}, u32[]{:S(2)}, u32[]{:S(2)}) collective-permute-start(bf16[256,1024]{1,0:T(8,128)(2,1)S(1)} %collective-permute-done.1.lo_even.rest_0_.hi_odd), channel_id=1, source_target_pairs={{0,1},{1,2},{2,3},{3,4},{4,5},{5,6},{6,7},{7,0},{8,9},{9,10},{10,1... | collective-permute-start | bytes 1572872 | tf_op jit(solution)/shard_map/ppermute | solution.py:512
  40.8 15.9 %collective-permute-start.7 = (bf16[256,1024]{1,0:T(8,128)(2,1)S(1)}, bf16[256,1024]{1,0:T(8,128)(2,1)S(1)}, u32[]{:S(2)}, u32[]{:S(2)}) collective-permute-start(bf16[256,1024]{1,0:T(8,128)(2,1)S(1)} %collective-permute-done.3.hi_odd.rest_1_.lo_even), channel_id=1, source_target_pairs={{0,7},{1,0},{2,1},{3,2},{4,3},{5,4},{6,5},{7,6},{8,15},{9,8},{10,9... | collective-permute-start | bytes 1572872 | tf_op jit(solution)/shard_map/ppermute | solution.py:513
  56.7 11.0 %collective-permute-start.9 = (bf16[128,1024]{1,0:T(8,128)(2,1)S(1)}, bf16[128,1024]{1,0:T(8,128)(2,1)S(1)}, u32[]{:S(2)}, u32[]{:S(2)}) collective-permute-start(bf16[128,1024]{1,0:T(8,128)(2,1)S(1)} %slice.15), channel_id=1, source_target_pairs={{0,7},{1,0},{2,1},{3,2},{4,3},{5,4},{6,5},{7,6},{8,15},{9,8},{10,9... | collective-permute-start | bytes 786440 | tf_op jit(solution)/shard_map/ppermute | solution.py:516
  59.9 8.4 %collective-permute-start.8 = (bf16[128,1024]{1,0:T(8,128)(2,1)S(1)}, bf16[128,1024]{1,0:T(8,128)(2,1)S(1)}, u32[]{:S(2)}, u32[]{:S(2)}) collective-permute-start(bf16[128,1024]{1,0:T(8,128)(2,1)S(1)} %slice.14), channel_id=1, source_target_pairs={{0,1},{1,2},{2,3},{3,4},{4,5},{5,6},{6,7},{7,0},{8,9},{9,10},{10,1... | collective-permute-start | bytes 786440 | tf_op jit(solution)/shard_map/ppermute | solution.py:515
  76.8 49.0 %collective-permute-start.10 = (bf16[8,128,1024]{2,1,0:T(8,128)(2,1)}, bf16[8,128,1024]{2,1,0:T(8,128)(2,1)}, u32[]{:S(2)}, u32[]{:S(2)}) collective-permute-start(bf16[8,128,1024]{2,1,0:T(8,128)(2,1)} %get-tuple-element.78), channel_id=1, source_target_pairs={{0,8},{8,0},{16,24},{24,16},{32,40},{40,32},{48,56},{56,48},{64,72... | collective-permute-start | bytes 6291464 | tf_op jit(solution)/shard_map/ppermute | solution.py:545
  78.4 17.6 %all-to-all-start = ((bf16[8,64,256]{2,1,0:T(8,128)(2,1)}), bf16[8,64,256]{2,1,0:T(8,128)(2,1)S(1)}, u32[]{:S(2)}, u32[]{:S(2)}) async-start(bf16[8,64,256]{2,1,0:T(8,128)(2,1)} %bitcast.16), calls=%async_computation | async-start | bytes 524288 | tf_op jit(solution)/shard_map/all_to_all | solution.py:463
  89.3 31.0 %copy-start.1 = (bf16[8,128,1024]{2,1,0:T(8,128)(2,1)S(1)}, bf16[8,128,1024]{2,1,0:T(8,128)(2,1)}, u32[]{:S(2)}) copy-start(bf16[8,128,1024]{2,1,0:T(8,128)(2,1)} %get-tuple-element.78) | copy-start | bytes 6291460
  96.0 19.3 %all-to-all-start.1 = ((bf16[32,64,128]{2,1,0:T(8,128)(2,1)}), bf16[32,64,128]{2,1,0:T(8,128)(2,1)S(1)}, u32[]{:S(2)}, u32[]{:S(2)}) async-start(bf16[32,64,128]{2,1,0:T(8,128)(2,1)} %weight_terms.1), calls=%async_computation.1 | async-start | bytes 1048576 | tf_op jit(solution)/shard_map/all_to_all | solution.py:463
  103.8 17.0 %collective-permute-start.11 = (bf16[2,1536,128]{2,1,0:T(8,128)(2,1)}, bf16[2,1536,128]{2,1,0:T(8,128)(2,1)}, u32[]{:S(2)}, u32[]{:S(2)}) collective-permute-start(bf16[2,1536,128]{2,1,0:T(8,128)(2,1)} %get-tuple-element.79), channel_id=1, source_target_pairs={{0,8},{8,16},{16,24},{24,32},{32,40},{40,48},{48,56},{56,64},{64,7... | collective-permute-start | bytes 2359304 | tf_op jit(solution)/shard_map/ppermute | solution.py:544
  107.3 13.6 %collective-permute-start.12 = (bf16[2,1536,128]{2,1,0:T(8,128)(2,1)}, bf16[2,1536,128]{2,1,0:T(8,128)(2,1)}, u32[]{:S(2)}, u32[]{:S(2)}) collective-permute-start(bf16[2,1536,128]{2,1,0:T(8,128)(2,1)} %get-tuple-element.80), channel_id=1, source_target_pairs={{8,0},{16,8},{24,16},{32,24},{40,32},{48,40},{56,48},{64,56},{72,6... | collective-permute-start | bytes 2359304 | tf_op jit(solution)/shard_map/ppermute | solution.py:543
  116.3 15.7 %all-to-all-start.2 = ((bf16[32,64,128]{2,1,0:T(8,128)(2,1)}), bf16[32,64,128]{2,1,0:T(8,128)(2,1)S(1)}, u32[]{:S(2)}, u32[]{:S(2)}) async-start(bf16[32,64,128]{2,1,0:T(8,128)(2,1)} %broadcast_in_dim.20), calls=%async_computation.2 | async-start | bytes 1048576 | tf_op jit(solution)/shard_map/all_to_all | solution.py:463
  (7 other events, 12.6 us)

commit v4 on v3

--- a/solution.py
+++ b/solution.py
@@ -35,48 +35,32 @@
     return jnp.where(row < DH, wide[:, :BLK], wide[:, BLK:])
 
 
-def spread_kernel(fill, *refs):
-    pieces = refs[: len(fill)]
-    natural, flipped = refs[-(len(fill) + 3) : -(len(fill) + 1)]
-    turned, sems = refs[-(len(fill) + 1) : -1], refs[-1]
-    copies = []
-    for number, (piece, first) in enumerate(zip(pieces, fill)):
-        rows = piece.shape[1]
-        copies.append(pltpu.make_async_copy(piece, natural.at[:, pl.ds(first, rows)], sems.at[number, 0]))
-        copies[-1].start()
-    for number, (piece, first) in enumerate(zip(pieces, fill)):
-        rows = piece.shape[1]
-        for half in range(2):
-            for row in range(0, rows, CHUNK):
-                turned[number][half, :, row : row + CHUNK] = piece[half, row : row + CHUNK, :].T
-            copies.append(
-                pltpu.make_async_copy(
-                    turned[number].at[half], flipped.at[half, :, pl.ds(first, rows)], sems.at[number, 1 + half]
-                )
-            )
-            copies[-1].start()
-    for copy in copies:
-        copy.wait()
-
-
 def pair_kernel(step_rows, window, scale, turn, moved, place, bias, lo_even, lo_odd, hi_even, hi_odd,
-                q_weight, o_weight, natural, flipped, *rest):
+                q_weight, o_weight, left, own, right, *rest):
     pieces, rest = rest[: len(moved)], rest[len(moved) :]
-    (grads, mixed, rows_out, weights, keys, values, keys_t, values_t, probs, parts, grad_out, mixed_out, x_rows, g_rows,
+    (grads, mixed, rows_out, weights, keys, values, probs, parts, grad_out, mixed_out, x_rows, g_rows,
      through, sems_in, sems_out, sems_row, sems_piece) = rest if turn == 0 else rest[4:]
     chunks, per = window // CHUNK, CHUNK // BLK
     pair = place[turn, 0]
     even = place[turn, 1] == 0
-    start = pl.multiple_of(pair * step_rows, step_rows)
-    span = pl.ds(start, window)
-    copies = [
-        pltpu.make_async_copy(natural.at[0, span], keys, sems_in.at[0]),
-        pltpu.make_async_copy(flipped.at[1, :, span], values_t, sems_in.at[1]),
-        pltpu.make_async_copy(natural.at[1, span], values, sems_in.at[2]),
-        pltpu.make_async_copy(flipped.at[0, :, span], keys_t, sems_in.at[3]),
-    ]
-    for copy in copies:
-        copy.start()
+    rim, span = left.shape[1], own.shape[1]
+    for block in range(bias.shape[0]):
+        start = block * step_rows
+
+        @pl.when(pair == block)
+        def _():
+            taken = 0
+            for source, first in ((left, 0), (own, rim), (right, rim + span)):
+                lo, hi = max(start, first), min(start + window, first + source.shape[1])
+                if hi > lo:
+                    for half, dest in enumerate((keys, values)):
+                        pltpu.make_async_copy(
+                            source.at[half, pl.ds(lo - first, hi - lo)], dest.at[pl.ds(taken, hi - lo)],
+                            sems_in.at[half],
+                        ).start()
+                    taken += hi - lo
+
+    copies = [pltpu.make_async_copy(own.at[half], dest, sems_in.at[half]) for half, dest in enumerate((keys, values))]
     half_rows = BLK // 2
 
     def fetch(lo, hi):
@@ -126,16 +110,16 @@
     fold = lambda t, op: op(op(t.reshape(CHUNK // 8, 8, 2 * BLK), axis=0), axis=0, keepdims=True)
 
     def weigh(c, half):
-        parts[c] = contract(values_t[:, at(c)], half, ((1,), (0,)))
+        parts[c] = contract(values[at(c), :].T, half, ((1,), (0,)))
 
     copies[0].wait()
     tops, sums = [], []
-    ahead, held = scores(0), None
+    queue, held = [scores(0), scores(1)], None
     copies[1].wait()
     for c in range(chunks):
-        s = ahead
-        if c + 1 < chunks:
-            ahead = scores(c + 1)
+        s = queue.pop(0)
+        if c + 2 < chunks:
+            queue.append(scores(c + 2))
         s = jnp.concatenate([s[j * BLK : (j + 1) * BLK] + bias[pair, c * per + j] for j in range(per)], axis=0)
         top = fold(s, jnp.max)
         e = jnp.exp(s - top)
@@ -169,19 +153,17 @@
         copy = pltpu.make_async_copy(through.at[number], weights.at[home], sems_piece.at[1, number])
         copy.start()
         kept.append(copy)
-    copies[2].wait()
-    copies[3].wait()
     lift = lambda c: contract(values[at(c), :], (wide * f[c : c + 1]).astype(jnp.bfloat16), ((1,), (0,)))
     total = jnp.zeros((BLK, 2 * BLK), jnp.float32)
-    ahead = lift(0)
+    queue = [lift(0), lift(1)]
     sent = []
     for c in range(chunks):
-        dp = ahead
-        if c + 1 < chunks:
-            ahead = lift(c + 1)
+        dp = queue.pop(0)
+        if c + 2 < chunks:
+            queue.append(lift(c + 2))
         e = probs[at(c), :]
         ds = (e.astype(jnp.float32) * (dp - delta * f[c : c + 1])).astype(jnp.bfloat16)
-        total = total + contract(keys_t[:, at(c)], ds, ((1,), (0,)))
+        total = total + contract(keys[at(c), :].T, ds, ((1,), (0,)))
         grad_out[0, at(c), :] = contract(ds, query_rows, ((1,), (0,))).astype(jnp.bfloat16)
         grad_out[1, at(c), :] = contract(
             e, (tall * f_t[:, c : c + 1]).astype(jnp.bfloat16), ((1,), (0,))
@@ -320,26 +302,7 @@
     )(flag, x, g, o_weight, q_weight, kv)
 
 
-def spread_rows(pieces, fill, ext, carried, name):
-    extra = () if carried is None else tuple(carried)
-    return pl.pallas_call(
-        functools.partial(spread_kernel, fill),
-        in_specs=[IN_VMEM] * len(pieces) + [ANYWHERE] * len(extra),
-        out_specs=[ANYWHERE] * 2,
-        out_shape=[
-            jax.ShapeDtypeStruct((2, ext, BLK), jnp.bfloat16),
-            jax.ShapeDtypeStruct((2, BLK, ext), jnp.bfloat16),
-        ],
-        input_output_aliases={len(pieces) + i: i for i in range(len(extra))},
-        scratch_shapes=[pltpu.VMEM((2, BLK, piece.shape[1]), jnp.bfloat16) for piece in pieces]
-        + [pltpu.SemaphoreType.DMA((len(pieces), 3))],
-        compiler_params=params(),
-        cost_estimate=cost(0, 8_000_000),
-        name=name,
-    )(*pieces, *extra)
-
-
-def attention_pair(turn, place, bias, shards, moved, q_weight, o_weight, natural, flipped, carried, blocks, homes,
+def attention_pair(turn, place, bias, shards, moved, q_weight, o_weight, left, own, right, carried, blocks, homes,
                    step_rows, window):
     width = q_weight.shape[0]
     chunks = window // CHUNK
@@ -351,25 +314,25 @@
     ]
     extra = () if carried is None else tuple(carried)
     pieces = [piece for piece, _, _ in moved]
-    first_extra = 10 + len(pieces)
+    first_extra = 11 + len(pieces)
     bf = lambda *shape: pltpu.VMEM(shape, jnp.bfloat16)
     return pl.pallas_call(
         functools.partial(pair_kernel, step_rows, window, DH ** -0.5, turn, [m[1:] for m in moved]),
-        in_specs=[IN_SMEM, IN_SMEM] + [ANYWHERE] * 4 + [IN_VMEM] * 2 + [ANYWHERE] * (2 + len(pieces) + len(extra)),
+        in_specs=[IN_SMEM, IN_SMEM] + [ANYWHERE] * 4 + [IN_VMEM] * 2 + [ANYWHERE] * (3 + len(pieces) + len(extra)),
         out_specs=[ANYWHERE] * 4,
         out_shape=shapes,
         input_output_aliases={first_extra + i: i for i in range(len(extra))},
         scratch_shapes=[
-            bf(window, BLK), bf(window, BLK), bf(BLK, window), bf(BLK, window),
+            bf(window, BLK), bf(window, BLK),
             bf(window, 2 * BLK), pltpu.VMEM((chunks, BLK, 2 * BLK), jnp.float32),
             bf(2, window, BLK), bf(BLK, 2 * BLK), bf(BLK, width), bf(BLK, width), bf(len(pieces), BLK, width),
-            pltpu.SemaphoreType.DMA((4,)), pltpu.SemaphoreType.DMA((chunks,)), pltpu.SemaphoreType.DMA((7,)),
+            pltpu.SemaphoreType.DMA((2,)), pltpu.SemaphoreType.DMA((chunks,)), pltpu.SemaphoreType.DMA((7,)),
             pltpu.SemaphoreType.DMA((2, len(pieces))),
         ],
         compiler_params=params(),
         cost_estimate=cost(4_000_000_000, 10_000_000, window * 2 * BLK),
         name="attention_pair",
-    )(place, bias, *shards, q_weight, o_weight, natural, flipped, *pieces, *extra)
+    )(place, bias, *shards, q_weight, o_weight, left, own, right, *pieces, *extra)
 
 
 def weight_terms(rows, mixed, parts):
@@ -424,25 +387,6 @@
     )(grads, from_left, from_right)
 
 
-def unpack_kernel(summed, q_out, o_out):
-    count, both, _ = summed.shape
-    cut = both // 2
-    groups = BLK // cut
-    for i in range(count):
-        q_out[i * cut : (i + 1) * cut, :] = summed[i, :cut, :].astype(jnp.float32)
-        row, column = (i % groups) * cut, (i // groups) * BLK
-        o_out[row : row + cut, column : column + BLK] = summed[i, cut:, :].astype(jnp.float32)
-
-
-def unpack_terms(summed, q_shape, o_shape):
-    return pl.pallas_call(
-        unpack_kernel,
-        out_shape=[jax.ShapeDtypeStruct(q_shape, jnp.float32), jax.ShapeDtypeStruct(o_shape, jnp.float32)],
-        cost_estimate=cost(0, 1_500_000),
-        name="unpack_terms",
-    )(summed)
-
-
 def shifted(count, by):
     return [(i, (i + by) % count) for i in range(count)]
 
@@ -488,10 +432,6 @@
     even = ctx_index % 2 == 0
     band_lists = lax.dynamic_slice_in_dim(mask_lists, ctx_index * query_blocks, query_blocks, 0)
     bias = band_bias(band_lists, ctx_index * fast_blocks, query_blocks, half_step, reach_blocks)
-    ext = 2 * rim + fast_rows
-    spread_own = spread_rows([fast_kv], [rim], ext, None, "spread_own")
-    natural, flipped = spread_rows([left, right], [0, rim + fast_rows], ext, spread_own, "spread_rims")
-
     tp_index = lax.axis_index("tp")
     parity = tp_index % 2
     turn = 1 - 2 * parity
@@ -528,7 +468,7 @@
     for number, pick in enumerate(picks):
         shards, moved = pick()
         carried = attention_pair(
-            number, place, bias, shards, moved, q_weight, o_weight, natural, flipped, carried, query_blocks, tp,
+            number, place, bias, shards, moved, q_weight, o_weight, left, fast_kv, right, carried, query_blocks, tp,
             step_rows, window,
         )
         if len(f) <= tp // 2:
@@ -536,9 +476,10 @@
     grads, rows_mixed, rows_all, mine = carried
 
     mixed = exchange(rows_mixed.reshape(tp, own_rows, 2 * BLK), "tp")
+    left_grads, right_grads = rim_grads(grads, rim, step_rows)
+    rows_all, left_grads, right_grads = lax.optimization_barrier((rows_all, left_grads, right_grads))
     terms = weight_terms(rows_all, rows_mixed, ctx)
-    left_grads, right_grads = rim_grads(grads, rim, step_rows)
-    terms, left_grads, right_grads, mixed = lax.optimization_barrier((terms, left_grads, right_grads, mixed))
+    terms, mixed = lax.optimization_barrier((terms, mixed))
     own_terms = added(exchange(terms, "ctx"))
     from_right = lax.ppermute(left_grads, "ctx", down)
     from_left = lax.ppermute(right_grads, "ctx", up)
@@ -557,7 +498,10 @@
     grad_slow = jnp.where(even, second, first)
 
     summed, attended, grad_slow, grad_kv = lax.optimization_barrier((summed, attended, grad_slow, grad_kv))
-    grad_q_weight, grad_o_weight = unpack_terms(summed, q_weight.shape, o_weight.shape)
+    cut = terms.shape[1] // 2
+    grad_q_weight = summed[:, :cut].astype(jnp.float32).reshape(q_weight.shape)
+    blocked = summed[:, cut:].reshape(width // BLK, BLK // cut, cut, BLK).transpose(1, 2, 0, 3)
+    grad_o_weight = blocked.astype(jnp.float32).reshape(o_weight.shape)
     return (attended, grad_slow, grad_q_weight, grad_o_weight, grad_kv)
 
 

time: 136 us -> 131 us (0.963)
  Pallas kernels: 54.3 us -> 46.5 us
    pallas_call x3 -> x0, Pallas kernels: 8.77 us -> none  [the longest x2 6.68 us: spread_rows(): pl.pallas_call(functools.partial(spread_kernel, fill), in_specs=[IN_VMEM]...]
    ppermute x3, waiting for transfers between devices: 0.29 us -> 3.81 us  [pass_on(): b.append(lax.ppermute(front, 'tp', behind))]
    ppermute x3, waiting for transfers between devices: 3.44 us -> 1.77 us  [pass_on(): f.append(lax.ppermute(back, 'tp', ahead))]
  transfers between devices with their start and end apart: 16 -> 16, of which waited for: 9 -> 8; matrix products, arithmetic and copies ran while one was open for 4% -> 5% of each run, Pallas kernels for 30% -> 26%
where the time goes in v4:
time: 131 us; the launch traced here: 130 us
  starting transfers between devices  48.2 us (37%)
  Pallas kernels  46.5 us (35%)
  waiting for transfers between devices  24.8 us (19%)
  local copies, waits for them, and re-layouts  4.25 us (3%)
  matrix products  3.26 us (2%)
  other arithmetic  2.4 us (2%)
    pallas_call x4, Pallas kernels, attention_pair(): pl.pallas_call(functools.partial(pair_kernel, step_rows, window, DH ** (-...  32.2 us
    all_to_all x3, starting transfers between devices, exchange(): return lax.all_to_all(parts, axis, 0, 0, tiled=True)  17.1 us
    all_to_all x3, waiting for transfers between devices, exchange(): return lax.all_to_all(parts, axis, 0, 0, tiled=True)  16.2 us
    ppermute x3, starting transfers between devices, pass_on(): b.append(lax.ppermute(front, 'tp', behind))  13.1 us
    pallas_call x1, Pallas kernels, combine_grads(): pl.pallas_call(functools.partial(combine_kernel, step_rows), in_specs=[AN...  4.81 us
    ppermute x1, starting transfers between devices, pass_on(): b.append(lax.ppermute(front[shared:], 'tp', behind))  4.2 us
    ppermute x1, starting transfers between devices, on_device(): left = lax.ppermute(tail, 'ctx', up)  3.95 us
    pallas_call x1, Pallas kernels, pack(): pl.pallas_call(pack_kernel, in_specs=[IN_SMEM] + [IN_VMEM] * 4 + [ANYWHER...  3.88 us
  transfers between devices with their start and end apart: 16, of which 8 were waited for; matrix products, arithmetic and copies ran while one was open for 5% of the time, Pallas kernels for 26%

profile of v4, /device:TPU:1, one launch (start us, length us, event | category | flops | bytes accessed | tf_op | source)
XLA Modules:
  0.0 130.4 jit_solution(8900253258128777583)
XLA Ops:
  0.7 3.9 %pack.1 = (bf16[256,1024]{1,0:T(8,128)(2,1)}, bf16[2,1536,128]{2,1,0:T(8,128)(2,1)}, bf16[2,1536,128]{2,1,0:T(8,128)(2,1)}) custom-call(s32[1]{0:T(128)} %bitcast.1.flag, bf16[64,1024]{1,0:T(8,128)(2,1)} %x.1, bf16[64,1024]{1,0:T(8,128)(2,1)} %g.1, bf16[128,1024]{1,0:T(8,128)(2,1)} %o_weight.9, bf16[1024,128]{1,0:T(8,128)(2,1)} %q_weight.9, ...), custom_call_target="tpu_custom_call" | custom-call | bytes 4000000 | tf_op jit(solution)/shard_map/pack/pallas_call | solution.py:294
  4.6 6.5 %collective-permute-start.2 = (bf16[256,1024]{1,0:T(8,128)(2,1)}, bf16[256,1024]{1,0:T(8,128)(2,1)S(1)}, u32[]{:S(2)}, u32[]{:S(2)}) collective-permute-start(bf16[256,1024]{1,0:T(8,128)(2,1)} %get-tuple-element.41.lo_even.hi_odd.rest_0_), channel_id=1, source_target_pairs={{0,7},{1,0},{2,1},{3,2},{4,3},{5,4},{6,5},{7,6},{8,15},{9,8},{10,9... | collective-permute-start | bytes 1572872 | tf_op jit(solution)/shard_map/ppermute | solution.py:453
  11.1 3.9 %collective-permute-start.4 = (bf16[2,1536,128]{2,1,0:T(8,128)(2,1)}, bf16[2,1536,128]{2,1,0:T(8,128)(2,1)S(1)}, u32[]{:S(2)}, u32[]{:S(2)}) collective-permute-start(bf16[2,1536,128]{2,1,0:T(8,128)(2,1)} %get-tuple-element.42), channel_id=1, source_target_pairs={{0,8},{8,16},{16,24},{24,32},{32,40},{40,48},{48,56},{56,64},{64,7... | collective-permute-start | bytes 2359304 | tf_op jit(solution)/shard_map/ppermute | solution.py:429
  18.2 3.8 %collective-permute-done.2.hi_even.rest_2_.lo_odd = bf16[256,1024]{1,0:T(8,128)(2,1)S(1)} collective-permute-done((bf16[256,1024]{1,0:T(8,128)(2,1)}, bf16[256,1024]{1,0:T(8,128)(2,1)S(1)}, u32[]{:S(2)}, u32[]{:S(2)}) %collective-permute-start.2) | collective-permute-done | bytes 524320 | tf_op jit(solution)/shard_map/ppermute | solution.py:453
  22.0 3.3 %collective-permute-start.3 = (bf16[256,1024]{1,0:T(8,128)(2,1)S(1)}, bf16[256,1024]{1,0:T(8,128)(2,1)S(1)}, u32[]{:S(2)}, u32[]{:S(2)}) collective-permute-start(bf16[256,1024]{1,0:T(8,128)(2,1)S(1)} %collective-permute-done.2.hi_even.rest_2_.lo_odd), channel_id=1, source_target_pairs={{0,7},{1,0},{2,1},{3,2},{4,3},{5,4},{6,5},{7,6},{8,15},{9,8},{10,9... | collective-permute-start | bytes 1572872 | tf_op jit(solution)/shard_map/ppermute | solution.py:453
  25.9 2.9 %collective-permute-done.5.right = bf16[2,1536,128]{2,1,0:T(8,128)(2,1)S(1)} collective-permute-done((bf16[2,1536,128]{2,1,0:T(8,128)(2,1)}, bf16[2,1536,128]{2,1,0:T(8,128)(2,1)S(1)}, u32[]{:S(2)}, u32[]{:S(2)}) %collective-permute-start.5) | collective-permute-done | bytes 786464 | tf_op jit(solution)/shard_map/ppermute | solution.py:430
  29.7 8.1 %attention_pair.4 = (bf16[4,2,4096,128]{3,2,1,0:T(8,128)(2,1)}, bf16[512,256]{1,0:T(8,128)(2,1)}, bf16[2,512,1024]{2,1,0:T(8,128)(2,1)}, bf16[8,128,1024]{2,1,0:T(8,128)(2,1)}) custom-call(s32[4,3]{1,0:T(4,128)} %add_add_fusion.place, f32[4,32]{1,0:T(4,128)} %broadcast_select_fusion.2.bias, bf16[256,1024]{1,0:T(8,128)(2,1)} %get-tuple-element.41.lo_even.hi_odd.rest_0_, ...), custom_call_target="tpu_custom_call" | custom-call | flops 4000000000 | bytes 10000000 | tf_op jit(solution)/shard_map/attention_pair/pallas_call | solution.py:319
  38.1 3.3 %collective-permute-start.7 = (bf16[256,1024]{1,0:T(8,128)(2,1)S(1)}, bf16[256,1024]{1,0:T(8,128)(2,1)S(1)}, u32[]{:S(2)}, u32[]{:S(2)}) collective-permute-start(bf16[256,1024]{1,0:T(8,128)(2,1)S(1)} %collective-permute-done.3.hi_odd.rest_1_.lo_even), channel_id=1, source_target_pairs={{0,7},{1,0},{2,1},{3,2},{4,3},{5,4},{6,5},{7,6},{8,15},{9,8},{10,9... | collective-permute-start | bytes 1572872 | tf_op jit(solution)/shard_map/ppermute | solution.py:453
  41.4 7.7 %attention_pair.5 = (bf16[4,2,4096,128]{3,2,1,0:T(8,128)(2,1)}, bf16[512,256]{1,0:T(8,128)(2,1)}, bf16[2,512,1024]{2,1,0:T(8,128)(2,1)}, bf16[8,128,1024]{2,1,0:T(8,128)(2,1)}) custom-call(s32[4,3]{1,0:T(4,128)} %add_add_fusion.place, ...), custom_call_target="tpu_custom_call", output_to_operand_aliasing={{0}: (13, {}), {1}: (14, {}), {2}: (15, {}), {3}: (16, {})} | custom-call | flops 4000000000 | bytes 10000000 | tf_op jit(solution)/shard_map/attention_pair/pallas_call | solution.py:319
  50.7 4.2 %collective-permute-start.9 = (bf16[128,1024]{1,0:T(8,128)(2,1)S(1)}, bf16[128,1024]{1,0:T(8,128)(2,1)S(1)}, u32[]{:S(2)}, u32[]{:S(2)}) collective-permute-start(bf16[128,1024]{1,0:T(8,128)(2,1)S(1)} %slice.21), channel_id=1, source_target_pairs={{0,7},{1,0},{2,1},{3,2},{4,3},{5,4},{6,5},{7,6},{8,15},{9,8},{10,9... | collective-permute-start | bytes 786440 | tf_op jit(solution)/shard_map/ppermute | solution.py:456
  54.9 8.2 %attention_pair.6 = (bf16[4,2,4096,128]{3,2,1,0:T(8,128)(2,1)}, bf16[512,256]{1,0:T(8,128)(2,1)}, bf16[2,512,1024]{2,1,0:T(8,128)(2,1)}, bf16[8,128,1024]{2,1,0:T(8,128)(2,1)}) custom-call(s32[4,3]{1,0:T(4,128)} %add_add_fusion.place, ...), custom_call_target="tpu_custom_call", output_to_operand_aliasing={{0}: (13, {}), {1}: (14, {}), {2}: (15, {}), {3}: (16, {})} | custom-call | flops 4000000000 | bytes 10000000 | tf_op jit(solution)/shard_map/attention_pair/pallas_call | solution.py:319
  63.9 8.1 %attention_pair.7 = (bf16[4,2,4096,128]{3,2,1,0:T(8,128)(2,1)}, bf16[512,256]{1,0:T(8,128)(2,1)}, bf16[2,512,1024]{2,1,0:T(8,128)(2,1)}, bf16[8,128,1024]{2,1,0:T(8,128)(2,1)}) custom-call(s32[4,3]{1,0:T(4,128)} %add_add_fusion.place, ...), custom_call_target="tpu_custom_call", output_to_operand_aliasing={{0}: (12, {}), {1}: (13, {}), {2}: (14, {}), {3}: (15, {})} | custom-call | flops 4000000000 | bytes 10000000 | tf_op jit(solution)/shard_map/attention_pair/pallas_call | solution.py:319
  72.1 2.5 %collective-permute-start.10 = (bf16[8,128,1024]{2,1,0:T(8,128)(2,1)}, bf16[8,128,1024]{2,1,0:T(8,128)(2,1)}, u32[]{:S(2)}, u32[]{:S(2)}) collective-permute-start(bf16[8,128,1024]{2,1,0:T(8,128)(2,1)} %get-tuple-element.70), channel_id=1, source_target_pairs={{0,8},{8,0},{16,24},{24,16},{32,40},{40,32},{48,56},{56,48},{64,72... | collective-permute-start | bytes 6291464 | tf_op jit(solution)/shard_map/ppermute | solution.py:486
  74.6 4.3 %all-to-all-start = ((bf16[8,64,256]{2,1,0:T(8,128)(2,1)}), bf16[8,64,256]{2,1,0:T(8,128)(2,1)S(1)}, u32[]{:S(2)}, u32[]{:S(2)}) async-start(bf16[8,64,256]{2,1,0:T(8,128)(2,1)} %bitcast.28), calls=%async_computation | async-start | bytes 524288 | tf_op jit(solution)/shard_map/all_to_all | solution.py:407
  78.9 2.8 %rim_grads.1 = (bf16[2,1536,128]{2,1,0:T(8,128)(2,1)}, bf16[2,1536,128]{2,1,0:T(8,128)(2,1)}) custom-call(bf16[4,2,4096,128]{3,2,1,0:T(8,128)(2,1)} %get-tuple-element.63.grads), custom_call_target="tpu_custom_call" | custom-call | flops 1000000 | bytes 5000000 | tf_op jit(solution)/shard_map/rim_grads/pallas_call | solution.py:354
  81.6 2.9 %weight_terms.1 = bf16[32,64,128]{2,1,0:T(8,128)(2,1)} custom-call(bf16[2,512,1024]{2,1,0:T(8,128)(2,1)} %get-tuple-element.66.rows, bf16[512,256]{1,0:T(8,128)(2,1)} %get-tuple-element.67.mixed), custom_call_target="tpu_custom_call" | custom-call | flops 1000000000 | bytes 4000000 | tf_op jit(solution)/shard_map/weight_terms/pallas_call | solution.py:340
  84.5 6.7 %all-to-all-done = bf16[8,64,256]{2,1,0:T(8,128)(2,1)S(1)} async-done(((bf16[8,64,256]{2,1,0:T(8,128)(2,1)}), bf16[8,64,256]{2,1,0:T(8,128)(2,1)S(1)}, u32[]{:S(2)}, u32[]{:S(2)}) %all-to-all-start) | async-done | bytes 262176 | tf_op jit(solution)/shard_map/all_to_all | solution.py:407
  91.2 8.8 %all-to-all-start.1 = ((bf16[32,64,128]{2,1,0:T(8,128)(2,1)}), bf16[32,64,128]{2,1,0:T(8,128)(2,1)S(1)}, u32[]{:S(2)}, u32[]{:S(2)}) async-start(bf16[32,64,128]{2,1,0:T(8,128)(2,1)} %weight_terms.1), calls=%async_computation.1 | async-start | bytes 1048576 | tf_op jit(solution)/shard_map/all_to_all | solution.py:407
  100.0 3.5 %collective-permute-start.11 = (bf16[2,1536,128]{2,1,0:T(8,128)(2,1)}, bf16[2,1536,128]{2,1,0:T(8,128)(2,1)}, u32[]{:S(2)}, u32[]{:S(2)}) collective-permute-start(bf16[2,1536,128]{2,1,0:T(8,128)(2,1)} %get-tuple-element.71), channel_id=1, source_target_pairs={{0,8},{8,16},{16,24},{24,32},{32,40},{40,48},{48,56},{56,64},{64,7... | collective-permute-start | bytes 2359304 | tf_op jit(solution)/shard_map/ppermute | solution.py:485
  105.5 6.1 %all-to-all-done.1 = bf16[32,64,128]{2,1,0:T(8,128)(2,1)S(1)} async-done(((bf16[32,64,128]{2,1,0:T(8,128)(2,1)}), bf16[32,64,128]{2,1,0:T(8,128)(2,1)S(1)}, u32[]{:S(2)}, u32[]{:S(2)}) %all-to-all-start.1) | async-done | bytes 524320 | tf_op jit(solution)/shard_map/all_to_all | solution.py:407
  112.6 4.0 %all-to-all-start.2 = ((bf16[32,64,128]{2,1,0:T(8,128)(2,1)}), bf16[32,64,128]{2,1,0:T(8,128)(2,1)S(1)}, u32[]{:S(2)}, u32[]{:S(2)}) async-start(bf16[32,64,128]{2,1,0:T(8,128)(2,1)} %broadcast_in_dim.20), calls=%async_computation.2 | async-start | bytes 1048576 | tf_op jit(solution)/shard_map/all_to_all | solution.py:407
  117.2 4.8 %combine_grads.1 = bf16[2,4096,128]{2,1,0:T(8,128)(2,1)} custom-call(bf16[4,2,4096,128]{3,2,1,0:T(8,128)(2,1)} %get-tuple-element.63.grads, bf16[2,1536,128]{2,1,0:T(8,128)(2,1)} %collective-permute-done.11.from_left, bf16[2,1536,128]{2,1,0:T(8,128)(2,1)} %collective-permute-done.12.from_right), custom_call_target="tpu_custom_call" | custom-call | flops 5000000 | bytes 10000000 | tf_op jit(solution)/shard_map/combine_grads/pallas_call | solution.py:373
  122.0 2.8 %broadcast_select_fusion = (bf16[64,1024]{1,0:T(8,128)(2,1)}, bf16[64,1024]{1,0:T(8,128)(2,1)}) fusion(bf16[64,1024]{1,0:T(8,128)(2,1)S(1)} %fusion, pred[]{:T(512)S(6)} %eq.25, bf16[8,128,1024]{2,1,0:T(8,128)(2,1)} %collective-permute-done.10, bf16[8,64,256]{2,1,0:T(8,128)(2,1)S(1)} %all-to-all-done), kind=kOutput, calls=%fused_computation.11 | convolution fusion | flops 134479872 | bytes 2753536 | tf_op jit(solution)/shard_map/trk,tkn->rn/dot_general | solution.py:492
  124.8 3.4 %all-to-all-done.2 = bf16[32,64,128]{2,1,0:T(8,128)(2,1)S(1)} async-done(((bf16[32,64,128]{2,1,0:T(8,128)(2,1)}), bf16[32,64,128]{2,1,0:T(8,128)(2,1)S(1)}, u32[]{:S(2)}, u32[]{:S(2)}) %all-to-all-start.2) | async-done | bytes 524320 | tf_op jit(solution)/shard_map/all_to_all | solution.py:407
  (66 shorter events, 12.9 us)
Async XLA Ops:
  0.6 16.4 %copy-start = (s32[128,32]{0,1:T(8,128)S(1)}, s32[128,32]{0,1:T(8,128)}, u32[]{:S(2)}) copy-start(s32[128,32]{0,1:T(8,128)} %param.12) | copy-start | bytes 49156
  0.6 16.5 %copy-start.12 = (s32[4]{0:T(128)S(1)}, s32[4]{0:T(128)}, u32[]{:S(2)}) copy-start(s32[4]{0:T(128)} %constant.78.clone) | copy-start | bytes 52
  0.7 16.5 %copy-start.13 = (s32[4]{0:T(128)S(1)}, s32[4]{0:T(128)}, u32[]{:S(2)}) copy-start(s32[4]{0:T(128)} %constant.77.clone) | copy-start | bytes 52
  4.6 17.4 %collective-permute-start.2 = (bf16[256,1024]{1,0:T(8,128)(2,1)}, bf16[256,1024]{1,0:T(8,128)(2,1)S(1)}, u32[]{:S(2)}, u32[]{:S(2)}) collective-permute-start(bf16[256,1024]{1,0:T(8,128)(2,1)} %get-tuple-element.41.lo_even.hi_odd.rest_0_), channel_id=1, source_target_pairs={{0,7},{1,0},{2,1},{3,2},{4,3},{5,4},{6,5},{7,6},{8,15},{9,8},{10,9... | collective-permute-start | bytes 1572872 | tf_op jit(solution)/shard_map/ppermute | solution.py:453
  11.1 14.2 %collective-permute-start = (bf16[256,1024]{1,0:T(8,128)(2,1)}, bf16[256,1024]{1,0:T(8,128)(2,1)S(1)}, u32[]{:S(2)}, u32[]{:S(2)}) collective-permute-start(bf16[256,1024]{1,0:T(8,128)(2,1)} %get-tuple-element.41.lo_even.hi_odd.rest_0_), channel_id=1, source_target_pairs={{0,1},{1,2},{2,3},{3,4},{4,5},{5,6},{6,7},{7,0},{8,9},{9,10},{10,1... | collective-permute-start | bytes 1572872 | tf_op jit(solution)/shard_map/ppermute | solution.py:452
  11.1 14.9 %collective-permute-start.4 = (bf16[2,1536,128]{2,1,0:T(8,128)(2,1)}, bf16[2,1536,128]{2,1,0:T(8,128)(2,1)S(1)}, u32[]{:S(2)}, u32[]{:S(2)}) collective-permute-start(bf16[2,1536,128]{2,1,0:T(8,128)(2,1)} %get-tuple-element.42), channel_id=1, source_target_pairs={{0,8},{8,16},{16,24},{24,32},{32,40},{40,48},{48,56},{56,64},{64,7... | collective-permute-start | bytes 2359304 | tf_op jit(solution)/shard_map/ppermute | solution.py:429
  15.0 13.8 %collective-permute-start.5 = (bf16[2,1536,128]{2,1,0:T(8,128)(2,1)}, bf16[2,1536,128]{2,1,0:T(8,128)(2,1)S(1)}, u32[]{:S(2)}, u32[]{:S(2)}) collective-permute-start(bf16[2,1536,128]{2,1,0:T(8,128)(2,1)} %get-tuple-element.43), channel_id=1, source_target_pairs={{8,0},{16,8},{24,16},{32,24},{40,32},{48,40},{56,48},{64,56},{72,6... | collective-permute-start | bytes 2359304 | tf_op jit(solution)/shard_map/ppermute | solution.py:430
  22.0 6.9 %copy-start.9 = (bf16[256,1024]{1,0:T(8,128)(2,1)}, bf16[256,1024]{1,0:T(8,128)(2,1)S(1)}, u32[]{:S(2)}) copy-start(bf16[256,1024]{1,0:T(8,128)(2,1)S(1)} %collective-permute-done.2.hi_even.rest_2_.lo_odd) | copy-start | bytes 1572868
  22.0 15.9 %collective-permute-start.3 = (bf16[256,1024]{1,0:T(8,128)(2,1)S(1)}, bf16[256,1024]{1,0:T(8,128)(2,1)S(1)}, u32[]{:S(2)}, u32[]{:S(2)}) collective-permute-start(bf16[256,1024]{1,0:T(8,128)(2,1)S(1)} %collective-permute-done.2.hi_even.rest_2_.lo_odd), channel_id=1, source_target_pairs={{0,7},{1,0},{2,1},{3,2},{4,3},{5,4},{6,5},{7,6},{8,15},{9,8},{10,9... | collective-permute-start | bytes 1572872 | tf_op jit(solution)/shard_map/ppermute | solution.py:453
  25.3 3.6 %copy-start.10 = (bf16[256,1024]{1,0:T(8,128)(2,1)}, bf16[256,1024]{1,0:T(8,128)(2,1)S(1)}, u32[]{:S(2)}) copy-start(bf16[256,1024]{1,0:T(8,128)(2,1)S(1)} %collective-permute-done.lo_odd.rest_1_.hi_even) | copy-start | bytes 1572868
  25.3 12.8 %collective-permute-start.1 = (bf16[256,1024]{1,0:T(8,128)(2,1)S(1)}, bf16[256,1024]{1,0:T(8,128)(2,1)S(1)}, u32[]{:S(2)}, u32[]{:S(2)}) collective-permute-start(bf16[256,1024]{1,0:T(8,128)(2,1)S(1)} %collective-permute-done.lo_odd.rest_1_.hi_even), channel_id=1, source_target_pairs={{0,1},{1,2},{2,3},{3,4},{4,5},{5,6},{6,7},{7,0},{8,9},{9,10},{10,1... | collective-permute-start | bytes 1572872 | tf_op jit(solution)/shard_map/ppermute | solution.py:452
  38.1 12.6 %collective-permute-start.6 = (bf16[256,1024]{1,0:T(8,128)(2,1)S(1)}, bf16[256,1024]{1,0:T(8,128)(2,1)S(1)}, u32[]{:S(2)}, u32[]{:S(2)}) collective-permute-start(bf16[256,1024]{1,0:T(8,128)(2,1)S(1)} %collective-permute-done.1.lo_even.rest_0_.hi_odd), channel_id=1, source_target_pairs={{0,1},{1,2},{2,3},{3,4},{4,5},{5,6},{6,7},{7,0},{8,9},{9,10},{10,1... | collective-permute-start | bytes 1572872 | tf_op jit(solution)/shard_map/ppermute | solution.py:452
  38.1 12.6 %collective-permute-start.7 = (bf16[256,1024]{1,0:T(8,128)(2,1)S(1)}, bf16[256,1024]{1,0:T(8,128)(2,1)S(1)}, u32[]{:S(2)}, u32[]{:S(2)}) collective-permute-start(bf16[256,1024]{1,0:T(8,128)(2,1)S(1)} %collective-permute-done.3.hi_odd.rest_1_.lo_even), channel_id=1, source_target_pairs={{0,7},{1,0},{2,1},{3,2},{4,3},{5,4},{6,5},{7,6},{8,15},{9,8},{10,9... | collective-permute-start | bytes 1572872 | tf_op jit(solution)/shard_map/ppermute | solution.py:453
  50.7 4.3 %copy-start.4 = (bf16[256,1024]{1,0:T(8,128)(2,1)}, bf16[256,1024]{1,0:T(8,128)(2,1)S(1)}, u32[]{:S(2)}) copy-start(bf16[256,1024]{1,0:T(8,128)(2,1)S(1)} %collective-permute-done.6.lo_odd.rest_0_.hi_even) | copy-start | bytes 1572868
  50.7 4.3 %copy-start.5 = (bf16[256,1024]{1,0:T(8,128)(2,1)}, bf16[256,1024]{1,0:T(8,128)(2,1)S(1)}, u32[]{:S(2)}) copy-start(bf16[256,1024]{1,0:T(8,128)(2,1)S(1)} %collective-permute-done.7.hi_even.rest_1_.lo_odd) | copy-start | bytes 1572868
  50.7 12.4 %collective-permute-start.9 = (bf16[128,1024]{1,0:T(8,128)(2,1)S(1)}, bf16[128,1024]{1,0:T(8,128)(2,1)S(1)}, u32[]{:S(2)}, u32[]{:S(2)}) collective-permute-start(bf16[128,1024]{1,0:T(8,128)(2,1)S(1)} %slice.21), channel_id=1, source_target_pairs={{0,7},{1,0},{2,1},{3,2},{4,3},{5,4},{6,5},{7,6},{8,15},{9,8},{10,9... | collective-permute-start | bytes 786440 | tf_op jit(solution)/shard_map/ppermute | solution.py:456
  54.9 8.3 %collective-permute-start.8 = (bf16[128,1024]{1,0:T(8,128)(2,1)S(1)}, bf16[128,1024]{1,0:T(8,128)(2,1)S(1)}, u32[]{:S(2)}, u32[]{:S(2)}) collective-permute-start(bf16[128,1024]{1,0:T(8,128)(2,1)S(1)} %slice.20), channel_id=1, source_target_pairs={{0,1},{1,2},{2,3},{3,4},{4,5},{5,6},{6,7},{7,0},{8,9},{9,10},{10,1... | collective-permute-start | bytes 786440 | tf_op jit(solution)/shard_map/ppermute | solution.py:455
  72.1 50.0 %collective-permute-start.10 = (bf16[8,128,1024]{2,1,0:T(8,128)(2,1)}, bf16[8,128,1024]{2,1,0:T(8,128)(2,1)}, u32[]{:S(2)}, u32[]{:S(2)}) collective-permute-start(bf16[8,128,1024]{2,1,0:T(8,128)(2,1)} %get-tuple-element.70), channel_id=1, source_target_pairs={{0,8},{8,0},{16,24},{24,16},{32,40},{40,32},{48,56},{56,48},{64,72... | collective-permute-start | bytes 6291464 | tf_op jit(solution)/shard_map/ppermute | solution.py:486
  74.6 16.7 %all-to-all-start = ((bf16[8,64,256]{2,1,0:T(8,128)(2,1)}), bf16[8,64,256]{2,1,0:T(8,128)(2,1)S(1)}, u32[]{:S(2)}, u32[]{:S(2)}) async-start(bf16[8,64,256]{2,1,0:T(8,128)(2,1)} %bitcast.28), calls=%async_computation | async-start | bytes 524288 | tf_op jit(solution)/shard_map/all_to_all | solution.py:407
  84.5 32.1 %copy-start.1 = (bf16[8,128,1024]{2,1,0:T(8,128)(2,1)S(1)}, bf16[8,128,1024]{2,1,0:T(8,128)(2,1)}, u32[]{:S(2)}) copy-start(bf16[8,128,1024]{2,1,0:T(8,128)(2,1)} %get-tuple-element.70) | copy-start | bytes 6291460
  91.2 20.4 %all-to-all-start.1 = ((bf16[32,64,128]{2,1,0:T(8,128)(2,1)}), bf16[32,64,128]{2,1,0:T(8,128)(2,1)S(1)}, u32[]{:S(2)}, u32[]{:S(2)}) async-start(bf16[32,64,128]{2,1,0:T(8,128)(2,1)} %weight_terms.1), calls=%async_computation.1 | async-start | bytes 1048576 | tf_op jit(solution)/shard_map/all_to_all | solution.py:407
  100.0 17.1 %collective-permute-start.11 = (bf16[2,1536,128]{2,1,0:T(8,128)(2,1)}, bf16[2,1536,128]{2,1,0:T(8,128)(2,1)}, u32[]{:S(2)}, u32[]{:S(2)}) collective-permute-start(bf16[2,1536,128]{2,1,0:T(8,128)(2,1)} %get-tuple-element.71), channel_id=1, source_target_pairs={{0,8},{8,16},{16,24},{24,32},{32,40},{40,48},{48,56},{56,64},{64,7... | collective-permute-start | bytes 2359304 | tf_op jit(solution)/shard_map/ppermute | solution.py:485
  103.6 13.6 %collective-permute-start.12 = (bf16[2,1536,128]{2,1,0:T(8,128)(2,1)}, bf16[2,1536,128]{2,1,0:T(8,128)(2,1)}, u32[]{:S(2)}, u32[]{:S(2)}) collective-permute-start(bf16[2,1536,128]{2,1,0:T(8,128)(2,1)} %get-tuple-element.72), channel_id=1, source_target_pairs={{8,0},{16,8},{24,16},{32,24},{40,32},{48,40},{56,48},{64,56},{72,6... | collective-permute-start | bytes 2359304 | tf_op jit(solution)/shard_map/ppermute | solution.py:484
  112.6 15.7 %all-to-all-start.2 = ((bf16[32,64,128]{2,1,0:T(8,128)(2,1)}), bf16[32,64,128]{2,1,0:T(8,128)(2,1)S(1)}, u32[]{:S(2)}, u32[]{:S(2)}) async-start(bf16[32,64,128]{2,1,0:T(8,128)(2,1)} %broadcast_in_dim.20), calls=%async_computation.2 | async-start | bytes 1048576 | tf_op jit(solution)/shard_map/all_to_all | solution.py:407
  (6 other events, 12.1 us)

commit v5 on v4

--- a/solution.py
+++ b/solution.py
@@ -179,18 +179,25 @@
         copy.wait()
 
 
-def terms_kernel(rows, mixed, out):
-    attn = mixed[:, :BLK]
-    pre = mixed[:, BLK:]
-    by_query = contract(pre, rows[0], ((0,), (0,))).T.astype(jnp.bfloat16)
-    by_output = contract(attn, rows[1], ((0,), (0,))).astype(jnp.bfloat16)
-    count, both, _ = out.shape
-    cut = both // 2
+def terms_kernel(flag, rows, mixed, keep, send):
+    by_query = contract(mixed[:, BLK:], rows[0], ((0,), (0,))).T.astype(jnp.bfloat16)
+    by_output = contract(mixed[:, :BLK], rows[1], ((0,), (0,))).astype(jnp.bfloat16)
+    count, cut, _ = keep.shape
     groups = BLK // cut
-    for i in range(count):
-        out[i, :cut, :] = by_query[i * cut : (i + 1) * cut, :]
-        row, column = (i % groups) * cut, (i // groups) * BLK
-        out[i, cut:, :] = by_output[row : row + cut, column : column + BLK]
+
+    def store(q_out, o_out):
+        for i in range(count):
+            q_out[i] = by_query[i * cut : (i + 1) * cut, :]
+            row, column = (i % groups) * cut, (i // groups) * BLK
+            o_out[i] = by_output[row : row + cut, column : column + BLK]
+
+    @pl.when(flag[0] == 0)
+    def _():
+        store(keep, send)
+
+    @pl.when(flag[0] != 0)
+    def _():
+        store(send, keep)
 
 
 def rim_kernel(step_rows, grads, left_out, right_out, far_l, near_l, far_r, near_r, sems):
@@ -335,17 +342,17 @@
     )(place, bias, *shards, q_weight, o_weight, left, own, right, *pieces, *extra)
 
 
-def weight_terms(rows, mixed, parts):
-    width = rows.shape[2]
+def weight_terms(flag, rows, mixed, parts):
+    half = jax.ShapeDtypeStruct((parts, rows.shape[2] // parts, BLK), jnp.bfloat16)
     return pl.pallas_call(
         terms_kernel,
-        in_specs=[IN_VMEM] * 2,
-        out_specs=IN_VMEM,
-        out_shape=jax.ShapeDtypeStruct((parts, 2 * width // parts, BLK), jnp.bfloat16),
+        in_specs=[IN_SMEM] + [IN_VMEM] * 2,
+        out_specs=[IN_VMEM] * 2,
+        out_shape=[half, half],
         compiler_params=params(),
         cost_estimate=cost(1_000_000_000, 4_000_000),
         name="weight_terms",
-    )(rows, mixed)
+    )(flag, rows, mixed)
 
 
 def rim_grads(grads, rim, step_rows):
@@ -403,8 +410,8 @@
     return jnp.sum(arrived.astype(jnp.float32), axis=0, keepdims=True).astype(jnp.bfloat16)
 
 
-def exchange(parts, axis):
-    return lax.all_to_all(parts, axis, 0, 0, tiled=True)
+def exchange(parts, axis, groups=None):
+    return lax.all_to_all(parts, axis, 0, 0, tiled=True, axis_index_groups=groups)
 
 
 def on_device(slow_x, q_weight, o_weight, fast_kv, mask_lists, cotangent):
@@ -478,13 +485,18 @@
     mixed = exchange(rows_mixed.reshape(tp, own_rows, 2 * BLK), "tp")
     left_grads, right_grads = rim_grads(grads, rim, step_rows)
     rows_all, left_grads, right_grads = lax.optimization_barrier((rows_all, left_grads, right_grads))
-    terms = weight_terms(rows_all, rows_mixed, ctx)
-    terms, mixed = lax.optimization_barrier((terms, mixed))
-    own_terms = added(exchange(terms, "ctx"))
+    keep, send = weight_terms(flag, rows_all, rows_mixed, ctx)
+    swap = [(i, i ^ 1) for i in range(ctx)]
+    groups = [list(range(side, ctx, 2)) for side in range(2)]
+    partner = lax.ppermute(send, "ctx", swap)
+    keep, mixed = lax.optimization_barrier((keep, mixed))
+    terms = (keep.astype(jnp.float32) + partner.astype(jnp.float32)).astype(jnp.bfloat16)
+    terms = terms.reshape(ctx // 2, -1, BLK)
+    own_terms = added(exchange(terms, "ctx", groups))
     from_right = lax.ppermute(left_grads, "ctx", down)
     from_left = lax.ppermute(right_grads, "ctx", up)
     other = lax.ppermute(mine, "ctx", [(i, i ^ 1) for i in range(ctx)])
-    summed = exchange(jnp.broadcast_to(own_terms, terms.shape), "ctx")
+    summed = exchange(jnp.broadcast_to(own_terms, terms.shape), "ctx", groups)
     grad_kv = combine_grads(grads, from_left, from_right, fast_rows, step_rows)
 
     first = jnp.where(even, mixed[:, :, :BLK], mixed[:, :, BLK:])
@@ -498,9 +510,10 @@
     grad_slow = jnp.where(even, second, first)
 
     summed, attended, grad_slow, grad_kv = lax.optimization_barrier((summed, attended, grad_slow, grad_kv))
-    cut = terms.shape[1] // 2
-    grad_q_weight = summed[:, :cut].astype(jnp.float32).reshape(q_weight.shape)
-    blocked = summed[:, cut:].reshape(width // BLK, BLK // cut, cut, BLK).transpose(1, 2, 0, 3)
+    swapped = lax.ppermute(summed, "ctx", swap)
+    cut = keep.shape[1]
+    grad_q_weight = jnp.where(even, summed, swapped).astype(jnp.float32).reshape(q_weight.shape)
+    blocked = jnp.where(even, swapped, summed).reshape(width // BLK, BLK // cut, cut, BLK).transpose(1, 2, 0, 3)
     grad_o_weight = blocked.astype(jnp.float32).reshape(o_weight.shape)
     return (attended, grad_slow, grad_q_weight, grad_o_weight, grad_kv)
 

time: 131 us -> 128 us (0.977)
  waiting for transfers between devices: 24.8 us -> 21 us
  starting transfers between devices: 48.2 us -> 46.4 us
  other arithmetic: 2.4 us -> 4.07 us
    all_to_all x3, waiting for transfers between devices: 16.2 us -> 8.6 us  [exchange(): lax.all_to_all(parts, axis, 0, 0, tiled=True, axis_index_groups=groups)]
    ppermute x3, waiting for transfers between devices: 1.77 us -> 8.5 us  [pass_on(): f.append(lax.ppermute(back, 'tp', ahead))]
    ppermute x3, waiting for transfers between devices: 3.81 us -> 0.01 us  [pass_on(): b.append(lax.ppermute(front, 'tp', behind))]
    ppermute x3, starting transfers between devices: 13.1 us -> 9.35 us  [pass_on(): b.append(lax.ppermute(front, 'tp', behind))]
    ppermute x0 -> x2, starting transfers between devices: none -> 3.17 us  [the longest x1 2.86 us: on_device(): swapped = lax.ppermute(summed, 'ctx', swap)]
    ppermute x3, starting transfers between devices: 0.01 us -> 2.63 us  [pass_on(): f.append(lax.ppermute(back, 'tp', ahead))]
    all_to_all x3, starting transfers between devices: 17.1 us -> 15.3 us  [exchange(): lax.all_to_all(parts, axis, 0, 0, tiled=True, axis_index_groups=groups)]
    convert_element_type x0 -> x1, other arithmetic: none -> 1.72 us  [on_device(): (keep.astype(jnp.float32) + partner.astype(jnp.float32)).astype(jnp.bfloa...]
  transfers between devices with their start and end apart: 16 -> 18, of which waited for: 8 -> 6; matrix products, arithmetic and copies ran while one was open for 5% -> 6% of each run, Pallas kernels for 26% -> 27%
where the time goes in v5:
time: 128 us; the launch traced here: 127 us
  Pallas kernels  46.7 us (36%)
  starting transfers between devices  46.4 us (36%)
  waiting for transfers between devices  21 us (16%)
  local copies, waits for them, and re-layouts  4.96 us (4%)
  other arithmetic  4.07 us (3%)
  matrix products  3.26 us (3%)
    pallas_call x4, Pallas kernels, attention_pair(): pl.pallas_call(functools.partial(pair_kernel, step_rows, window, DH ** (-...  32.2 us
    all_to_all x3, starting transfers between devices, exchange(): lax.all_to_all(parts, axis, 0, 0, tiled=True, axis_index_groups=groups)  15.3 us
    ppermute x3, starting transfers between devices, pass_on(): b.append(lax.ppermute(front, 'tp', behind))  9.35 us
    all_to_all x3, waiting for transfers between devices, exchange(): lax.all_to_all(parts, axis, 0, 0, tiled=True, axis_index_groups=groups)  8.6 us
    ppermute x3, waiting for transfers between devices, pass_on(): f.append(lax.ppermute(back, 'tp', ahead))  8.5 us
    pallas_call x1, Pallas kernels, combine_grads(): pl.pallas_call(functools.partial(combine_kernel, step_rows), in_specs=[AN...  4.8 us
    ppermute x1, starting transfers between devices, on_device(): left = lax.ppermute(tail, 'ctx', up)  3.95 us
    pallas_call x1, Pallas kernels, pack(): pl.pallas_call(pack_kernel, in_specs=[IN_SMEM] + [IN_VMEM] * 4 + [ANYWHER...  3.87 us
  transfers between devices with their start and end apart: 18, of which 6 were waited for; matrix products, arithmetic and copies ran while one was open for 6% of the time, Pallas kernels for 27%

profile of v5, /device:TPU:1, one launch (start us, length us, event | category | flops | bytes accessed | tf_op | source)
XLA Modules:
  0.0 127.4 jit_solution(3467358059139571990)
XLA Ops:
  0.7 3.9 %pack.1 = (bf16[256,1024]{1,0:T(8,128)(2,1)}, bf16[2,1536,128]{2,1,0:T(8,128)(2,1)}, bf16[2,1536,128]{2,1,0:T(8,128)(2,1)}) custom-call(s32[1]{0:T(128)} %bitcast.flag, bf16[64,1024]{1,0:T(8,128)(2,1)} %x.1, bf16[64,1024]{1,0:T(8,128)(2,1)} %g.1, bf16[128,1024]{1,0:T(8,128)(2,1)} %o_weight.9, bf16[1024,128]{1,0:T(8,128)(2,1)} %q_weight.9, ...), custom_call_target="tpu_custom_call" | custom-call | bytes 4000000 | tf_op jit(solution)/shard_map/pack/pallas_call | solution.py:301
  4.6 2.5 %collective-permute-start = (bf16[256,1024]{1,0:T(8,128)(2,1)}, bf16[256,1024]{1,0:T(8,128)(2,1)S(1)}, u32[]{:S(2)}, u32[]{:S(2)}) collective-permute-start(bf16[256,1024]{1,0:T(8,128)(2,1)} %get-tuple-element.43.lo_even.hi_odd.rest_0_), channel_id=1, source_target_pairs={{0,1},{1,2},{2,3},{3,4},{4,5},{5,6},{6,7},{7,0},{8,9},{9,10},{10,1... | collective-permute-start | bytes 1572872 | tf_op jit(solution)/shard_map/ppermute | solution.py:459
  7.1 4.0 %collective-permute-start.2 = (bf16[256,1024]{1,0:T(8,128)(2,1)}, bf16[256,1024]{1,0:T(8,128)(2,1)S(1)}, u32[]{:S(2)}, u32[]{:S(2)}) collective-permute-start(bf16[256,1024]{1,0:T(8,128)(2,1)} %get-tuple-element.43.lo_even.hi_odd.rest_0_), channel_id=1, source_target_pairs={{0,7},{1,0},{2,1},{3,2},{4,3},{5,4},{6,5},{7,6},{8,15},{9,8},{10,9... | collective-permute-start | bytes 1572872 | tf_op jit(solution)/shard_map/ppermute | solution.py:460
  11.1 3.9 %collective-permute-start.4 = (bf16[2,1536,128]{2,1,0:T(8,128)(2,1)}, bf16[2,1536,128]{2,1,0:T(8,128)(2,1)S(1)}, u32[]{:S(2)}, u32[]{:S(2)}) collective-permute-start(bf16[2,1536,128]{2,1,0:T(8,128)(2,1)} %get-tuple-element.44), channel_id=1, source_target_pairs={{0,8},{8,16},{16,24},{24,32},{32,40},{40,48},{48,56},{56,64},{64,7... | collective-permute-start | bytes 2359304 | tf_op jit(solution)/shard_map/ppermute | solution.py:436
  18.2 4.7 %collective-permute-done.lo_odd.rest_1_.hi_even = bf16[256,1024]{1,0:T(8,128)(2,1)S(1)} collective-permute-done((bf16[256,1024]{1,0:T(8,128)(2,1)}, bf16[256,1024]{1,0:T(8,128)(2,1)S(1)}, u32[]{:S(2)}, u32[]{:S(2)}) %collective-permute-start) | collective-permute-done | bytes 524320 | tf_op jit(solution)/shard_map/ppermute | solution.py:459
  22.9 2.7 %collective-permute-start.3 = (bf16[256,1024]{1,0:T(8,128)(2,1)S(1)}, bf16[256,1024]{1,0:T(8,128)(2,1)S(1)}, u32[]{:S(2)}, u32[]{:S(2)}) collective-permute-start(bf16[256,1024]{1,0:T(8,128)(2,1)S(1)} %collective-permute-done.2.hi_even.rest_2_.lo_odd), channel_id=1, source_target_pairs={{0,7},{1,0},{2,1},{3,2},{4,3},{5,4},{6,5},{7,6},{8,15},{9,8},{10,9... | collective-permute-start | bytes 1572872 | tf_op jit(solution)/shard_map/ppermute | solution.py:460
  26.2 2.7 %collective-permute-done.5.right = bf16[2,1536,128]{2,1,0:T(8,128)(2,1)S(1)} collective-permute-done((bf16[2,1536,128]{2,1,0:T(8,128)(2,1)}, bf16[2,1536,128]{2,1,0:T(8,128)(2,1)S(1)}, u32[]{:S(2)}, u32[]{:S(2)}) %collective-permute-start.5) | collective-permute-done | bytes 786464 | tf_op jit(solution)/shard_map/ppermute | solution.py:437
  29.8 8.2 %attention_pair.4 = (bf16[4,2,4096,128]{3,2,1,0:T(8,128)(2,1)}, bf16[512,256]{1,0:T(8,128)(2,1)}, bf16[2,512,1024]{2,1,0:T(8,128)(2,1)}, bf16[8,128,1024]{2,1,0:T(8,128)(2,1)}) custom-call(s32[4,3]{1,0:T(4,128)} %add_add_fusion.place, f32[4,32]{1,0:T(4,128)} %broadcast_select_fusion.4.bias, bf16[256,1024]{1,0:T(8,128)(2,1)} %get-tuple-element.43.lo_even.hi_odd.rest_0_, ...), custom_call_target="tpu_custom_call" | custom-call | flops 4000000000 | bytes 10000000 | tf_op jit(solution)/shard_map/attention_pair/pallas_call | solution.py:326
  38.1 2.7 %collective-permute-start.7 = (bf16[256,1024]{1,0:T(8,128)(2,1)S(1)}, bf16[256,1024]{1,0:T(8,128)(2,1)S(1)}, u32[]{:S(2)}, u32[]{:S(2)}) collective-permute-start(bf16[256,1024]{1,0:T(8,128)(2,1)S(1)} %collective-permute-done.3.hi_odd.rest_1_.lo_even), channel_id=1, source_target_pairs={{0,7},{1,0},{2,1},{3,2},{4,3},{5,4},{6,5},{7,6},{8,15},{9,8},{10,9... | collective-permute-start | bytes 1572872 | tf_op jit(solution)/shard_map/ppermute | solution.py:460
  40.8 7.7 %attention_pair.5 = (bf16[4,2,4096,128]{3,2,1,0:T(8,128)(2,1)}, bf16[512,256]{1,0:T(8,128)(2,1)}, bf16[2,512,1024]{2,1,0:T(8,128)(2,1)}, bf16[8,128,1024]{2,1,0:T(8,128)(2,1)}) custom-call(s32[4,3]{1,0:T(4,128)} %add_add_fusion.place, ...), custom_call_target="tpu_custom_call", output_to_operand_aliasing={{0}: (13, {}), {1}: (14, {}), {2}: (15, {}), {3}: (16, {})} | custom-call | flops 4000000000 | bytes 10000000 | tf_op jit(solution)/shard_map/attention_pair/pallas_call | solution.py:326
  48.5 3.8 %collective-permute-done.6.lo_odd.rest_0_.hi_even = bf16[256,1024]{1,0:T(8,128)(2,1)S(1)} collective-permute-done((bf16[256,1024]{1,0:T(8,128)(2,1)S(1)}, bf16[256,1024]{1,0:T(8,128)(2,1)S(1)}, u32[]{:S(2)}, u32[]{:S(2)}) %collective-permute-start.6) | collective-permute-done | bytes 524320 | tf_op jit(solution)/shard_map/ppermute | solution.py:459
  52.5 3.0 %collective-permute-start.9 = (bf16[128,1024]{1,0:T(8,128)(2,1)S(1)}, bf16[128,1024]{1,0:T(8,128)(2,1)S(1)}, u32[]{:S(2)}, u32[]{:S(2)}) collective-permute-start(bf16[128,1024]{1,0:T(8,128)(2,1)S(1)} %slice.15), channel_id=1, source_target_pairs={{0,7},{1,0},{2,1},{3,2},{4,3},{5,4},{6,5},{7,6},{8,15},{9,8},{10,9... | collective-permute-start | bytes 786440 | tf_op jit(solution)/shard_map/ppermute | solution.py:463
  55.4 8.2 %attention_pair.6 = (bf16[4,2,4096,128]{3,2,1,0:T(8,128)(2,1)}, bf16[512,256]{1,0:T(8,128)(2,1)}, bf16[2,512,1024]{2,1,0:T(8,128)(2,1)}, bf16[8,128,1024]{2,1,0:T(8,128)(2,1)}) custom-call(s32[4,3]{1,0:T(4,128)} %add_add_fusion.place, ...), custom_call_target="tpu_custom_call", output_to_operand_aliasing={{0}: (13, {}), {1}: (14, {}), {2}: (15, {}), {3}: (16, {})} | custom-call | flops 4000000000 | bytes 10000000 | tf_op jit(solution)/shard_map/attention_pair/pallas_call | solution.py:326
  64.5 8.1 %attention_pair.7 = (bf16[4,2,4096,128]{3,2,1,0:T(8,128)(2,1)}, bf16[512,256]{1,0:T(8,128)(2,1)}, bf16[2,512,1024]{2,1,0:T(8,128)(2,1)}, bf16[8,128,1024]{2,1,0:T(8,128)(2,1)}) custom-call(s32[4,3]{1,0:T(4,128)} %add_add_fusion.place, ...), custom_call_target="tpu_custom_call", output_to_operand_aliasing={{0}: (12, {}), {1}: (13, {}), {2}: (14, {}), {3}: (15, {})} | custom-call | flops 4000000000 | bytes 10000000 | tf_op jit(solution)/shard_map/attention_pair/pallas_call | solution.py:326
  74.5 5.0 %all-to-all-start = ((bf16[8,64,256]{2,1,0:T(8,128)(2,1)}), bf16[8,64,256]{2,1,0:T(8,128)(2,1)S(1)}, u32[]{:S(2)}, u32[]{:S(2)}) async-start(bf16[8,64,256]{2,1,0:T(8,128)(2,1)} %bitcast.29), calls=%async_computation | async-start | bytes 524288 | tf_op jit(solution)/shard_map/all_to_all | solution.py:414
  79.5 2.8 %rim_grads.1 = (bf16[2,1536,128]{2,1,0:T(8,128)(2,1)}, bf16[2,1536,128]{2,1,0:T(8,128)(2,1)}) custom-call(bf16[4,2,4096,128]{3,2,1,0:T(8,128)(2,1)} %get-tuple-element.65.grads), custom_call_target="tpu_custom_call" | custom-call | flops 1000000 | bytes 5000000 | tf_op jit(solution)/shard_map/rim_grads/pallas_call | solution.py:361
  82.3 3.1 %weight_terms.1 = (bf16[32,32,128]{2,1,0:T(8,128)(2,1)}, bf16[32,32,128]{2,1,0:T(8,128)(2,1)}) custom-call(s32[1]{0:T(128)} %bitcast.flag, bf16[2,512,1024]{2,1,0:T(8,128)(2,1)} %get-tuple-element.68.rows, bf16[512,256]{1,0:T(8,128)(2,1)} %get-tuple-element.69.mixed), custom_call_target="tpu_custom_call" | custom-call | flops 1000000000 | bytes 4000000 | tf_op jit(solution)/shard_map/weight_terms/pallas_call | solution.py:347
  85.7 3.2 %collective-permute-start.12 = (bf16[2,1536,128]{2,1,0:T(8,128)(2,1)}, bf16[2,1536,128]{2,1,0:T(8,128)(2,1)S(1)}, u32[]{:S(2)}, u32[]{:S(2)}) collective-permute-start(bf16[2,1536,128]{2,1,0:T(8,128)(2,1)} %get-tuple-element.75), channel_id=1, source_target_pairs={{0,8},{8,16},{16,24},{24,32},{32,40},{40,48},{48,56},{56,64},{64,7... | collective-permute-start | bytes 2359304 | tf_op jit(solution)/shard_map/ppermute | solution.py:497
  93.6 6.5 %all-to-all-start.1 = ((bf16[16,64,128]{2,1,0:T(8,128)(2,1)}), bf16[16,64,128]{2,1,0:T(8,128)(2,1)S(1)}, u32[]{:S(2)}, u32[]{:S(2)}) async-start(bf16[16,64,128]{2,1,0:T(8,128)(2,1)} %bitcast.3), calls=%async_computation.1 | async-start | bytes 524288 | tf_op jit(solution)/shard_map/all_to_all | solution.py:414
  100.6 7.5 %all-to-all-done.1 = bf16[16,64,128]{2,1,0:T(8,128)(2,1)S(1)} async-done(((bf16[16,64,128]{2,1,0:T(8,128)(2,1)}), bf16[16,64,128]{2,1,0:T(8,128)(2,1)S(1)}, u32[]{:S(2)}, u32[]{:S(2)}) %all-to-all-start.1) | async-done | bytes 262176 | tf_op jit(solution)/shard_map/all_to_all | solution.py:414
  108.9 3.8 %all-to-all-start.2 = ((bf16[16,64,128]{2,1,0:T(8,128)(2,1)}), bf16[16,64,128]{2,1,0:T(8,128)(2,1)S(1)}, u32[]{:S(2)}, u32[]{:S(2)}) async-start(bf16[16,64,128]{2,1,0:T(8,128)(2,1)} %broadcast_in_dim.20), calls=%async_computation.2 | async-start | bytes 524288 | tf_op jit(solution)/shard_map/all_to_all | solution.py:414
  113.6 4.8 %combine_grads.1 = bf16[2,4096,128]{2,1,0:T(8,128)(2,1)} custom-call(bf16[4,2,4096,128]{3,2,1,0:T(8,128)(2,1)} %get-tuple-element.65.grads, bf16[2,1536,128]{2,1,0:T(8,128)(2,1)} %copy-done.9, bf16[2,1536,128]{2,1,0:T(8,128)(2,1)} %collective-permute-done.13.from_right), custom_call_target="tpu_custom_call" | custom-call | flops 5000000 | bytes 10000000 | tf_op jit(solution)/shard_map/combine_grads/pallas_call | solution.py:380
  118.4 2.8 %broadcast_select_fusion.2 = (bf16[64,1024]{1,0:T(8,128)(2,1)}, bf16[64,1024]{1,0:T(8,128)(2,1)}) fusion(bf16[64,1024]{1,0:T(8,128)(2,1)S(1)} %fusion, pred[]{:T(512)S(6)} %eq.25, bf16[8,128,1024]{2,1,0:T(8,128)(2,1)} %collective-permute-done.11, bf16[8,64,256]{2,1,0:T(8,128)(2,1)S(1)} %all-to-all-done), kind=kOutput, calls=%fused_computation.14 | convolution fusion | flops 134479872 | bytes 2753536 | tf_op jit(solution)/shard_map/trk,tkn->rn/dot_general | solution.py:504
  121.2 2.9 %collective-permute-start.14 = (bf16[16,64,128]{2,1,0:T(8,128)(2,1)S(1)}, bf16[16,64,128]{2,1,0:T(8,128)(2,1)S(1)}, u32[]{:S(2)}, u32[]{:S(2)}) collective-permute-start(bf16[16,64,128]{2,1,0:T(8,128)(2,1)S(1)} %all-to-all-done.2), channel_id=1, source_target_pairs={{0,8},{8,0},{16,24},{24,16},{32,40},{40,32},{48,56},{56,48},{64,72... | collective-permute-start | bytes 786440 | tf_op jit(solution)/shard_map/ppermute | solution.py:513
  (73 shorter events, 18.1 us)
Async XLA Ops:
  0.6 16.5 %copy-start = (s32[128,32]{0,1:T(8,128)S(1)}, s32[128,32]{0,1:T(8,128)}, u32[]{:S(2)}) copy-start(s32[128,32]{0,1:T(8,128)} %param.12) | copy-start | bytes 49156
  0.6 16.4 %copy-start.13 = (s32[4]{0:T(128)S(1)}, s32[4]{0:T(128)}, u32[]{:S(2)}) copy-start(s32[4]{0:T(128)} %constant.77.clone) | copy-start | bytes 52
  0.7 16.4 %copy-start.14 = (s32[4]{0:T(128)S(1)}, s32[4]{0:T(128)}, u32[]{:S(2)}) copy-start(s32[4]{0:T(128)} %constant.78.clone) | copy-start | bytes 52
  4.6 18.3 %collective-permute-start = (bf16[256,1024]{1,0:T(8,128)(2,1)}, bf16[256,1024]{1,0:T(8,128)(2,1)S(1)}, u32[]{:S(2)}, u32[]{:S(2)}) collective-permute-start(bf16[256,1024]{1,0:T(8,128)(2,1)} %get-tuple-element.43.lo_even.hi_odd.rest_0_), channel_id=1, source_target_pairs={{0,1},{1,2},{2,3},{3,4},{4,5},{5,6},{6,7},{7,0},{8,9},{9,10},{10,1... | collective-permute-start | bytes 1572872 | tf_op jit(solution)/shard_map/ppermute | solution.py:459
  7.1 15.8 %collective-permute-start.2 = (bf16[256,1024]{1,0:T(8,128)(2,1)}, bf16[256,1024]{1,0:T(8,128)(2,1)S(1)}, u32[]{:S(2)}, u32[]{:S(2)}) collective-permute-start(bf16[256,1024]{1,0:T(8,128)(2,1)} %get-tuple-element.43.lo_even.hi_odd.rest_0_), channel_id=1, source_target_pairs={{0,7},{1,0},{2,1},{3,2},{4,3},{5,4},{6,5},{7,6},{8,15},{9,8},{10,9... | collective-permute-start | bytes 1572872 | tf_op jit(solution)/shard_map/ppermute | solution.py:460
  11.1 15.0 %collective-permute-start.4 = (bf16[2,1536,128]{2,1,0:T(8,128)(2,1)}, bf16[2,1536,128]{2,1,0:T(8,128)(2,1)S(1)}, u32[]{:S(2)}, u32[]{:S(2)}) collective-permute-start(bf16[2,1536,128]{2,1,0:T(8,128)(2,1)} %get-tuple-element.44), channel_id=1, source_target_pairs={{0,8},{8,16},{16,24},{24,32},{32,40},{40,48},{48,56},{56,64},{64,7... | collective-permute-start | bytes 2359304 | tf_op jit(solution)/shard_map/ppermute | solution.py:436
  15.1 13.8 %collective-permute-start.5 = (bf16[2,1536,128]{2,1,0:T(8,128)(2,1)}, bf16[2,1536,128]{2,1,0:T(8,128)(2,1)S(1)}, u32[]{:S(2)}, u32[]{:S(2)}) collective-permute-start(bf16[2,1536,128]{2,1,0:T(8,128)(2,1)} %get-tuple-element.45), channel_id=1, source_target_pairs={{8,0},{16,8},{24,16},{32,24},{40,32},{48,40},{56,48},{64,56},{72,6... | collective-permute-start | bytes 2359304 | tf_op jit(solution)/shard_map/ppermute | solution.py:437
  22.9 6.0 %copy-start.10 = (bf16[256,1024]{1,0:T(8,128)(2,1)}, bf16[256,1024]{1,0:T(8,128)(2,1)S(1)}, u32[]{:S(2)}) copy-start(bf16[256,1024]{1,0:T(8,128)(2,1)S(1)} %collective-permute-done.lo_odd.rest_1_.hi_even) | copy-start | bytes 1572868
  22.9 15.1 %collective-permute-start.1 = (bf16[256,1024]{1,0:T(8,128)(2,1)S(1)}, bf16[256,1024]{1,0:T(8,128)(2,1)S(1)}, u32[]{:S(2)}, u32[]{:S(2)}) collective-permute-start(bf16[256,1024]{1,0:T(8,128)(2,1)S(1)} %collective-permute-done.lo_odd.rest_1_.hi_even), channel_id=1, source_target_pairs={{0,1},{1,2},{2,3},{3,4},{4,5},{5,6},{6,7},{7,0},{8,9},{9,10},{10,1... | collective-permute-start | bytes 1572872 | tf_op jit(solution)/shard_map/ppermute | solution.py:459
  22.9 6.0 %copy-start.11 = (bf16[256,1024]{1,0:T(8,128)(2,1)}, bf16[256,1024]{1,0:T(8,128)(2,1)S(1)}, u32[]{:S(2)}) copy-start(bf16[256,1024]{1,0:T(8,128)(2,1)S(1)} %collective-permute-done.2.hi_even.rest_2_.lo_odd) | copy-start | bytes 1572868
  22.9 15.0 %collective-permute-start.3 = (bf16[256,1024]{1,0:T(8,128)(2,1)S(1)}, bf16[256,1024]{1,0:T(8,128)(2,1)S(1)}, u32[]{:S(2)}, u32[]{:S(2)}) collective-permute-start(bf16[256,1024]{1,0:T(8,128)(2,1)S(1)} %collective-permute-done.2.hi_even.rest_2_.lo_odd), channel_id=1, source_target_pairs={{0,7},{1,0},{2,1},{3,2},{4,3},{5,4},{6,5},{7,6},{8,15},{9,8},{10,9... | collective-permute-start | bytes 1572872 | tf_op jit(solution)/shard_map/ppermute | solution.py:460
  38.0 14.3 %collective-permute-start.6 = (bf16[256,1024]{1,0:T(8,128)(2,1)S(1)}, bf16[256,1024]{1,0:T(8,128)(2,1)S(1)}, u32[]{:S(2)}, u32[]{:S(2)}) collective-permute-start(bf16[256,1024]{1,0:T(8,128)(2,1)S(1)} %collective-permute-done.1.lo_even.rest_0_.hi_odd), channel_id=1, source_target_pairs={{0,1},{1,2},{2,3},{3,4},{4,5},{5,6},{6,7},{7,0},{8,9},{9,10},{10,1... | collective-permute-start | bytes 1572872 | tf_op jit(solution)/shard_map/ppermute | solution.py:459
  38.1 14.2 %collective-permute-start.7 = (bf16[256,1024]{1,0:T(8,128)(2,1)S(1)}, bf16[256,1024]{1,0:T(8,128)(2,1)S(1)}, u32[]{:S(2)}, u32[]{:S(2)}) collective-permute-start(bf16[256,1024]{1,0:T(8,128)(2,1)S(1)} %collective-permute-done.3.hi_odd.rest_1_.lo_even), channel_id=1, source_target_pairs={{0,7},{1,0},{2,1},{3,2},{4,3},{5,4},{6,5},{7,6},{8,15},{9,8},{10,9... | collective-permute-start | bytes 1572872 | tf_op jit(solution)/shard_map/ppermute | solution.py:460
  52.3 11.3 %collective-permute-start.8 = (bf16[128,1024]{1,0:T(8,128)(2,1)S(1)}, bf16[128,1024]{1,0:T(8,128)(2,1)S(1)}, u32[]{:S(2)}, u32[]{:S(2)}) collective-permute-start(bf16[128,1024]{1,0:T(8,128)(2,1)S(1)} %slice.14), channel_id=1, source_target_pairs={{0,1},{1,2},{2,3},{3,4},{4,5},{5,6},{6,7},{7,0},{8,9},{9,10},{10,1... | collective-permute-start | bytes 786440 | tf_op jit(solution)/shard_map/ppermute | solution.py:462
  52.5 11.2 %collective-permute-start.9 = (bf16[128,1024]{1,0:T(8,128)(2,1)S(1)}, bf16[128,1024]{1,0:T(8,128)(2,1)S(1)}, u32[]{:S(2)}, u32[]{:S(2)}) collective-permute-start(bf16[128,1024]{1,0:T(8,128)(2,1)S(1)} %slice.15), channel_id=1, source_target_pairs={{0,7},{1,0},{2,1},{3,2},{4,3},{5,4},{6,5},{7,6},{8,15},{9,8},{10,9... | collective-permute-start | bytes 786440 | tf_op jit(solution)/shard_map/ppermute | solution.py:463
  72.6 45.9 %collective-permute-start.11 = (bf16[8,128,1024]{2,1,0:T(8,128)(2,1)}, bf16[8,128,1024]{2,1,0:T(8,128)(2,1)}, u32[]{:S(2)}, u32[]{:S(2)}) collective-permute-start(bf16[8,128,1024]{2,1,0:T(8,128)(2,1)} %get-tuple-element.74), channel_id=1, source_target_pairs={{0,8},{8,0},{16,24},{24,16},{32,40},{40,32},{48,56},{56,48},{64,72... | collective-permute-start | bytes 6291464 | tf_op jit(solution)/shard_map/ppermute | solution.py:498
  74.5 17.4 %all-to-all-start = ((bf16[8,64,256]{2,1,0:T(8,128)(2,1)}), bf16[8,64,256]{2,1,0:T(8,128)(2,1)S(1)}, u32[]{:S(2)}, u32[]{:S(2)}) async-start(bf16[8,64,256]{2,1,0:T(8,128)(2,1)} %bitcast.29), calls=%async_computation | async-start | bytes 524288 | tf_op jit(solution)/shard_map/all_to_all | solution.py:414
  82.3 17.8 %copy-start.1 = (bf16[8,128,1024]{2,1,0:T(8,128)(2,1)S(1)}, bf16[8,128,1024]{2,1,0:T(8,128)(2,1)}, u32[]{:S(2)}) copy-start(bf16[8,128,1024]{2,1,0:T(8,128)(2,1)} %get-tuple-element.74) | copy-start | bytes 6291460
  85.4 6.5 %collective-permute-start.10 = (bf16[32,32,128]{2,1,0:T(8,128)(2,1)}, bf16[32,32,128]{2,1,0:T(8,128)(2,1)S(1)}, u32[]{:S(2)}, u32[]{:S(2)}) collective-permute-start(bf16[32,32,128]{2,1,0:T(8,128)(2,1)} %get-tuple-element.72), channel_id=1, source_target_pairs={{0,8},{8,0},{16,24},{24,16},{32,40},{40,32},{48,56},{56,48},{64,72... | collective-permute-start | bytes 786440 | tf_op jit(solution)/shard_map/ppermute | solution.py:491
  85.7 27.0 %collective-permute-start.12 = (bf16[2,1536,128]{2,1,0:T(8,128)(2,1)}, bf16[2,1536,128]{2,1,0:T(8,128)(2,1)S(1)}, u32[]{:S(2)}, u32[]{:S(2)}) collective-permute-start(bf16[2,1536,128]{2,1,0:T(8,128)(2,1)} %get-tuple-element.75), channel_id=1, source_target_pairs={{0,8},{8,16},{16,24},{24,32},{32,40},{40,48},{48,56},{56,64},{64,7... | collective-permute-start | bytes 2359304 | tf_op jit(solution)/shard_map/ppermute | solution.py:497
  88.9 23.8 %collective-permute-start.13 = (bf16[2,1536,128]{2,1,0:T(8,128)(2,1)}, bf16[2,1536,128]{2,1,0:T(8,128)(2,1)}, u32[]{:S(2)}, u32[]{:S(2)}) collective-permute-start(bf16[2,1536,128]{2,1,0:T(8,128)(2,1)} %get-tuple-element.76), channel_id=1, source_target_pairs={{8,0},{16,8},{24,16},{32,24},{40,32},{48,40},{56,48},{64,56},{72,6... | collective-permute-start | bytes 2359304 | tf_op jit(solution)/shard_map/ppermute | solution.py:496
  93.6 14.5 %all-to-all-start.1 = ((bf16[16,64,128]{2,1,0:T(8,128)(2,1)}), bf16[16,64,128]{2,1,0:T(8,128)(2,1)S(1)}, u32[]{:S(2)}, u32[]{:S(2)}) async-start(bf16[16,64,128]{2,1,0:T(8,128)(2,1)} %bitcast.3), calls=%async_computation.1 | async-start | bytes 524288 | tf_op jit(solution)/shard_map/all_to_all | solution.py:414
  108.9 12.3 %all-to-all-start.2 = ((bf16[16,64,128]{2,1,0:T(8,128)(2,1)}), bf16[16,64,128]{2,1,0:T(8,128)(2,1)S(1)}, u32[]{:S(2)}, u32[]{:S(2)}) async-start(bf16[16,64,128]{2,1,0:T(8,128)(2,1)} %broadcast_in_dim.20), calls=%async_computation.2 | async-start | bytes 524288 | tf_op jit(solution)/shard_map/all_to_all | solution.py:414
  121.2 4.0 %collective-permute-start.14 = (bf16[16,64,128]{2,1,0:T(8,128)(2,1)S(1)}, bf16[16,64,128]{2,1,0:T(8,128)(2,1)S(1)}, u32[]{:S(2)}, u32[]{:S(2)}) collective-permute-start(bf16[16,64,128]{2,1,0:T(8,128)(2,1)S(1)} %all-to-all-done.2), channel_id=1, source_target_pairs={{0,8},{8,0},{16,24},{24,16},{32,40},{40,32},{48,56},{56,48},{64,72... | collective-permute-start | bytes 786440 | tf_op jit(solution)/shard_map/ppermute | solution.py:513
  (9 other events, 17.8 us)

commit v6 on v5

--- a/solution.py
+++ b/solution.py
@@ -349,7 +349,7 @@
         in_specs=[IN_SMEM] + [IN_VMEM] * 2,
         out_specs=[IN_VMEM] * 2,
         out_shape=[half, half],
-        compiler_params=params(),
+        compiler_params=pltpu.CompilerParams(vmem_limit_bytes=24 * 1024 * 1024),
         cost_estimate=cost(1_000_000_000, 4_000_000),
         name="weight_terms",
     )(flag, rows, mixed)
@@ -492,11 +492,10 @@
     keep, mixed = lax.optimization_barrier((keep, mixed))
     terms = (keep.astype(jnp.float32) + partner.astype(jnp.float32)).astype(jnp.bfloat16)
     terms = terms.reshape(ctx // 2, -1, BLK)
-    own_terms = added(exchange(terms, "ctx", groups))
+    arrived_terms = exchange(terms, "ctx", groups)
     from_right = lax.ppermute(left_grads, "ctx", down)
     from_left = lax.ppermute(right_grads, "ctx", up)
     other = lax.ppermute(mine, "ctx", [(i, i ^ 1) for i in range(ctx)])
-    summed = exchange(jnp.broadcast_to(own_terms, terms.shape), "ctx", groups)
     grad_kv = combine_grads(grads, from_left, from_right, fast_rows, step_rows)
 
     first = jnp.where(even, mixed[:, :, :BLK], mixed[:, :, BLK:])
@@ -509,7 +508,10 @@
     attended = jnp.where(even, first, second)
     grad_slow = jnp.where(even, second, first)
 
-    summed, attended, grad_slow, grad_kv = lax.optimization_barrier((summed, attended, grad_slow, grad_kv))
+    arrived_terms, attended, grad_slow = lax.optimization_barrier((arrived_terms, attended, grad_slow))
+    own_terms = added(arrived_terms)
+    summed = exchange(jnp.broadcast_to(own_terms, terms.shape), "ctx", groups)
+    summed, grad_kv = lax.optimization_barrier((summed, grad_kv))
     swapped = lax.ppermute(summed, "ctx", swap)
     cut = keep.shape[1]
     grad_q_weight = jnp.where(even, summed, swapped).astype(jnp.float32).reshape(q_weight.shape)

time: 128 us -> 126 us (0.984)
  Pallas kernels: 46.7 us -> 44.4 us
  waiting for transfers between devices: 21 us -> 23.3 us
    pallas_call x1, Pallas kernels: 3.05 us -> 0.52 us  [weight_terms(): pl.pallas_call(terms_kernel, in_specs=[IN_SMEM] + [IN_VMEM] * 2, out_spec...]
    all_to_all x3, waiting for transfers between devices: 8.6 us -> 10.8 us  [exchange(): lax.all_to_all(parts, axis, 0, 0, tiled=True, axis_index_groups=groups)]
    unnamed x31 -> x33, local copies, waits for them, and re-layouts: 3.47 us -> 2.64 us
  transfers between devices with their start and end apart: 18 -> 18, of which waited for: 6 -> 7; matrix products, arithmetic and copies ran while one was open for 6% -> 5% of each run, Pallas kernels for 27% -> 26%
where the time goes in v6:
time: 126 us; the launch traced here: 125 us
  starting transfers between devices  45.9 us (36%)
  Pallas kernels  44.4 us (35%)
  waiting for transfers between devices  23.3 us (18%)
  local copies, waits for them, and re-layouts  4.13 us (3%)
  matrix products  3.26 us (3%)
  other arithmetic  3.12 us (2%)
    pallas_call x4, Pallas kernels, attention_pair(): pl.pallas_call(functools.partial(pair_kernel, step_rows, window, DH ** (-...  32.2 us
    all_to_all x3, starting transfers between devices, exchange(): lax.all_to_all(parts, axis, 0, 0, tiled=True, axis_index_groups=groups)  15 us
    all_to_all x3, waiting for transfers between devices, exchange(): lax.all_to_all(parts, axis, 0, 0, tiled=True, axis_index_groups=groups)  10.8 us
    ppermute x3, starting transfers between devices, pass_on(): b.append(lax.ppermute(front, 'tp', behind))  9.35 us
    ppermute x3, waiting for transfers between devices, pass_on(): f.append(lax.ppermute(back, 'tp', ahead))  8.54 us
    pallas_call x1, Pallas kernels, combine_grads(): pl.pallas_call(functools.partial(combine_kernel, step_rows), in_specs=[AN...  4.81 us
    ppermute x1, starting transfers between devices, on_device(): left = lax.ppermute(tail, 'ctx', up)  3.95 us
    pallas_call x1, Pallas kernels, pack(): pl.pallas_call(pack_kernel, in_specs=[IN_SMEM] + [IN_VMEM] * 4 + [ANYWHER...  3.88 us
  transfers between devices with their start and end apart: 18, of which 7 were waited for; matrix products, arithmetic and copies ran while one was open for 5% of the time, Pallas kernels for 26%

profile of v6, /device:TPU:1, one launch (start us, length us, event | category | flops | bytes accessed | tf_op | source)
XLA Modules:
  0.0 125.1 jit_solution(8870153825295719545)
XLA Ops:
  0.7 3.9 %pack.1 = (bf16[256,1024]{1,0:T(8,128)(2,1)}, bf16[2,1536,128]{2,1,0:T(8,128)(2,1)}, bf16[2,1536,128]{2,1,0:T(8,128)(2,1)}) custom-call(s32[1]{0:T(128)} %bitcast.flag, bf16[64,1024]{1,0:T(8,128)(2,1)} %x.1, bf16[64,1024]{1,0:T(8,128)(2,1)} %g.1, bf16[128,1024]{1,0:T(8,128)(2,1)} %o_weight.9, bf16[1024,128]{1,0:T(8,128)(2,1)} %q_weight.9, ...), custom_call_target="tpu_custom_call" | custom-call | bytes 4000000 | tf_op jit(solution)/shard_map/pack/pallas_call | solution.py:301
  7.1 4.0 %collective-permute-start.2 = (bf16[256,1024]{1,0:T(8,128)(2,1)}, bf16[256,1024]{1,0:T(8,128)(2,1)S(1)}, u32[]{:S(2)}, u32[]{:S(2)}) collective-permute-start(bf16[256,1024]{1,0:T(8,128)(2,1)} %get-tuple-element.44.lo_even.hi_odd.rest_0_), channel_id=1, source_target_pairs={{0,7},{1,0},{2,1},{3,2},{4,3},{5,4},{6,5},{7,6},{8,15},{9,8},{10,9... | collective-permute-start | bytes 1572872 | tf_op jit(solution)/shard_map/ppermute | solution.py:460
  11.1 3.9 %collective-permute-start.4 = (bf16[2,1536,128]{2,1,0:T(8,128)(2,1)}, bf16[2,1536,128]{2,1,0:T(8,128)(2,1)S(1)}, u32[]{:S(2)}, u32[]{:S(2)}) collective-permute-start(bf16[2,1536,128]{2,1,0:T(8,128)(2,1)} %get-tuple-element.45), channel_id=1, source_target_pairs={{0,8},{8,16},{16,24},{24,32},{32,40},{40,48},{48,56},{56,64},{64,7... | collective-permute-start | bytes 2359304 | tf_op jit(solution)/shard_map/ppermute | solution.py:436
  18.3 4.7 %collective-permute-done.lo_odd.rest_1_.hi_even = bf16[256,1024]{1,0:T(8,128)(2,1)S(1)} collective-permute-done((bf16[256,1024]{1,0:T(8,128)(2,1)}, bf16[256,1024]{1,0:T(8,128)(2,1)S(1)}, u32[]{:S(2)}, u32[]{:S(2)}) %collective-permute-start) | collective-permute-done | bytes 524320 | tf_op jit(solution)/shard_map/ppermute | solution.py:459
  22.9 2.7 %collective-permute-start.3 = (bf16[256,1024]{1,0:T(8,128)(2,1)S(1)}, bf16[256,1024]{1,0:T(8,128)(2,1)S(1)}, u32[]{:S(2)}, u32[]{:S(2)}) collective-permute-start(bf16[256,1024]{1,0:T(8,128)(2,1)S(1)} %collective-permute-done.2.hi_even.rest_2_.lo_odd), channel_id=1, source_target_pairs={{0,7},{1,0},{2,1},{3,2},{4,3},{5,4},{6,5},{7,6},{8,15},{9,8},{10,9... | collective-permute-start | bytes 1572872 | tf_op jit(solution)/shard_map/ppermute | solution.py:460
  26.2 2.7 %collective-permute-done.5.right = bf16[2,1536,128]{2,1,0:T(8,128)(2,1)S(1)} collective-permute-done((bf16[2,1536,128]{2,1,0:T(8,128)(2,1)}, bf16[2,1536,128]{2,1,0:T(8,128)(2,1)S(1)}, u32[]{:S(2)}, u32[]{:S(2)}) %collective-permute-start.5) | collective-permute-done | bytes 786464 | tf_op jit(solution)/shard_map/ppermute | solution.py:437
  29.8 8.2 %attention_pair.4 = (bf16[4,2,4096,128]{3,2,1,0:T(8,128)(2,1)}, bf16[512,256]{1,0:T(8,128)(2,1)}, bf16[2,512,1024]{2,1,0:T(8,128)(2,1)}, bf16[8,128,1024]{2,1,0:T(8,128)(2,1)}) custom-call(s32[4,3]{1,0:T(4,128)} %add_add_fusion.place, f32[4,32]{1,0:T(4,128)} %broadcast_select_fusion.4.bias, bf16[256,1024]{1,0:T(8,128)(2,1)} %get-tuple-element.44.lo_even.hi_odd.rest_0_, ...), custom_call_target="tpu_custom_call" | custom-call | flops 4000000000 | bytes 10000000 | tf_op jit(solution)/shard_map/attention_pair/pallas_call | solution.py:326
  38.1 2.7 %collective-permute-start.7 = (bf16[256,1024]{1,0:T(8,128)(2,1)S(1)}, bf16[256,1024]{1,0:T(8,128)(2,1)S(1)}, u32[]{:S(2)}, u32[]{:S(2)}) collective-permute-start(bf16[256,1024]{1,0:T(8,128)(2,1)S(1)} %collective-permute-done.3.hi_odd.rest_1_.lo_even), channel_id=1, source_target_pairs={{0,7},{1,0},{2,1},{3,2},{4,3},{5,4},{6,5},{7,6},{8,15},{9,8},{10,9... | collective-permute-start | bytes 1572872 | tf_op jit(solution)/shard_map/ppermute | solution.py:460
  40.8 7.7 %attention_pair.5 = (bf16[4,2,4096,128]{3,2,1,0:T(8,128)(2,1)}, bf16[512,256]{1,0:T(8,128)(2,1)}, bf16[2,512,1024]{2,1,0:T(8,128)(2,1)}, bf16[8,128,1024]{2,1,0:T(8,128)(2,1)}) custom-call(s32[4,3]{1,0:T(4,128)} %add_add_fusion.place, ...), custom_call_target="tpu_custom_call", output_to_operand_aliasing={{0}: (13, {}), {1}: (14, {}), {2}: (15, {}), {3}: (16, {})} | custom-call | flops 4000000000 | bytes 10000000 | tf_op jit(solution)/shard_map/attention_pair/pallas_call | solution.py:326
  48.5 3.9 %collective-permute-done.6.lo_odd.rest_0_.hi_even = bf16[256,1024]{1,0:T(8,128)(2,1)S(1)} collective-permute-done((bf16[256,1024]{1,0:T(8,128)(2,1)S(1)}, bf16[256,1024]{1,0:T(8,128)(2,1)S(1)}, u32[]{:S(2)}, u32[]{:S(2)}) %collective-permute-start.6) | collective-permute-done | bytes 524320 | tf_op jit(solution)/shard_map/ppermute | solution.py:459
  52.6 2.7 %collective-permute-start.9 = (bf16[128,1024]{1,0:T(8,128)(2,1)S(1)}, bf16[128,1024]{1,0:T(8,128)(2,1)S(1)}, u32[]{:S(2)}, u32[]{:S(2)}) collective-permute-start(bf16[128,1024]{1,0:T(8,128)(2,1)S(1)} %slice.15), channel_id=1, source_target_pairs={{0,7},{1,0},{2,1},{3,2},{4,3},{5,4},{6,5},{7,6},{8,15},{9,8},{10,9... | collective-permute-start | bytes 786440 | tf_op jit(solution)/shard_map/ppermute | solution.py:463
  55.3 8.2 %attention_pair.6 = (bf16[4,2,4096,128]{3,2,1,0:T(8,128)(2,1)}, bf16[512,256]{1,0:T(8,128)(2,1)}, bf16[2,512,1024]{2,1,0:T(8,128)(2,1)}, bf16[8,128,1024]{2,1,0:T(8,128)(2,1)}) custom-call(s32[4,3]{1,0:T(4,128)} %add_add_fusion.place, ...), custom_call_target="tpu_custom_call", output_to_operand_aliasing={{0}: (13, {}), {1}: (14, {}), {2}: (15, {}), {3}: (16, {})} | custom-call | flops 4000000000 | bytes 10000000 | tf_op jit(solution)/shard_map/attention_pair/pallas_call | solution.py:326
  64.4 8.1 %attention_pair.7 = (bf16[4,2,4096,128]{3,2,1,0:T(8,128)(2,1)}, bf16[512,256]{1,0:T(8,128)(2,1)}, bf16[2,512,1024]{2,1,0:T(8,128)(2,1)}, bf16[8,128,1024]{2,1,0:T(8,128)(2,1)}) custom-call(s32[4,3]{1,0:T(4,128)} %add_add_fusion.place, ...), custom_call_target="tpu_custom_call", output_to_operand_aliasing={{0}: (12, {}), {1}: (13, {}), {2}: (14, {}), {3}: (15, {})} | custom-call | flops 4000000000 | bytes 10000000 | tf_op jit(solution)/shard_map/attention_pair/pallas_call | solution.py:326
  74.4 5.0 %all-to-all-start = ((bf16[8,64,256]{2,1,0:T(8,128)(2,1)}), bf16[8,64,256]{2,1,0:T(8,128)(2,1)S(1)}, u32[]{:S(2)}, u32[]{:S(2)}) async-start(bf16[8,64,256]{2,1,0:T(8,128)(2,1)} %bitcast.29), calls=%async_computation | async-start | bytes 524288 | tf_op jit(solution)/shard_map/all_to_all | solution.py:414
  79.4 2.9 %rim_grads.1 = (bf16[2,1536,128]{2,1,0:T(8,128)(2,1)}, bf16[2,1536,128]{2,1,0:T(8,128)(2,1)}) custom-call(bf16[4,2,4096,128]{3,2,1,0:T(8,128)(2,1)} %get-tuple-element.66.grads), custom_call_target="tpu_custom_call" | custom-call | flops 1000000 | bytes 5000000 | tf_op jit(solution)/shard_map/rim_grads/pallas_call | solution.py:361
  83.3 3.2 %collective-permute-start.12 = (bf16[2,1536,128]{2,1,0:T(8,128)(2,1)}, bf16[2,1536,128]{2,1,0:T(8,128)(2,1)}, u32[]{:S(2)}, u32[]{:S(2)}) collective-permute-start(bf16[2,1536,128]{2,1,0:T(8,128)(2,1)} %get-tuple-element.79), channel_id=1, source_target_pairs={{0,8},{8,16},{16,24},{24,32},{32,40},{40,48},{48,56},{56,64},{64,7... | collective-permute-start | bytes 2359304 | tf_op jit(solution)/shard_map/ppermute | solution.py:497
  88.5 3.3 %all-to-all-done = bf16[8,64,256]{2,1,0:T(8,128)(2,1)S(1)} async-done(((bf16[8,64,256]{2,1,0:T(8,128)(2,1)}), bf16[8,64,256]{2,1,0:T(8,128)(2,1)S(1)}, u32[]{:S(2)}, u32[]{:S(2)}) %all-to-all-start) | async-done | bytes 262176 | tf_op jit(solution)/shard_map/all_to_all | solution.py:414
  92.5 6.5 %all-to-all-start.1 = ((bf16[16,64,128]{2,1,0:T(8,128)(2,1)}), bf16[16,64,128]{2,1,0:T(8,128)(2,1)S(1)}, u32[]{:S(2)}, u32[]{:S(2)}) async-start(bf16[16,64,128]{2,1,0:T(8,128)(2,1)} %bitcast.3), calls=%async_computation.1 | async-start | bytes 524288 | tf_op jit(solution)/shard_map/all_to_all | solution.py:414
  99.5 2.8 %broadcast_select_fusion.2 = (bf16[64,1024]{1,0:T(8,128)(2,1)}, bf16[64,1024]{1,0:T(8,128)(2,1)}) fusion(bf16[64,1024]{1,0:T(8,128)(2,1)S(1)} %fusion, pred[]{:T(512)S(6)} %eq.25, bf16[8,128,1024]{2,1,0:T(8,128)(2,1)} %collective-permute-done.11, bf16[8,64,256]{2,1,0:T(8,128)(2,1)S(1)} %all-to-all-done), kind=kOutput, calls=%fused_computation.14 | convolution fusion | flops 134479872 | bytes 2753536 | tf_op jit(solution)/shard_map/trk,tkn->rn/dot_general | solution.py:503
  102.3 4.7 %all-to-all-done.1 = bf16[16,64,128]{2,1,0:T(8,128)(2,1)S(1)} async-done(((bf16[16,64,128]{2,1,0:T(8,128)(2,1)}), bf16[16,64,128]{2,1,0:T(8,128)(2,1)S(1)}, u32[]{:S(2)}, u32[]{:S(2)}) %all-to-all-start.1) | async-done | bytes 262176 | tf_op jit(solution)/shard_map/all_to_all | solution.py:414
  107.8 3.5 %all-to-all-start.2 = ((bf16[16,64,128]{2,1,0:T(8,128)(2,1)}), bf16[16,64,128]{2,1,0:T(8,128)(2,1)S(1)}, u32[]{:S(2)}, u32[]{:S(2)}) async-start(bf16[16,64,128]{2,1,0:T(8,128)(2,1)} %broadcast_in_dim.20), calls=%async_computation.2 | async-start | bytes 524288 | tf_op jit(solution)/shard_map/all_to_all | solution.py:414
  111.4 4.8 %combine_grads.1 = bf16[2,4096,128]{2,1,0:T(8,128)(2,1)} custom-call(bf16[4,2,4096,128]{3,2,1,0:T(8,128)(2,1)} %get-tuple-element.66.grads, bf16[2,1536,128]{2,1,0:T(8,128)(2,1)} %collective-permute-done.12.from_left, bf16[2,1536,128]{2,1,0:T(8,128)(2,1)} %collective-permute-done.13.from_right), custom_call_target="tpu_custom_call" | custom-call | flops 5000000 | bytes 10000000 | tf_op jit(solution)/shard_map/combine_grads/pallas_call | solution.py:380
  116.2 2.8 %all-to-all-done.2 = bf16[16,64,128]{2,1,0:T(8,128)(2,1)S(1)} async-done(((bf16[16,64,128]{2,1,0:T(8,128)(2,1)}), bf16[16,64,128]{2,1,0:T(8,128)(2,1)S(1)}, u32[]{:S(2)}, u32[]{:S(2)}) %all-to-all-start.2) | async-done | bytes 262176 | tf_op jit(solution)/shard_map/all_to_all | solution.py:414
  119.0 2.8 %collective-permute-start.14 = (bf16[16,64,128]{2,1,0:T(8,128)(2,1)S(1)}, bf16[16,64,128]{2,1,0:T(8,128)(2,1)S(1)}, u32[]{:S(2)}, u32[]{:S(2)}) collective-permute-start(bf16[16,64,128]{2,1,0:T(8,128)(2,1)S(1)} %all-to-all-done.2), channel_id=1, source_target_pairs={{0,8},{8,0},{16,24},{24,16},{32,40},{40,32},{48,56},{56,48},{64,72... | collective-permute-start | bytes 786440 | tf_op jit(solution)/shard_map/ppermute | solution.py:515
  (75 shorter events, 18.4 us)
Async XLA Ops:
  0.6 16.6 %copy-start = (s32[128,32]{0,1:T(8,128)S(1)}, s32[128,32]{0,1:T(8,128)}, u32[]{:S(2)}) copy-start(s32[128,32]{0,1:T(8,128)} %param.12) | copy-start | bytes 49156
  0.6 16.4 %copy-start.14 = (s32[4]{0:T(128)S(1)}, s32[4]{0:T(128)}, u32[]{:S(2)}) copy-start(s32[4]{0:T(128)} %constant.77.clone) | copy-start | bytes 52
  0.7 16.4 %copy-start.15 = (s32[4]{0:T(128)S(1)}, s32[4]{0:T(128)}, u32[]{:S(2)}) copy-start(s32[4]{0:T(128)} %constant.78.clone) | copy-start | bytes 52
  4.6 18.3 %collective-permute-start = (bf16[256,1024]{1,0:T(8,128)(2,1)}, bf16[256,1024]{1,0:T(8,128)(2,1)S(1)}, u32[]{:S(2)}, u32[]{:S(2)}) collective-permute-start(bf16[256,1024]{1,0:T(8,128)(2,1)} %get-tuple-element.44.lo_even.hi_odd.rest_0_), channel_id=1, source_target_pairs={{0,1},{1,2},{2,3},{3,4},{4,5},{5,6},{6,7},{7,0},{8,9},{9,10},{10,1... | collective-permute-start | bytes 1572872 | tf_op jit(solution)/shard_map/ppermute | solution.py:459
  7.1 15.8 %collective-permute-start.2 = (bf16[256,1024]{1,0:T(8,128)(2,1)}, bf16[256,1024]{1,0:T(8,128)(2,1)S(1)}, u32[]{:S(2)}, u32[]{:S(2)}) collective-permute-start(bf16[256,1024]{1,0:T(8,128)(2,1)} %get-tuple-element.44.lo_even.hi_odd.rest_0_), channel_id=1, source_target_pairs={{0,7},{1,0},{2,1},{3,2},{4,3},{5,4},{6,5},{7,6},{8,15},{9,8},{10,9... | collective-permute-start | bytes 1572872 | tf_op jit(solution)/shard_map/ppermute | solution.py:460
  11.1 15.0 %collective-permute-start.4 = (bf16[2,1536,128]{2,1,0:T(8,128)(2,1)}, bf16[2,1536,128]{2,1,0:T(8,128)(2,1)S(1)}, u32[]{:S(2)}, u32[]{:S(2)}) collective-permute-start(bf16[2,1536,128]{2,1,0:T(8,128)(2,1)} %get-tuple-element.45), channel_id=1, source_target_pairs={{0,8},{8,16},{16,24},{24,32},{32,40},{40,48},{48,56},{56,64},{64,7... | collective-permute-start | bytes 2359304 | tf_op jit(solution)/shard_map/ppermute | solution.py:436
  15.1 13.8 %collective-permute-start.5 = (bf16[2,1536,128]{2,1,0:T(8,128)(2,1)}, bf16[2,1536,128]{2,1,0:T(8,128)(2,1)S(1)}, u32[]{:S(2)}, u32[]{:S(2)}) collective-permute-start(bf16[2,1536,128]{2,1,0:T(8,128)(2,1)} %get-tuple-element.46), channel_id=1, source_target_pairs={{8,0},{16,8},{24,16},{32,24},{40,32},{48,40},{56,48},{64,56},{72,6... | collective-permute-start | bytes 2359304 | tf_op jit(solution)/shard_map/ppermute | solution.py:437
  22.9 6.0 %copy-start.11 = (bf16[256,1024]{1,0:T(8,128)(2,1)}, bf16[256,1024]{1,0:T(8,128)(2,1)S(1)}, u32[]{:S(2)}) copy-start(bf16[256,1024]{1,0:T(8,128)(2,1)S(1)} %collective-permute-done.lo_odd.rest_1_.hi_even) | copy-start | bytes 1572868
  22.9 15.1 %collective-permute-start.1 = (bf16[256,1024]{1,0:T(8,128)(2,1)S(1)}, bf16[256,1024]{1,0:T(8,128)(2,1)S(1)}, u32[]{:S(2)}, u32[]{:S(2)}) collective-permute-start(bf16[256,1024]{1,0:T(8,128)(2,1)S(1)} %collective-permute-done.lo_odd.rest_1_.hi_even), channel_id=1, source_target_pairs={{0,1},{1,2},{2,3},{3,4},{4,5},{5,6},{6,7},{7,0},{8,9},{9,10},{10,1... | collective-permute-start | bytes 1572872 | tf_op jit(solution)/shard_map/ppermute | solution.py:459
  22.9 6.0 %copy-start.12 = (bf16[256,1024]{1,0:T(8,128)(2,1)}, bf16[256,1024]{1,0:T(8,128)(2,1)S(1)}, u32[]{:S(2)}) copy-start(bf16[256,1024]{1,0:T(8,128)(2,1)S(1)} %collective-permute-done.2.hi_even.rest_2_.lo_odd) | copy-start | bytes 1572868
  22.9 15.1 %collective-permute-start.3 = (bf16[256,1024]{1,0:T(8,128)(2,1)S(1)}, bf16[256,1024]{1,0:T(8,128)(2,1)S(1)}, u32[]{:S(2)}, u32[]{:S(2)}) collective-permute-start(bf16[256,1024]{1,0:T(8,128)(2,1)S(1)} %collective-permute-done.2.hi_even.rest_2_.lo_odd), channel_id=1, source_target_pairs={{0,7},{1,0},{2,1},{3,2},{4,3},{5,4},{6,5},{7,6},{8,15},{9,8},{10,9... | collective-permute-start | bytes 1572872 | tf_op jit(solution)/shard_map/ppermute | solution.py:460
  38.0 14.4 %collective-permute-start.6 = (bf16[256,1024]{1,0:T(8,128)(2,1)S(1)}, bf16[256,1024]{1,0:T(8,128)(2,1)S(1)}, u32[]{:S(2)}, u32[]{:S(2)}) collective-permute-start(bf16[256,1024]{1,0:T(8,128)(2,1)S(1)} %collective-permute-done.1.lo_even.rest_0_.hi_odd), channel_id=1, source_target_pairs={{0,1},{1,2},{2,3},{3,4},{4,5},{5,6},{6,7},{7,0},{8,9},{9,10},{10,1... | collective-permute-start | bytes 1572872 | tf_op jit(solution)/shard_map/ppermute | solution.py:459
  38.1 14.3 %collective-permute-start.7 = (bf16[256,1024]{1,0:T(8,128)(2,1)S(1)}, bf16[256,1024]{1,0:T(8,128)(2,1)S(1)}, u32[]{:S(2)}, u32[]{:S(2)}) collective-permute-start(bf16[256,1024]{1,0:T(8,128)(2,1)S(1)} %collective-permute-done.3.hi_odd.rest_1_.lo_even), channel_id=1, source_target_pairs={{0,7},{1,0},{2,1},{3,2},{4,3},{5,4},{6,5},{7,6},{8,15},{9,8},{10,9... | collective-permute-start | bytes 1572872 | tf_op jit(solution)/shard_map/ppermute | solution.py:460
  52.5 11.1 %collective-permute-start.8 = (bf16[128,1024]{1,0:T(8,128)(2,1)S(1)}, bf16[128,1024]{1,0:T(8,128)(2,1)S(1)}, u32[]{:S(2)}, u32[]{:S(2)}) collective-permute-start(bf16[128,1024]{1,0:T(8,128)(2,1)S(1)} %slice.14), channel_id=1, source_target_pairs={{0,1},{1,2},{2,3},{3,4},{4,5},{5,6},{6,7},{7,0},{8,9},{9,10},{10,1... | collective-permute-start | bytes 786440 | tf_op jit(solution)/shard_map/ppermute | solution.py:462
  52.6 11.0 %collective-permute-start.9 = (bf16[128,1024]{1,0:T(8,128)(2,1)S(1)}, bf16[128,1024]{1,0:T(8,128)(2,1)S(1)}, u32[]{:S(2)}, u32[]{:S(2)}) collective-permute-start(bf16[128,1024]{1,0:T(8,128)(2,1)S(1)} %slice.15), channel_id=1, source_target_pairs={{0,7},{1,0},{2,1},{3,2},{4,3},{5,4},{6,5},{7,6},{8,15},{9,8},{10,9... | collective-permute-start | bytes 786440 | tf_op jit(solution)/shard_map/ppermute | solution.py:463
  72.5 27.0 %collective-permute-start.11 = (bf16[8,128,1024]{2,1,0:T(8,128)(2,1)}, bf16[8,128,1024]{2,1,0:T(8,128)(2,1)}, u32[]{:S(2)}, u32[]{:S(2)}) collective-permute-start(bf16[8,128,1024]{2,1,0:T(8,128)(2,1)} %get-tuple-element.75), channel_id=1, source_target_pairs={{0,8},{8,0},{16,24},{24,16},{32,40},{40,32},{48,56},{56,48},{64,72... | collective-permute-start | bytes 6291464 | tf_op jit(solution)/shard_map/ppermute | solution.py:498
  74.4 17.4 %all-to-all-start = ((bf16[8,64,256]{2,1,0:T(8,128)(2,1)}), bf16[8,64,256]{2,1,0:T(8,128)(2,1)S(1)}, u32[]{:S(2)}, u32[]{:S(2)}) async-start(bf16[8,64,256]{2,1,0:T(8,128)(2,1)} %bitcast.29), calls=%async_computation | async-start | bytes 524288 | tf_op jit(solution)/shard_map/all_to_all | solution.py:414
  82.4 16.6 %copy-start.3 = (bf16[8,128,1024]{2,1,0:T(8,128)(2,1)S(1)}, bf16[8,128,1024]{2,1,0:T(8,128)(2,1)}, u32[]{:S(2)}) copy-start(bf16[8,128,1024]{2,1,0:T(8,128)(2,1)} %get-tuple-element.75) | copy-start | bytes 6291460
  82.9 8.9 %collective-permute-start.10 = (bf16[32,32,128]{2,1,0:T(8,128)(2,1)S(1)}, bf16[32,32,128]{2,1,0:T(8,128)(2,1)S(1)}, u32[]{:S(2)}, u32[]{:S(2)}) collective-permute-start(bf16[32,32,128]{2,1,0:T(8,128)(2,1)S(1)} %get-tuple-element.73), channel_id=1, source_target_pairs={{0,8},{8,0},{16,24},{24,16},{32,40},{40,32},{48,56},{56,48},{64,72... | collective-permute-start | bytes 786440 | tf_op jit(solution)/shard_map/ppermute | solution.py:491
  83.3 28.1 %collective-permute-start.12 = (bf16[2,1536,128]{2,1,0:T(8,128)(2,1)}, bf16[2,1536,128]{2,1,0:T(8,128)(2,1)}, u32[]{:S(2)}, u32[]{:S(2)}) collective-permute-start(bf16[2,1536,128]{2,1,0:T(8,128)(2,1)} %get-tuple-element.79), channel_id=1, source_target_pairs={{0,8},{8,16},{16,24},{24,32},{32,40},{40,48},{48,56},{56,64},{64,7... | collective-permute-start | bytes 2359304 | tf_op jit(solution)/shard_map/ppermute | solution.py:497
  86.5 24.9 %collective-permute-start.13 = (bf16[2,1536,128]{2,1,0:T(8,128)(2,1)}, bf16[2,1536,128]{2,1,0:T(8,128)(2,1)}, u32[]{:S(2)}, u32[]{:S(2)}) collective-permute-start(bf16[2,1536,128]{2,1,0:T(8,128)(2,1)} %get-tuple-element.80), channel_id=1, source_target_pairs={{8,0},{16,8},{24,16},{32,24},{40,32},{48,40},{56,48},{64,56},{72,6... | collective-permute-start | bytes 2359304 | tf_op jit(solution)/shard_map/ppermute | solution.py:496
  92.5 14.5 %all-to-all-start.1 = ((bf16[16,64,128]{2,1,0:T(8,128)(2,1)}), bf16[16,64,128]{2,1,0:T(8,128)(2,1)S(1)}, u32[]{:S(2)}, u32[]{:S(2)}) async-start(bf16[16,64,128]{2,1,0:T(8,128)(2,1)} %bitcast.3), calls=%async_computation.1 | async-start | bytes 524288 | tf_op jit(solution)/shard_map/all_to_all | solution.py:414
  107.8 11.2 %all-to-all-start.2 = ((bf16[16,64,128]{2,1,0:T(8,128)(2,1)}), bf16[16,64,128]{2,1,0:T(8,128)(2,1)S(1)}, u32[]{:S(2)}, u32[]{:S(2)}) async-start(bf16[16,64,128]{2,1,0:T(8,128)(2,1)} %broadcast_in_dim.20), calls=%async_computation.2 | async-start | bytes 524288 | tf_op jit(solution)/shard_map/all_to_all | solution.py:414
  119.0 3.9 %collective-permute-start.14 = (bf16[16,64,128]{2,1,0:T(8,128)(2,1)S(1)}, bf16[16,64,128]{2,1,0:T(8,128)(2,1)S(1)}, u32[]{:S(2)}, u32[]{:S(2)}) collective-permute-start(bf16[16,64,128]{2,1,0:T(8,128)(2,1)S(1)} %all-to-all-done.2), channel_id=1, source_target_pairs={{0,8},{8,0},{16,24},{24,16},{32,40},{40,32},{48,56},{56,48},{64,72... | collective-permute-start | bytes 786440 | tf_op jit(solution)/shard_map/ppermute | solution.py:515
  (10 other events, 22.4 us)
